TPU v7x, 32 devices: a whole 2x2x4 slice. The times are simulated.
32 devices in a mesh: copies: 2 (over y), users: 4 (over z), items: 4 (over x, core).
Axes of the slice: x: 2, y: 2, z: 4, core: 2. Of those that a mesh axis runs over, the one named last changes fastest.
Arguments:
- ratings: float32 [16384, 2048], P(('copies', 'users'), 'items'), parts along dimension 0, may hold values from -6 to 6
- entry_mask: int32 [16384, 2048], P(('copies', 'users'), 'items'), parts along dimension 0, may hold values 0 or 1
- pattern: int32 [128, 16], P(('copies', 'users'), 'items'), parts along dimension 0, may hold values from 0 to 1, as said below
- left: float32 [16384, 64], P(('copies', 'users')), parts along dimension 0, may hold values from -1.5 to 1.5
- left_dir: float32 [16384, 64], P(('copies', 'users')), parts along dimension 0, may hold values from -1.5 to 1.5
- right: float32 [4096, 64], P(('copies', 'items', 'users')), parts along dimension 0, may hold values from -3 to 3
- right_dir: float32 [4096, 64], P(('copies', 'items', 'users')), parts along dimension 0, may hold values from -3 to 3
Outputs:
- grad_left: float32 [16384, 64], P(('copies', 'users')), parts along dimension 0
- hess_left: float32 [16384, 64], P(('copies', 'users')), parts along dimension 0
- grad_right: float32 [4096, 64], P(('copies', 'items', 'users')), parts along dimension 0
- hess_right: float32 [4096, 64], P(('copies', 'items', 'users')), parts along dimension 0
- inner: float32 [4], P('copies'), parts along dimension 0
There are 2 independent parts, one for each index of `copies`. A program takes and returns all parts, laid end to end along the dimension named above; each array names one. Nothing has to cross between parts.
Inputs may be any that keep to these rules, and one draw needn't show every extreme that they name: `pattern`: 1 marks an observed tile; the share of observed tiles differs between user tiles.
All inputs are finite; a program needn't handle non-finite values. No bound on the sum of `entry_mask` on one device may be relied on, other than what follows from the above.
Results may differ from a plain program's by a relative error of at most 0.00007.
Values sent between devices are 32-bit elements; how exact they have to be, the bound alone decides.
No kernel may reach another device: no remote copies, remote signals or barrier semaphores. Data moves between devices by JAX's collectives and lax.ppermute only.
A program may use at most 64 MiB of HBM per device.

v0:
```python
import jax
import jax.numpy as jnp
from jax import lax
from jax.sharding import PartitionSpec as P


def mult(a, b):
    return jnp.dot(a, b, precision=lax.Precision.HIGHEST, preferred_element_type=jnp.float32)


def per_device(ratings, entry_mask, pattern, left, left_dir, right, right_dir):
    panel, panel_dir = (
        lax.all_gather(right, "users", axis=0, tiled=True),
        lax.all_gather(right_dir, "users", axis=0, tiled=True),
    )
    tile_side = ratings.shape[0] // pattern.shape[0]
    tiles = jnp.repeat(jnp.repeat(pattern, tile_side, axis=0), tile_side, axis=1)
    observed = entry_mask.astype(jnp.float32) * tiles.astype(jnp.float32)
    res = observed * (mult(left, panel.T) - ratings)
    change = observed * (mult(left_dir, panel.T) + mult(left, panel_dir.T))
    item_grad = mult(res.T, left) / 64.0
    item_hess = (mult(change.T, left) + mult(res.T, left_dir)) / 64.0
    user_grad = mult(res, panel) / 64.0
    user_hess = (mult(change, panel) + mult(res, panel_dir)) / 64.0
    grad_right, hess_right = (
        lax.psum_scatter(item_grad, "users", scatter_dimension=0, tiled=True),
        lax.psum_scatter(item_hess, "users", scatter_dimension=0, tiled=True),
    )
    right_gnorm = jnp.sum(grad_right * grad_right)
    right_curve = jnp.sum(right_dir * hess_right)
    grad_left, hess_left = lax.psum((user_grad, user_hess), "items")
    share = 1.0 / lax.axis_size("items")
    left_gnorm = share * jnp.sum(grad_left * grad_left)
    left_curve = share * jnp.sum(left_dir * hess_left)
    gnorm = lax.psum(left_gnorm + right_gnorm, ("users", "items"))
    curve = lax.psum(left_curve + right_curve, ("users", "items"))
    inner = jnp.stack([gnorm, curve])
    return (grad_left, hess_left, grad_right, hess_right, inner)


def solution(mesh):
    placed = (
        P(("copies", "users"), "items"),
        P(("copies", "users"), "items"),
        P(("copies", "users"), "items"),
        P(("copies", "users"), None),
        P(("copies", "users"), None),
        P(("copies", "items", "users"), None),
        P(("copies", "items", "users"), None),
    )
    return jax.shard_map(
        per_device,
        mesh=mesh,
        in_specs=placed,
        out_specs=(
            P(("copies", "users"), None),
            P(("copies", "users"), None),
            P(("copies", "items", "users"), None),
            P(("copies", "items", "users"), None),
            P("copies"),
        ),
        check_vma=False,
    )
```

profile of v0, /device:TPU:0, one launch (start us, length us, event | category | flops | bytes accessed | tf_op | source)
XLA Modules:
  0.0 180.4 jit_solution(15671920019215861883)
XLA Ops:
  8.0 0.0 reduce-scatter.3.cloned.1.call-start
  8.1 15.4 %all_gather.6 = f32[512,64]{0,1:T(8,128)S(1)} all-gather(f32[128,64]{0,1:T(8,128)} %param.12), channel_id=1, replica_groups=mesh['copies'=2,'users'=4,'items'=4] {'users'}, dimensions={0}, use_global_device_ids=true | all-gather | bytes 163840 | tf_op jit(solution)/shard_map/all_gather | solution.py:13
  23.5 0.7 convert_element_type.15
  24.2 0.1 copy.12
  24.2 0.1 broadcast_in_dim.6
  24.3 4.7 %broadcast_in_dim.7 = f32[2048,4,128]{2,1,0:T(4,128)S(1)} broadcast(f32[2048,4]{1,0:T(8,128)S(1)} %bitcast.30), dimensions={0,1} | broadcast | bytes 4227072 | tf_op jit(solution)/shard_map/broadcast_in_dim | solution.py:17
  29.0 7.3 %subtract_multiply_fusion = f32[2048,512]{1,0:T(8,128)S(1)} fusion(f32[2048,512]{1,0:T(8,128)} %param.7, f32[2048,64]{0,1:T(8,128)S(1)} %copy-done, f32[512,64]{0,1:T(8,128)S(1)} %all_gather.6, f32[256,8,4,128]{3,2,1,0:T(4,128)S(1)} %bitcast.28, s32[2048,512]{1,0:T(8,128)S(1)} %copy-done.7), kind=kOutput, calls=%fused_computation.2 | convolution fusion | flops 809500672 | bytes 17432576 | tf_op jit(solution)/shard_map/dot_general | solution.py:8
  36.3 1.9 %copy-done.1 = f32[2048,512]{1,0:T(8,128)} copy-done((f32[2048,512]{1,0:T(8,128)}, f32[2048,512]{1,0:T(8,128)S(1)}, u32[]{:S(2)}) %copy-start.1) | copy-done | bytes 4194328
  38.3 3.4 %convolution_multiply_fusion.1 = f32[512,64]{0,1:T(8,128)} fusion(f32[2048,512]{1,0:T(8,128)S(1)} %subtract_multiply_fusion, f32[2048,64]{0,1:T(8,128)S(1)} %copy-done), kind=kOutput, calls=%fused_computation.8 | convolution fusion | flops 805339136 | bytes 4849664 | tf_op jit(solution)/shard_map/dot_general | solution.py:8
  41.7 0.0 reduce-scatter.5.cloned.1.call-start
  41.8 3.5 %fusion.2 = f32[2048,512]{1,0:T(8,128)S(1)} fusion(f32[2048,64]{0,1:T(8,128)S(1)} %copy-done.8, f32[512,64]{0,1:T(8,128)S(1)} %all_gather.6), kind=kOutput, calls=%fused_computation.14 | convolution fusion | flops 805306368 | bytes 4849664 | tf_op jit(solution)/shard_map/dot_general | solution.py:8
  45.3 13.8 %all_gather.7 = f32[512,64]{0,1:T(8,128)S(1)} all-gather(f32[128,64]{0,1:T(8,128)S(1)} %copy-done.9), channel_id=1, replica_groups=mesh['copies'=2,'users'=4,'items'=4] {'users'}, dimensions={0}, use_global_device_ids=true | all-gather | bytes 163840 | tf_op jit(solution)/shard_map/all_gather | solution.py:14
  59.1 5.8 %add_multiply_fusion = f32[2048,512]{1,0:T(8,128)S(1)} fusion(f32[2048,512]{1,0:T(8,128)S(1)} %fusion.2, f32[2048,64]{0,1:T(8,128)S(1)} %copy-done, f32[512,64]{0,1:T(8,128)S(1)} %all_gather.7, f32[256,8,4,128]{3,2,1,0:T(4,128)S(1)} %bitcast.29, s32[2048,512]{1,0:T(8,128)} %param.8), kind=kOutput, calls=%fused_computation.1 | convolution fusion | flops 809500672 | bytes 17432576 | tf_op jit(solution)/shard_map/dot_general | solution.py:8
  64.9 2.0 %copy-done.6 = f32[2048,512]{1,0:T(8,128)} copy-done((f32[2048,512]{1,0:T(8,128)}, f32[2048,512]{1,0:T(8,128)S(1)}, u32[]{:S(2)}) %copy-start.6) | copy-done | bytes 4194328
  66.9 2.8 %fusion.4 = f32[512,64]{0,1:T(8,128)S(1)} fusion(f32[2048,512]{1,0:T(8,128)S(1)} %add_multiply_fusion, f32[2048,64]{0,1:T(8,128)S(1)} %copy-done), kind=kOutput, calls=%fused_computation.16 | convolution fusion | flops 805306368 | bytes 4849664 | tf_op jit(solution)/shard_map/dot_general | solution.py:8
  69.7 3.4 %fusion.1 = f32[512,64]{0,1:T(8,128)} fusion(f32[512,64]{0,1:T(8,128)S(1)} %fusion.4, f32[2048,512]{1,0:T(8,128)S(1)} %copy-done.2, f32[2048,64]{0,1:T(8,128)S(1)} %copy-done.8), kind=kOutput, calls=%fused_computation.7 | convolution fusion | flops 805371904 | bytes 4980736 | tf_op jit(solution)/shard_map/dot_general | solution.py:8
  73.1 0.3 all-reduce.4.cloned.1.call-start
  73.4 6.5 %fusion.3 = f32[2048,64]{0,1:T(8,128)S(1)} fusion(f32[2048,512]{1,0:T(8,128)} %copy-done.6, f32[512,64]{0,1:T(8,128)S(1)} %all_gather.6), kind=kOutput, calls=%fused_computation.15 | convolution fusion | flops 805306368 | bytes 4849664 | tf_op jit(solution)/shard_map/dot_general | solution.py:8
  79.9 5.0 %fusion = f32[2048,64]{0,1:T(8,128)} fusion(f32[2048,64]{0,1:T(8,128)S(1)} %fusion.3, f32[2048,512]{1,0:T(8,128)S(1)} %copy-done.3, f32[512,64]{0,1:T(8,128)S(1)} %all_gather.7), kind=kOutput, calls=%fused_computation.4 | convolution fusion | flops 805568512 | bytes 5373952 | tf_op jit(solution)/shard_map/dot_general | solution.py:8
  84.9 5.0 %convolution_multiply_fusion = f32[2048,64]{0,1:T(8,128)} fusion(f32[2048,512]{1,0:T(8,128)S(1)} %copy-done.3, f32[512,64]{0,1:T(8,128)S(1)} %all_gather.6), kind=kOutput, calls=%fused_computation.5 | convolution fusion | flops 805437440 | bytes 4849664 | tf_op jit(solution)/shard_map/dot_general | solution.py:8
  89.9 0.0 all-reduce.4.cloned.1.call-update
  89.9 0.0 reduce-scatter.3.cloned.1.call-done
  90.0 1.4 multiply_reduce_fusion.3
  91.4 2.1 %reduce-scatter.5.cloned.1.call-done = f32[128,64]{0,1:T(8,128)} async-done(((f32[512,64]{0,1:T(8,128)}), f32[128,64]{0,1:T(8,128)}) %reduce-scatter.5.cloned.1.call-update) | async-done | bytes 32784 | tf_op jit(solution)/shard_map/reduce_scatter | solution.py:27
  93.6 1.4 multiply_reduce_fusion.2
  94.9 32.8 %all-reduce.4.cloned.1.call-done = (f32[2048,64]{0,1:T(8,128)}, f32[2048,64]{0,1:T(8,128)}) async-done(((f32[2048,64]{0,1:T(8,128)}, f32[2048,64]{0,1:T(8,128)}), (f32[2048,64]{0,1:T(8,128)}, f32[2048,64]{0,1:T(8,128)})) %all-reduce.4.cloned.1.call-update) | async-done | bytes 1048592 | tf_op jit(solution)/shard_map/psum | solution.py:31
  127.7 1.8 multiply_reduce_fusion
  129.5 1.8 multiply_reduce_fusion.1
  133.8 33.5 %all-reduce = (f32[1]{0:T(128)}, f32[1]{0:T(128)}) all-reduce(f32[1]{0:T(128)} %bitcast.2, f32[1]{0:T(128)} %bitcast.1), channel_id=1, replica_groups=mesh['copies'=2,'users'=4,'items'=4] {'users','items'}, use_global_device_ids=true, to_apply=%region_9.0 | all-reduce | flops 2 | bytes 16 | tf_op jit(solution)/shard_map/psum | solution.py:36
  167.3 1.9 %pad_maximum_fusion = f32[2]{0:T(128)} fusion(f32[1]{0:T(128)} %get-tuple-element.5, f32[1]{0:T(128)} %get-tuple-element.6), kind=kLoop, calls=%fused_computation.13 | loop fusion | flops 2 | bytes 16 | tf_op jit(solution)/shard_map/stack | solution.py:37
  169.2 1.9 %copy.21 = f32[2048,64]{0,1:T(8,128)} copy(f32[2048,64]{0,1:T(8,128)} %get-tuple-element.9) | data formatting | bytes 1048576
  171.1 1.9 %copy.22 = f32[2048,64]{0,1:T(8,128)} copy(f32[2048,64]{0,1:T(8,128)} %get-tuple-element.10) | data formatting | bytes 1048576
  (20 shorter events, 0.1 us)
Async XLA Ops:
  8.0 21.0 %copy-start = (f32[2048,64]{0,1:T(8,128)S(1)}, f32[2048,64]{0,1:T(8,128)}, u32[]{:S(2)}) copy-start(f32[2048,64]{0,1:T(8,128)} %param.10) | copy-start | bytes 1572868
  8.0 81.9 %reduce-scatter.3.cloned.1.call-start = ((), (), s32[]{:S(2)}) async-start(), calls=%async_computation.2 | async-start | bytes 163840 | tf_op jit(solution)/shard_map/reduce_scatter | solution.py:26
  24.2 4.8 %copy-start.7 = (s32[2048,512]{1,0:T(8,128)S(1)}, s32[2048,512]{1,0:T(8,128)}, u32[]{:S(2)}) copy-start(s32[2048,512]{1,0:T(8,128)} %param.8) | copy-start | bytes 12582916
  29.0 7.3 %copy-start.4 = (f32[2048,4,128]{2,1,0:T(4,128)}, f32[2048,4,128]{2,1,0:T(4,128)S(1)}, u32[]{:S(2)}) copy-start(f32[2048,4,128]{2,1,0:T(4,128)S(1)} %broadcast_in_dim.7) | copy-start | bytes 12582916
  36.3 1.9 %copy-start.1 = (f32[2048,512]{1,0:T(8,128)}, f32[2048,512]{1,0:T(8,128)S(1)}, u32[]{:S(2)}) copy-start(f32[2048,512]{1,0:T(8,128)S(1)} %subtract_multiply_fusion) | copy-start | bytes 12582916
  38.2 3.5 %copy-start.8 = (f32[2048,64]{0,1:T(8,128)S(1)}, f32[2048,64]{0,1:T(8,128)}, u32[]{:S(2)}) copy-start(f32[2048,64]{0,1:T(8,128)} %param.11) | copy-start | bytes 1572868
  38.2 7.0 %copy-start.9 = (f32[128,64]{0,1:T(8,128)S(1)}, f32[128,64]{0,1:T(8,128)}, u32[]{:S(2)}) copy-start(f32[128,64]{0,1:T(8,128)} %param.13) | copy-start | bytes 98308
  41.7 51.8 %reduce-scatter.5.cloned.1.call-start = ((), (), s32[]{:S(2)}) async-start(), calls=%async_computation.3 | async-start | bytes 163840 | tf_op jit(solution)/shard_map/reduce_scatter | solution.py:27
  41.8 17.3 %copy-start.5 = (f32[2048,4,128]{2,1,0:T(4,128)S(1)}, f32[2048,4,128]{2,1,0:T(4,128)}, u32[]{:S(2)}) copy-start(f32[2048,4,128]{2,1,0:T(4,128)} %copy-done.4) | copy-start | bytes 12582916
  64.9 2.0 %copy-start.6 = (f32[2048,512]{1,0:T(8,128)}, f32[2048,512]{1,0:T(8,128)S(1)}, u32[]{:S(2)}) copy-start(f32[2048,512]{1,0:T(8,128)S(1)} %add_multiply_fusion) | copy-start | bytes 12582916
  66.9 2.8 %copy-start.2 = (f32[2048,512]{1,0:T(8,128)S(1)}, f32[2048,512]{1,0:T(8,128)}, u32[]{:S(2)}) copy-start(f32[2048,512]{1,0:T(8,128)} %copy-done.1) | copy-start | bytes 12582916
  73.1 54.6 %all-reduce.4.cloned.1.call-start = ((), (), s32[]{:S(2)}) async-start(), calls=%async_computation.4 | async-start | bytes 2097152 | tf_op jit(solution)/shard_map/psum | solution.py:31
  73.4 6.5 %copy-start.3 = (f32[2048,512]{1,0:T(8,128)S(1)}, f32[2048,512]{1,0:T(8,128)}, u32[]{:S(2)}) copy-start(f32[2048,512]{1,0:T(8,128)} %copy-done.1) | copy-start | bytes 12582916
Sparse Core Ops, SparseCore 0:
  41.8 20.4 reduce-scatter.2
  73.3 20.2 reduce-scatter.4
Sparse Core Ops, SparseCore 1:
  90.0 37.6 all-reduce.3
where the time goes:
time: 181 us; the launch traced here: 180 us
  blocking collectives  62.8 us (35%)
  matrix products  42.7 us (24%)
  waiting for transfers between devices  35 us (19%)
  between operations  18.2 us (10%)
  local copies, waits for them, and re-layouts  12.5 us (7%)
  other arithmetic  8.94 us (5%)
    dot_general x9, matrix products, mult(): jnp.dot(a, b, precision=lax.Precision.HIGHEST, preferred_element_type=jnp...  42.7 us
    psum x1, blocking collectives, per_device(): curve = lax.psum(left_curve + right_curve, ('users', 'items'))  33.5 us
    psum x1, waiting for transfers between devices, per_device(): grad_left, hess_left = lax.psum((user_grad, user_hess), 'items')  32.8 us
    all_gather x1, blocking collectives, per_device(): lax.all_gather(right, 'users', axis=0, tiled=True)  15.4 us
    all_gather x1, blocking collectives, per_device(): lax.all_gather(right_dir, 'users', axis=0, tiled=True)  13.8 us
    unnamed x22, local copies, waits for them, and re-layouts  7.66 us
    broadcast_in_dim x1, local copies, waits for them, and re-layouts, per_device(): jnp.repeat(jnp.repeat(pattern, tile_side, axis=0), tile_side, axis=1)  4.67 us
  transfers between devices with their start and end apart: 3, of which 2 were waited for; matrix products, arithmetic and copies ran while one was open for 19% of the time, Pallas kernels for 0%

commit v1 on v0

v1 whole, which is shorter than its diff:
```python
import functools

import jax
import jax.numpy as jnp
from jax import lax
from jax.experimental import pallas as pl
from jax.experimental.pallas import tpu as pltpu
from jax.sharding import PartitionSpec as P

F32 = jnp.float32
BF16 = jnp.bfloat16
SMEM = pl.BlockSpec(memory_space=pltpu.SMEM)


def dot(a, b):
    return jnp.dot(a, b, preferred_element_type=F32)


def halves(x):
    high = x.astype(BF16)
    return high, (x - high.astype(F32)).astype(BF16)


def tile_sum(x):
    total = jnp.sum(x, axis=0, keepdims=True)
    return functools.reduce(jnp.add, [total[:, i : i + 128] for i in range(0, total.shape[1], 128)])


def main_kernel(blocks, tile, scale, where, pattern, ratings, mask, left, left_dir, *refs):
    panels, refs = refs[:blocks], refs[blocks:]
    keep, send, curve, items = refs[0], refs[1], refs[2], refs[3 : 3 + blocks]
    forward, forward_low, back = refs[3 + blocks :]
    step = pl.program_id(0)
    rank, rows = left.shape
    wide = panels[0].shape[1]
    half = rank // 2
    flip = where[blocks] == 1

    def own_first(x):
        return jnp.where(flip, jnp.concatenate([x[half:], x[:half]], axis=0), x)

    @pl.when(step == 0)
    def _():
        for k in range(blocks):
            p, d = panels[k][:rank], panels[k][rank:]
            zero = jnp.zeros_like(p)
            q = jnp.concatenate(
                [jnp.concatenate([p, d], axis=1), jnp.concatenate([zero, p], axis=1)], axis=0
            )
            high, low = halves(q)
            forward[k, : 2 * rank] = high
            forward[k, 2 * rank :] = high
            forward_low[k] = low
            p, d, zero = own_first(p), own_first(d), zero[:half]
            s = jnp.concatenate(
                [
                    jnp.concatenate([p[:half], zero], axis=1),
                    jnp.concatenate([d[:half], p[:half]], axis=1),
                    jnp.concatenate([p[half:], zero], axis=1),
                    jnp.concatenate([d[half:], p[half:]], axis=1),
                ],
                axis=0,
            ).T
            high, low = halves(s)
            back[k, :, : 2 * rank] = high
            back[k, :, 2 * rank :] = low
            items[k][...] = jnp.zeros_like(items[k])
        curve[...] = jnp.zeros_like(curve)

    both = jnp.concatenate([left[...], left_dir[...]], axis=0)
    high, low = halves(both)
    factors = jnp.concatenate([high, low], axis=0)
    high_t, low_t = halves(both.T)
    factors_t = jnp.concatenate([high_t, low_t], axis=1)
    total = None
    for k in range(blocks):
        columns = pl.ds(pl.multiple_of(where[k] * wide, wide), wide)
        raw = dot(factors_t, forward[k]) + dot(high_t, forward_low[k])
        seen = mask[:, columns].astype(F32)
        seen = jnp.concatenate(
            [
                seen[t * tile : (t + 1) * tile]
                * (pattern[step * (rows // tile) + t, where[k]].astype(F32) * scale)
                for t in range(rows // tile)
            ],
            axis=0,
        )
        res = seen * (raw[:, :wide] - ratings[:, columns])
        change = seen * raw[:, wide:]
        rc_high, rc_low = halves(jnp.concatenate([res, change], axis=1))
        out = dot(rc_high, back[k])
        out = out[:, : 2 * rank] + out[:, 2 * rank :] + dot(rc_low, back[k, :, : 2 * rank])
        total = out if total is None else total + out
        got = dot(factors, rc_high)
        got = got[: 2 * rank] + got[2 * rank :] + dot(high, rc_low)
        items[k][:rank] += got[:rank, :wide]
        items[k][rank:] += got[:rank, wide:] + got[rank:, :wide]
    user = total.T
    keep[...] = user[:rank]
    send[...] = user[rank:]
    turned = own_first(left_dir[...])
    curve[...] += tile_sum(turned[:half] * user[half:rank] + turned[half:] * user[rank + half :])

    @pl.when(step == pl.num_programs(0) - 1)
    def _():
        for k in range(blocks):
            curve[...] += tile_sum(items[k][rank:] * panels[k][rank:])


def main_call(where, pattern, ratings, mask, left, left_dir, panels):
    users, width = ratings.shape
    rank = left.shape[0]
    blocks, wide = len(panels), panels[0].shape[1]
    rows = 256
    whole = lambda shape: pl.BlockSpec(shape, lambda i: (0,) * len(shape))
    row_block = pl.BlockSpec((rows, width), lambda i: (i, 0))
    column_block = pl.BlockSpec((rank, rows), lambda i: (0, i))
    shape = jax.ShapeDtypeStruct
    out = pl.pallas_call(
        functools.partial(main_kernel, blocks, users // pattern.shape[0], 1.0 / 64.0),
        grid=(users // rows,),
        in_specs=[SMEM, SMEM, row_block, row_block, column_block, column_block]
        + [whole((2 * rank, wide))] * blocks,
        out_specs=[column_block, column_block, whole((1, 128))] + [whole((2 * rank, wide))] * blocks,
        out_shape=[shape((rank, users), F32), shape((rank, users), F32), shape((1, 128), F32)]
        + [shape((2 * rank, wide), F32)] * blocks,
        scratch_shapes=[
            pltpu.VMEM((blocks, 4 * rank, 2 * wide), BF16),
            pltpu.VMEM((blocks, 2 * rank, 2 * wide), BF16),
            pltpu.VMEM((blocks, 2 * wide, 4 * rank), BF16),
        ],
        compiler_params=pltpu.CompilerParams(vmem_limit_bytes=48 * 1024 * 1024),
        cost_estimate=pl.CostEstimate(
            flops=2 * users * width * rank * 54, bytes_accessed=10 * users * width, transcendentals=0
        ),
        name="main",
    )(where, pattern, ratings, mask, left, left_dir, *panels)
    return out[0], out[1], out[2], out[3:]


def items_kernel(count, *refs):
    terms, (curve, grad, hess, sums) = refs[:count], refs[count:]
    total = functools.reduce(jnp.add, [t[...] for t in terms])
    rank = total.shape[0] // 2
    grad[...] = total[:rank]
    hess[...] = total[rank:]
    squares = jnp.sum(total[:rank] * total[:rank], axis=0, keepdims=True)
    wide = squares.shape[1]
    if wide < 128:
        squares = jnp.concatenate([squares, jnp.zeros((1, 128 - wide), F32)], axis=1)
    sums[...] = jnp.concatenate([squares, curve[...], jnp.zeros((6, 128), F32)], axis=0)


def items_call(terms, curve):
    rows, wide = terms[0].shape
    shape = jax.ShapeDtypeStruct
    return pl.pallas_call(
        functools.partial(items_kernel, len(terms)),
        out_shape=[shape((rows // 2, wide), F32), shape((rows // 2, wide), F32), shape((8, 128), F32)],
        name="items_total",
    )(*terms, curve)


def squares_kernel(a, b, sums, total, new):
    x = a[...] + b[...]
    total[...] = x
    new[...] = sums[...]
    new[0:1] += tile_sum(x * x)


def squares_call(a, b, sums):
    shape = jax.ShapeDtypeStruct
    return pl.pallas_call(
        squares_kernel,
        out_shape=[shape(a.shape, F32), shape(sums.shape, F32)],
        name="squares",
    )(a, b, sums)


def swap(x, axis, bit):
    return lax.ppermute(x, axis, [(i, i ^ bit) for i in range(lax.axis_size(axis))])


def bits(axis):
    return [1 << i for i in range(lax.axis_size(axis).bit_length() - 1)]


def per_device(ratings, entry_mask, pattern, left, left_dir, right, right_dir):
    rank = left.shape[1]
    wide = right.shape[0]
    n = lax.axis_size("users")
    me = lax.axis_index("users")
    core = lax.axis_index("items") % 2
    own = jnp.concatenate([right.T, right_dir.T], axis=0)
    direct = wide == 128
    if direct:
        panels = [own] + [swap(own, "users", k) for k in range(1, n)]
        index = [me ^ k for k in range(n)]
    else:
        panel = lax.all_gather(own, "users", axis=1, tiled=True)
        panels = [panel[:, i : i + 128] for i in range(0, panel.shape[1], 128)]
        index = list(range(len(panels)))
    where = jnp.stack([jnp.asarray(i, jnp.int32) for i in index + [core]])
    keep, send, curve, items = main_call(
        where, pattern, ratings, entry_mask, left.T, left_dir.T, panels
    )
    got = swap(send, "items", 1)
    half = rank // 2
    g = keep[:half] + got[:half]
    h = keep[half:] + got[half:]
    if direct:
        terms = [items[0]] + [swap(items[k], "users", k) for k in range(1, n)]
    else:
        terms = [
            lax.psum_scatter(jnp.concatenate(items, axis=1), "users", scatter_dimension=1, tiled=True)
        ]
    grad_right, hess_right, sums = items_call(terms, curve)
    across = bits("items")[1:]
    for bit in across:
        sums = sums + swap(sums, "items", bit)
    for bit in across[:-1]:
        g = g + swap(g, "items", bit)
        h = h + swap(h, "items", bit)
    other_g = swap(g, "items", across[-1])
    other_h = swap(h, "items", across[-1])
    g, sums = squares_call(g, other_g, sums)
    h = h + other_h
    for bit in bits("users"):
        sums = sums + swap(sums, "users", bit)
    sums = sums + swap(sums, "items", 1)
    inner = jnp.sum(sums[:2], axis=1)

    def joined(mine):
        other = swap(mine, "items", 1)
        return jnp.concatenate([jnp.where(core == 0, mine, other), jnp.where(core == 0, other, mine)], axis=0)

    return joined(g).T, joined(h).T, grad_right.T, hess_right.T, inner


def solution(mesh):
    placed = (
        P(("copies", "users"), "items"),
        P(("copies", "users"), "items"),
        P(("copies", "users"), "items"),
        P(("copies", "users"), None),
        P(("copies", "users"), None),
        P(("copies", "items", "users"), None),
        P(("copies", "items", "users"), None),
    )
    return jax.shard_map(
        per_device,
        mesh=mesh,
        in_specs=placed,
        out_specs=(
            P(("copies", "users"), None),
            P(("copies", "users"), None),
            P(("copies", "items", "users"), None),
            P(("copies", "items", "users"), None),
            P("copies"),
        ),
        check_vma=False,
    )
```

time: 181 us -> 73.1 us (0.40)
  blocking collectives: 62.8 us -> 0 us
  matrix products: 42.7 us -> 0 us
  Pallas kernels: 0 us -> 17.5 us
  between operations: 18.2 us -> 0.75 us
  starting transfers between devices: 0.34 us -> 17.7 us
  waiting for transfers between devices: 35 us -> 26.2 us
  local copies, waits for them, and re-layouts: 12.5 us -> 4.29 us
  other arithmetic: 8.94 us -> 6.15 us
    dot_general x9 -> x0, matrix products: 42.7 us -> none  [mult(): jnp.dot(a, b, precision=lax.Precision.HIGHEST, preferred_element_type=jnp...]
    psum x1 -> x0, blocking collectives: 33.5 us -> none  [per_device(): curve = lax.psum(left_curve + right_curve, ('users', 'items'))]
    psum x1 -> x0, waiting for transfers between devices: 32.8 us -> none  [per_device(): grad_left, hess_left = lax.psum((user_grad, user_hess), 'items')]
    all_gather x2 -> x0, blocking collectives: 29.2 us -> none  [the longest x1 15.4 us: per_device(): lax.all_gather(right, 'users', axis=0, tiled=True)]
    ppermute x0 -> x15, waiting for transfers between devices: none -> 26.2 us  [swap(): lax.ppermute(x, axis, [(i, i ^ bit) for i in range(lax.axis_size(axis))])]
    ppermute x0 -> x15, starting transfers between devices: none -> 17.7 us  [swap(): lax.ppermute(x, axis, [(i, i ^ bit) for i in range(lax.axis_size(axis))])]
    pallas_call x0 -> x3, Pallas kernels: none -> 17.5 us  [the longest x1 14.2 us: main_call(): pl.pallas_call(functools.partial(main_kernel, blocks, users // pattern.sh...]
    reduce_sum x4 -> x1, other arithmetic: 6.38 us -> 0.63 us  [per_device(): inner = jnp.sum(sums[:2], axis=1)]
  transfers between devices with their start and end apart: 3 -> 15, of which waited for: 2 -> 10; matrix products, arithmetic and copies ran while one was open for 19% -> 6% of each run, Pallas kernels for 0% -> 5%
where the time goes in v1:
time: 73.1 us; the launch traced here: 72.6 us
  waiting for transfers between devices  26.2 us (36%)
  starting transfers between devices  17.7 us (24%)
  Pallas kernels  17.5 us (24%)
  other arithmetic  6.15 us (8%)
  local copies, waits for them, and re-layouts  4.29 us (6%)
  between operations  0.75 us (1%)
    ppermute x15, waiting for transfers between devices, swap(): lax.ppermute(x, axis, [(i, i ^ bit) for i in range(lax.axis_size(axis))])  26.2 us
    ppermute x15, starting transfers between devices, swap(): lax.ppermute(x, axis, [(i, i ^ bit) for i in range(lax.axis_size(axis))])  17.7 us
    pallas_call x1, Pallas kernels, main_call(): pl.pallas_call(functools.partial(main_kernel, blocks, users // pattern.sh...  14.2 us
    unnamed x19, local copies, waits for them, and re-layouts  4.21 us
    pallas_call x1, Pallas kernels, squares_call(): pl.pallas_call(squares_kernel, out_shape=[shape(a.shape, F32), shape(sums...  1.76 us
    transpose x2, other arithmetic, per_device(): return (joined(g).T, joined(h).T, grad_right.T, hess_right.T, inner)  1.66 us
    pallas_call x1, Pallas kernels, items_call(): pl.pallas_call(functools.partial(items_kernel, len(terms)), out_shape=[sh...  1.57 us
  transfers between devices with their start and end apart: 15, of which 10 were waited for; matrix products, arithmetic and copies ran while one was open for 6% of the time, Pallas kernels for 5%

profile of v1, /device:TPU:0, one launch (start us, length us, event | category | flops | bytes accessed | tf_op | source)
XLA Modules:
  0.0 72.6 jit_solution(2958932782175535272)
XLA Ops:
  0.6 0.8 %pad_maximum_fusion.refs_0_ = f32[128,128]{1,0:T(8,128)S(1)} fusion(f32[64,128]{1,0:T(8,128)} %bitcast.17, f32[64,128]{1,0:T(8,128)} %bitcast.18), kind=kLoop, calls=%fused_computation.8 | loop fusion | flops 16384 | bytes 131072 | tf_op jit(solution)/shard_map/concatenate | solution.py:194
  1.4 5.0 %collective-permute-start.2 = (f32[128,128]{1,0:T(8,128)S(1)}, f32[128,128]{1,0:T(8,128)S(1)}, u32[]{:S(2)}, u32[]{:S(2)}) collective-permute-start(f32[128,128]{1,0:T(8,128)S(1)} %pad_maximum_fusion.refs_0_), channel_id=1, source_target_pairs={{0,12},{4,8},{8,4},{12,0},{1,13},{5,9},{9,5},{13,1},{2,14},{6,10},... | collective-permute-start | bytes 196616 | tf_op jit(solution)/shard_map/ppermute | solution.py:181
  6.5 0.6 collective-permute-start
  7.1 0.8 %copy.12.pattern = s32[16,4]{1,0:T(8,128)S(1)} copy(s32[16,4]{0,1:T(4,128)} %param.9) | data formatting | bytes 512 | tf_op args[2]
  7.9 1.1 %collective-permute-done.2.refs_3_ = f32[128,128]{1,0:T(8,128)S(1)} collective-permute-done((f32[128,128]{1,0:T(8,128)S(1)}, f32[128,128]{1,0:T(8,128)S(1)}, u32[]{:S(2)}, u32[]{:S(2)}) %collective-permute-start.2) | collective-permute-done | bytes 65568 | tf_op jit(solution)/shard_map/ppermute | solution.py:181
  9.0 3.0 %collective-permute-done.1.refs_2_ = f32[128,128]{1,0:T(8,128)S(1)} collective-permute-done((f32[128,128]{1,0:T(8,128)S(1)}, f32[128,128]{1,0:T(8,128)S(1)}, u32[]{:S(2)}, u32[]{:S(2)}) %collective-permute-start.1) | collective-permute-done | bytes 65568 | tf_op jit(solution)/shard_map/ppermute | solution.py:181
  12.1 1.0 %copy-done.2 = f32[2048,64]{0,1:T(8,128)S(1)} copy-done((f32[2048,64]{0,1:T(8,128)S(1)}, f32[2048,64]{0,1:T(8,128)}, u32[]{:S(2)}) %copy-start.2) | copy-done | bytes 524312
  13.1 1.0 %copy-done.3 = f32[2048,64]{0,1:T(8,128)S(1)} copy-done((f32[2048,64]{0,1:T(8,128)S(1)}, f32[2048,64]{0,1:T(8,128)}, u32[]{:S(2)}) %copy-start.3) | copy-done | bytes 524312
  14.2 14.2 %main.1 = (f32[64,2048]{1,0:T(8,128)S(1)}, f32[64,2048]{1,0:T(8,128)S(1)}, f32[1,128]{1,0:T(1,128)S(1)}, f32[128,128]{1,0:T(8,128)S(1)}, f32[128,128]{1,0:T(8,12...) custom-call(s32[5]{0:T(128)S(1)} %stack.23.where, s32[16,4]{1,0:T(8,128)S(1)} %copy.12.pattern, ...), custom_call_target="tpu_custom_call" | custom-call | flops 7247757312 | bytes 10485760 | tf_op jit(solution)/shard_map/main/pallas_call | solution.py:119
  28.5 1.9 %collective-permute-done.3 = f32[64,2048]{1,0:T(8,128)S(1)} collective-permute-done((f32[64,2048]{1,0:T(8,128)S(1)}, f32[64,2048]{1,0:T(8,128)S(1)}, u32[]{:S(2)}, u32[]{:S(2)}) %collective-permute-start.3) | collective-permute-done | bytes 524320 | tf_op jit(solution)/shard_map/ppermute | solution.py:181
  30.5 1.6 %collective-permute-start.10 = (f32[32,2048]{1,0:T(8,128)S(1)}, f32[32,2048]{1,0:T(8,128)S(1)}, u32[]{:S(2)}, u32[]{:S(2)}) collective-permute-start(f32[32,2048]{1,0:T(8,128)S(1)} %get-tuple-element.29), channel_id=1, source_target_pairs={{0,2},{1,3},{2,0},{3,1},{4,6},{5,7},{6,4},{7,5},{8,10},{9,11},{10,... | collective-permute-start | bytes 786440 | tf_op jit(solution)/shard_map/ppermute | solution.py:181
  32.6 7.1 %collective-permute-done.10 = f32[32,2048]{1,0:T(8,128)S(1)} collective-permute-done((f32[32,2048]{1,0:T(8,128)S(1)}, f32[32,2048]{1,0:T(8,128)S(1)}, u32[]{:S(2)}, u32[]{:S(2)}) %collective-permute-start.10) | collective-permute-done | bytes 262176 | tf_op jit(solution)/shard_map/ppermute | solution.py:181
  39.8 1.1 %collective-permute-start.5 = (f32[128,128]{1,0:T(8,128)S(1)}, f32[128,128]{1,0:T(8,128)S(1)}, u32[]{:S(2)}, u32[]{:S(2)}) collective-permute-start(f32[128,128]{1,0:T(8,128)S(1)} %get-tuple-element.20), channel_id=1, source_target_pairs={{0,4},{4,0},{8,12},{12,8},{1,5},{5,1},{9,13},{13,9},{2,6},{6,2},{1... | collective-permute-start | bytes 196616 | tf_op jit(solution)/shard_map/ppermute | solution.py:181
  40.9 2.3 %collective-permute-start.6 = (f32[128,128]{1,0:T(8,128)S(1)}, f32[128,128]{1,0:T(8,128)S(1)}, u32[]{:S(2)}, u32[]{:S(2)}) collective-permute-start(f32[128,128]{1,0:T(8,128)S(1)} %get-tuple-element.21), channel_id=1, source_target_pairs={{0,8},{4,12},{8,0},{12,4},{1,9},{5,13},{9,1},{13,5},{2,10},{6,14},... | collective-permute-start | bytes 196616 | tf_op jit(solution)/shard_map/ppermute | solution.py:181
  43.1 1.1 %collective-permute-start.7 = (f32[128,128]{1,0:T(8,128)S(1)}, f32[128,128]{1,0:T(8,128)S(1)}, u32[]{:S(2)}, u32[]{:S(2)}) collective-permute-start(f32[128,128]{1,0:T(8,128)S(1)} %get-tuple-element.22), channel_id=1, source_target_pairs={{0,12},{4,8},{8,4},{12,0},{1,13},{5,9},{9,5},{13,1},{2,14},{6,10},... | collective-permute-start | bytes 196616 | tf_op jit(solution)/shard_map/ppermute | solution.py:181
  44.3 5.0 %collective-permute-done.6.refs_2_ = f32[128,128]{1,0:T(8,128)S(1)} collective-permute-done((f32[128,128]{1,0:T(8,128)S(1)}, f32[128,128]{1,0:T(8,128)S(1)}, u32[]{:S(2)}, u32[]{:S(2)}) %collective-permute-start.6) | collective-permute-done | bytes 65568 | tf_op jit(solution)/shard_map/ppermute | solution.py:181
  50.0 1.6 %items_total.1 = (f32[64,128]{1,0:T(8,128)}, f32[64,128]{1,0:T(8,128)}, f32[8,128]{1,0:T(8,128)}) custom-call(f32[128,128]{1,0:T(8,128)} %copy-done, f32[128,128]{1,0:T(8,128)} %copy-done.6, f32[128,128]{1,0:T(8,128)} %copy-done.7, f32[128,128]{1,0:T(8,128)} %copy-done.8, f32[1,128]{1,0:T(1,128)} %copy-done.1), custom_call_target="tpu_custom_call" | custom-call | tf_op jit(solution)/shard_map/items_total/pallas_call | solution.py:157
  51.6 1.5 %collective-permute-start.8 = (f32[8,128]{1,0:T(8,128)}, f32[8,128]{1,0:T(8,128)S(1)}, u32[]{:S(2)}, u32[]{:S(2)}) collective-permute-start(f32[8,128]{1,0:T(8,128)} %get-tuple-element.24), channel_id=1, source_target_pairs={{0,2},{1,3},{2,0},{3,1},{4,6},{5,7},{6,4},{7,5},{8,10},{9,11},{10,... | collective-permute-start | bytes 12296 | tf_op jit(solution)/shard_map/ppermute | solution.py:181
  53.1 2.3 %collective-permute-done.8 = f32[8,128]{1,0:T(8,128)S(1)} collective-permute-done((f32[8,128]{1,0:T(8,128)}, f32[8,128]{1,0:T(8,128)S(1)}, u32[]{:S(2)}, u32[]{:S(2)}) %collective-permute-start.8) | collective-permute-done | bytes 4128 | tf_op jit(solution)/shard_map/ppermute | solution.py:181
  55.4 1.3 %add.27.sums = f32[8,128]{1,0:T(8,128)} add(f32[8,128]{1,0:T(8,128)} %get-tuple-element.24, f32[8,128]{1,0:T(8,128)S(1)} %collective-permute-done.8) | non-fusion elementwise | flops 1024 | bytes 12288 | tf_op jit(solution)/shard_map/add | solution.py:220
  56.6 0.7 copy-done.5
  57.3 1.8 %squares.1 = (f32[32,2048]{1,0:T(8,128)}, f32[8,128]{1,0:T(8,128)}) custom-call(f32[32,2048]{1,0:T(8,128)} %copy-done.4, f32[32,2048]{1,0:T(8,128)} %copy-done.5, f32[8,128]{1,0:T(8,128)} %add.27.sums), custom_call_target="tpu_custom_call" | custom-call | tf_op jit(solution)/shard_map/squares/pallas_call | solution.py:173
  59.1 1.3 %collective-permute-start.12 = (f32[8,128]{1,0:T(8,128)}, f32[8,128]{1,0:T(8,128)S(1)}, u32[]{:S(2)}, u32[]{:S(2)}) collective-permute-start(f32[8,128]{1,0:T(8,128)} %get-tuple-element.28), channel_id=1, source_target_pairs={{0,4},{4,0},{8,12},{12,8},{1,5},{5,1},{9,13},{13,9},{2,6},{6,2},{1... | collective-permute-start | bytes 12296 | tf_op jit(solution)/shard_map/ppermute | solution.py:181
  60.4 2.5 %collective-permute-done.12 = f32[8,128]{1,0:T(8,128)S(1)} collective-permute-done((f32[8,128]{1,0:T(8,128)}, f32[8,128]{1,0:T(8,128)S(1)}, u32[]{:S(2)}, u32[]{:S(2)}) %collective-permute-start.12) | collective-permute-done | bytes 4128 | tf_op jit(solution)/shard_map/ppermute | solution.py:181
  62.9 0.7 add.30
  63.6 1.9 %collective-permute-start.13 = (f32[8,128]{1,0:T(8,128)S(1)}, f32[8,128]{1,0:T(8,128)S(1)}, u32[]{:S(2)}, u32[]{:S(2)}) collective-permute-start(f32[8,128]{1,0:T(8,128)S(1)} %add.30), channel_id=1, source_target_pairs={{0,8},{4,12},{8,0},{12,4},{1,9},{5,13},{9,1},{13,5},{2,10},{6,14},... | collective-permute-start | bytes 12296 | tf_op jit(solution)/shard_map/ppermute | solution.py:181
  65.5 2.6 %collective-permute-done.13 = f32[8,128]{1,0:T(8,128)S(1)} collective-permute-done((f32[8,128]{1,0:T(8,128)S(1)}, f32[8,128]{1,0:T(8,128)S(1)}, u32[]{:S(2)}, u32[]{:S(2)}) %collective-permute-start.13) | collective-permute-done | bytes 4128 | tf_op jit(solution)/shard_map/ppermute | solution.py:181
  68.6 0.7 collective-permute-done.14
  69.3 0.6 slice_reduce_fusion
  70.0 0.8 %maximum_bitcast_fusion.1 = f32[2048,64]{0,1:T(8,128)} fusion(f32[32,2048]{1,0:T(8,128)S(1)} %get-tuple-element.32, f32[32,2048]{1,0:T(8,128)S(1)} %get-tuple-element.31), kind=kLoop, calls=%fused_computation.1 | loop fusion | flops 131072 | bytes 1048576 | tf_op jit(solution)/shard_map/transpose | solution.py:237
  70.8 1.0 %broadcast_select_fusion.3 = (f32[32,2048]{1,0:T(8,128)S(1)}, f32[32,2048]{1,0:T(8,128)S(1)}) fusion(f32[32,2048]{1,0:T(8,128)} %get-tuple-element.25, f32[32,2048]{1,0:T(8,128)S(1)} %collective-permute-done.9, pred[]{:T(512)S(6)} %eq.4), kind=kLoop, calls=%fused_computation.7 | loop fusion | flops 131072 | bytes 1048577 | tf_op jit(solution)/shard_map/jit(_where)/select_n | solution.py:235
  71.8 0.8 %maximum_bitcast_fusion = f32[2048,64]{0,1:T(8,128)} fusion(f32[32,2048]{1,0:T(8,128)S(1)} %get-tuple-element.34, f32[32,2048]{1,0:T(8,128)S(1)} %get-tuple-element.33), kind=kLoop, calls=%fused_computation | loop fusion | flops 131072 | bytes 1048576 | tf_op jit(solution)/shard_map/transpose | solution.py:237
  (33 shorter events, 2.1 us)
Async XLA Ops:
  1.4 7.6 %collective-permute-start.2 = (f32[128,128]{1,0:T(8,128)S(1)}, f32[128,128]{1,0:T(8,128)S(1)}, u32[]{:S(2)}, u32[]{:S(2)}) collective-permute-start(f32[128,128]{1,0:T(8,128)S(1)} %pad_maximum_fusion.refs_0_), channel_id=1, source_target_pairs={{0,12},{4,8},{8,4},{12,0},{1,13},{5,9},{9,5},{13,1},{2,14},{6,10},... | collective-permute-start | bytes 196616 | tf_op jit(solution)/shard_map/ppermute | solution.py:181
  6.5 5.6 %collective-permute-start.1 = (f32[128,128]{1,0:T(8,128)S(1)}, f32[128,128]{1,0:T(8,128)S(1)}, u32[]{:S(2)}, u32[]{:S(2)}) collective-permute-start(f32[128,128]{1,0:T(8,128)S(1)} %pad_maximum_fusion.refs_0_), channel_id=1, source_target_pairs={{0,8},{4,12},{8,0},{12,4},{1,9},{5,13},{9,1},{13,5},{2,10},{6,14},... | collective-permute-start | bytes 196616 | tf_op jit(solution)/shard_map/ppermute | solution.py:181
  6.5 5.6 %collective-permute-start = (f32[128,128]{1,0:T(8,128)S(1)}, f32[128,128]{1,0:T(8,128)S(1)}, u32[]{:S(2)}, u32[]{:S(2)}) collective-permute-start(f32[128,128]{1,0:T(8,128)S(1)} %pad_maximum_fusion.refs_0_), channel_id=1, source_target_pairs={{0,4},{4,0},{8,12},{12,8},{1,5},{5,1},{9,13},{13,9},{2,6},{6,2},{1... | collective-permute-start | bytes 196616 | tf_op jit(solution)/shard_map/ppermute | solution.py:181
  12.1 1.0 %copy-start.2 = (f32[2048,64]{0,1:T(8,128)S(1)}, f32[2048,64]{0,1:T(8,128)}, u32[]{:S(2)}) copy-start(f32[2048,64]{0,1:T(8,128)} %param.10) | copy-start | bytes 1572868
  13.1 1.0 %copy-start.3 = (f32[2048,64]{0,1:T(8,128)S(1)}, f32[2048,64]{0,1:T(8,128)}, u32[]{:S(2)}) copy-start(f32[2048,64]{0,1:T(8,128)} %param.11) | copy-start | bytes 1572868
  28.4 2.1 %copy-start = (f32[128,128]{1,0:T(8,128)}, f32[128,128]{1,0:T(8,128)S(1)}, u32[]{:S(2)}) copy-start(f32[128,128]{1,0:T(8,128)S(1)} %get-tuple-element.19.refs_0_) | copy-start | bytes 196612
  28.4 2.1 %copy-start.1 = (f32[1,128]{1,0:T(1,128)}, f32[1,128]{1,0:T(1,128)S(1)}, u32[]{:S(2)}) copy-start(f32[1,128]{1,0:T(1,128)S(1)} %get-tuple-element.23.refs_4_) | copy-start | bytes 1540
  28.4 2.0 %collective-permute-start.3 = (f32[64,2048]{1,0:T(8,128)S(1)}, f32[64,2048]{1,0:T(8,128)S(1)}, u32[]{:S(2)}, u32[]{:S(2)}) collective-permute-start(f32[64,2048]{1,0:T(8,128)S(1)} %get-tuple-element.18), channel_id=1, source_target_pairs={{0,1},{1,0},{2,3},{3,2},{4,5},{5,4},{6,7},{7,6},{8,9},{9,8},{10,11... | collective-permute-start | bytes 1572872 | tf_op jit(solution)/shard_map/ppermute | solution.py:181
  30.4 26.2 %copy-start.4 = (f32[32,2048]{1,0:T(8,128)}, f32[32,2048]{1,0:T(8,128)S(1)}, u32[]{:S(2)}) copy-start(f32[32,2048]{1,0:T(8,128)S(1)} %get-tuple-element.30.a) | copy-start | bytes 786436
  30.5 9.2 %collective-permute-start.10 = (f32[32,2048]{1,0:T(8,128)S(1)}, f32[32,2048]{1,0:T(8,128)S(1)}, u32[]{:S(2)}, u32[]{:S(2)}) collective-permute-start(f32[32,2048]{1,0:T(8,128)S(1)} %get-tuple-element.29), channel_id=1, source_target_pairs={{0,2},{1,3},{2,0},{3,1},{4,6},{5,7},{6,4},{7,5},{8,10},{9,11},{10,... | collective-permute-start | bytes 786440 | tf_op jit(solution)/shard_map/ppermute | solution.py:181
  32.1 24.6 %collective-permute-start.4 = (f32[32,2048]{1,0:T(8,128)S(1)}, f32[32,2048]{1,0:T(8,128)S(1)}, u32[]{:S(2)}, u32[]{:S(2)}) collective-permute-start(f32[32,2048]{1,0:T(8,128)S(1)} %get-tuple-element.30.a), channel_id=1, source_target_pairs={{0,2},{1,3},{2,0},{3,1},{4,6},{5,7},{6,4},{7,5},{8,10},{9,11},{10,... | collective-permute-start | bytes 786440 | tf_op jit(solution)/shard_map/ppermute | solution.py:181
  39.7 30.2 %collective-permute-start.11 = (f32[32,2048]{1,0:T(8,128)S(1)}, f32[32,2048]{1,0:T(8,128)S(1)}, u32[]{:S(2)}, u32[]{:S(2)}) collective-permute-start(f32[32,2048]{1,0:T(8,128)S(1)} %add.29), channel_id=1, source_target_pairs={{0,1},{1,0},{2,3},{3,2},{4,5},{5,4},{6,7},{7,6},{8,9},{9,8},{10,11... | collective-permute-start | bytes 786440 | tf_op jit(solution)/shard_map/ppermute | solution.py:181
  39.8 4.5 %collective-permute-start.5 = (f32[128,128]{1,0:T(8,128)S(1)}, f32[128,128]{1,0:T(8,128)S(1)}, u32[]{:S(2)}, u32[]{:S(2)}) collective-permute-start(f32[128,128]{1,0:T(8,128)S(1)} %get-tuple-element.20), channel_id=1, source_target_pairs={{0,4},{4,0},{8,12},{12,8},{1,5},{5,1},{9,13},{13,9},{2,6},{6,2},{1... | collective-permute-start | bytes 196616 | tf_op jit(solution)/shard_map/ppermute | solution.py:181
  40.9 8.5 %collective-permute-start.6 = (f32[128,128]{1,0:T(8,128)S(1)}, f32[128,128]{1,0:T(8,128)S(1)}, u32[]{:S(2)}, u32[]{:S(2)}) collective-permute-start(f32[128,128]{1,0:T(8,128)S(1)} %get-tuple-element.21), channel_id=1, source_target_pairs={{0,8},{4,12},{8,0},{12,4},{1,9},{5,13},{9,1},{13,5},{2,10},{6,14},... | collective-permute-start | bytes 196616 | tf_op jit(solution)/shard_map/ppermute | solution.py:181
  43.1 6.2 %collective-permute-start.7 = (f32[128,128]{1,0:T(8,128)S(1)}, f32[128,128]{1,0:T(8,128)S(1)}, u32[]{:S(2)}, u32[]{:S(2)}) collective-permute-start(f32[128,128]{1,0:T(8,128)S(1)} %get-tuple-element.22), channel_id=1, source_target_pairs={{0,12},{4,8},{8,4},{12,0},{1,13},{5,9},{9,5},{13,1},{2,14},{6,10},... | collective-permute-start | bytes 196616 | tf_op jit(solution)/shard_map/ppermute | solution.py:181
  44.3 5.0 %copy-start.6 = (f32[128,128]{1,0:T(8,128)}, f32[128,128]{1,0:T(8,128)S(1)}, u32[]{:S(2)}) copy-start(f32[128,128]{1,0:T(8,128)S(1)} %collective-permute-done.5.refs_1_) | copy-start | bytes 196612
  49.3 0.6 copy-start.7
  49.3 0.6 copy-start.8
  51.6 3.8 %collective-permute-start.8 = (f32[8,128]{1,0:T(8,128)}, f32[8,128]{1,0:T(8,128)S(1)}, u32[]{:S(2)}, u32[]{:S(2)}) collective-permute-start(f32[8,128]{1,0:T(8,128)} %get-tuple-element.24), channel_id=1, source_target_pairs={{0,2},{1,3},{2,0},{3,1},{4,6},{5,7},{6,4},{7,5},{8,10},{9,11},{10,... | collective-permute-start | bytes 12296 | tf_op jit(solution)/shard_map/ppermute | solution.py:181
  56.6 0.7 copy-start.5
  59.1 3.8 %collective-permute-start.12 = (f32[8,128]{1,0:T(8,128)}, f32[8,128]{1,0:T(8,128)S(1)}, u32[]{:S(2)}, u32[]{:S(2)}) collective-permute-start(f32[8,128]{1,0:T(8,128)} %get-tuple-element.28), channel_id=1, source_target_pairs={{0,4},{4,0},{8,12},{12,8},{1,5},{5,1},{9,13},{13,9},{2,6},{6,2},{1... | collective-permute-start | bytes 12296 | tf_op jit(solution)/shard_map/ppermute | solution.py:181
  63.6 4.5 %collective-permute-start.13 = (f32[8,128]{1,0:T(8,128)S(1)}, f32[8,128]{1,0:T(8,128)S(1)}, u32[]{:S(2)}, u32[]{:S(2)}) collective-permute-start(f32[8,128]{1,0:T(8,128)S(1)} %add.30), channel_id=1, source_target_pairs={{0,8},{4,12},{8,0},{12,4},{1,9},{5,13},{9,1},{13,5},{2,10},{6,14},... | collective-permute-start | bytes 12296 | tf_op jit(solution)/shard_map/ppermute | solution.py:181
  68.1 1.2 %collective-permute-start.14 = (f32[8,128]{1,0:T(8,128)S(1)}, f32[8,128]{1,0:T(8,128)S(1)}, u32[]{:S(2)}, u32[]{:S(2)}) collective-permute-start(f32[8,128]{1,0:T(8,128)S(1)} %add.31), channel_id=1, source_target_pairs={{0,1},{1,0},{2,3},{3,2},{4,5},{5,4},{6,7},{7,6},{8,9},{9,8},{10,11... | collective-permute-start | bytes 12296 | tf_op jit(solution)/shard_map/ppermute | solution.py:181
  68.1 2.7 %collective-permute-start.9 = (f32[32,2048]{1,0:T(8,128)}, f32[32,2048]{1,0:T(8,128)S(1)}, u32[]{:S(2)}, u32[]{:S(2)}) collective-permute-start(f32[32,2048]{1,0:T(8,128)} %get-tuple-element.25), channel_id=1, source_target_pairs={{0,1},{1,0},{2,3},{3,2},{4,5},{5,4},{6,7},{7,6},{8,9},{9,8},{10,11... | collective-permute-start | bytes 786440 | tf_op jit(solution)/shard_map/ppermute | solution.py:181

commit v2 on v0

v2 whole, which is shorter than its diff:
```python
import functools
import itertools
import jax
import jax.numpy as jnp
from jax import lax
from jax.experimental import pallas as pl
from jax.experimental.pallas import tpu as pltpu
from jax.sharding import PartitionSpec as P

F32 = jnp.float32
BF16 = jnp.bfloat16
SMEM = pl.BlockSpec(memory_space=pltpu.SMEM)
VMEM = pl.BlockSpec(memory_space=pltpu.VMEM)
HBM = pl.BlockSpec(memory_space=pltpu.HBM)


def dot(a, b):
    return jnp.dot(a, b, preferred_element_type=F32)


def halves(x):
    high = x.astype(BF16)
    return high, (x - high.astype(F32)).astype(BF16)


def tile_sum(x):
    total = jnp.sum(x, axis=0, keepdims=True)
    return functools.reduce(jnp.add, [total[:, i : i + 128] for i in range(0, total.shape[1], 128)])


def first_loads(where, rows, factors, factors_to, factor_sems, grids, grids_to, own_sems, other_sems):
    users, width = grids[0].shape
    wide = 128
    block = lambda k: pl.ds(pl.multiple_of(where[k] * wide, wide), wide)
    steps = []
    for step in range(users // rows):
        here = pl.ds(step * rows, rows)
        steps.append(
            [
                pltpu.make_async_copy(a.at[:, here], b.at[:, here], factor_sems.at[i, step])
                for i, (a, b) in enumerate(zip(factors, factors_to))
            ]
            + [
                pltpu.make_async_copy(a.at[here, block(0)], b.at[here, block(0)], own_sems.at[i, step])
                for i, (a, b) in enumerate(zip(grids, grids_to))
            ]
        )
    rest = [
        pltpu.make_async_copy(a.at[:, block(k)], b.at[:, block(k)], other_sems.at[i, k - 1])
        for k in range(1, width // wide)
        for i, (a, b) in enumerate(zip(grids, grids_to))
    ]
    return steps, rest


def block_kernel(blocks, first, last, span, rows, tile, loop, where, pattern, ratings, mask, *refs):
    refs = list(refs)
    take = lambda n: [refs.pop(0) for _ in range(n)]
    if first:
        left_hbm, left_dir_hbm = take(2)
    else:
        factors_t, factors, acc = take(3)
        left_dir = take(1)[0] if last else None
    panels = take(blocks)
    start, stop = span
    items_in = take(blocks) if last and start > 0 else None
    if first:
        factors_t, factors, ratings_hbm, mask_hbm = *take(2), ratings, mask
        ratings, mask, left_dir = take(3)
    if last:
        keep, send = take(2)
    else:
        acc_out = take(1)[0]
    curve = take(1)[0]
    items = take(blocks)
    forward, forward_low, back = take(3)
    if first:
        left, factor_sems, own_sems, other_sems = refs
        loads = first_loads(
            where, rows, (left_hbm, left_dir_hbm), (left, left_dir), factor_sems,
            (ratings_hbm, mask_hbm), (ratings, mask), own_sems, other_sems,
        )
        for copy in itertools.chain(*loads[0], loads[1]):
            copy.start()
    rank2, wide = panels[0].shape
    rank = rank2 // 2
    half = rank // 2
    flip = where[ratings.shape[1] // wide if first else blocks] == 1

    def own_first(x):
        return jnp.where(flip, jnp.concatenate([x[half:], x[:half]], axis=0), x)

    for k in range(blocks):
        p, d = panels[k][:rank], panels[k][rank:]
        zero = jnp.zeros_like(p)
        q = jnp.concatenate([jnp.concatenate([p, d], axis=1), jnp.concatenate([zero, p], axis=1)], axis=0)
        high, low = halves(q)
        forward[k, : 2 * rank] = high
        forward[k, 2 * rank :] = high
        forward_low[k] = low
        p, d, zero = own_first(p), own_first(d), zero[:half]
        s = jnp.concatenate(
            [
                jnp.concatenate([p[:half], zero], axis=1),
                jnp.concatenate([d[:half], p[:half]], axis=1),
                jnp.concatenate([p[half:], zero], axis=1),
                jnp.concatenate([d[half:], p[half:]], axis=1),
            ],
            axis=0,
        ).T
        high, low = halves(s)
        back[k, :, : 2 * rank] = high
        back[k, :, 2 * rank :] = low
        items[k][...] = jnp.zeros_like(items[k]) if items_in is None else items_in[k][...]
    curve[...] = jnp.zeros_like(curve)

    def do(step):
        here = pl.ds(step if isinstance(step, int) else pl.multiple_of(step, rows), rows)
        if first:
            for copy in loads[0][step // rows]:
                copy.wait()
            both = jnp.concatenate([left[:, here], left_dir[:, here]], axis=0)
            high, low = halves(both)
            factors[: 2 * rank, here] = high
            factors[2 * rank :, here] = low
            high_t, low_t = halves(both.T)
            factors_t[here, : 2 * rank] = high_t
            factors_t[here, 2 * rank :] = low_t
            total = None
        else:
            total = acc[here, :]
        for k in range(blocks):
            columns = pl.ds(pl.multiple_of(where[k] * wide, wide), wide)
            raw = dot(factors_t[here, :], forward[k]) + dot(factors_t[here, : 2 * rank], forward_low[k])
            seen = mask[here, columns].astype(F32)
            seen = jnp.concatenate(
                [
                    seen[t * tile : (t + 1) * tile]
                    * (pattern[where[k], step // tile + t].astype(F32) * (1.0 / 64.0))
                    for t in range(rows // tile)
                ],
                axis=0,
            )
            res = seen * (raw[:, :wide] - ratings[here, columns])
            change = seen * raw[:, wide:]
            rc_high, rc_low = halves(jnp.concatenate([res, change], axis=1))
            out = dot(rc_high, back[k])
            out = out[:, : 2 * rank] + out[:, 2 * rank :] + dot(rc_low, back[k, :, : 2 * rank])
            total = out if total is None else total + out
            got = dot(factors[:, here], rc_high)
            got = got[: 2 * rank] + got[2 * rank :] + dot(factors[: 2 * rank, here], rc_low)
            items[k][:rank] += got[:rank, :wide]
            items[k][rank:] += got[:rank, wide:] + got[rank:, :wide]
        if last:
            user = total.T
            there = pl.ds(step - start if isinstance(step, int) else pl.multiple_of(step - start, rows), rows)
            keep[:, there] = user[:rank]
            send[:, there] = user[rank:]
            turned = own_first(left_dir[:, here])
            curve[...] += tile_sum(turned[:half] * user[half:rank] + turned[half:] * user[rank + half :])
        else:
            acc_out[here, :] = total

    if loop:
        def body(i, c):
            do(start + i * rows)
            return c
        lax.fori_loop(0, (stop - start) // rows, body, 0)
    else:
        for s in range(start, stop, rows):
            do(s)
    if first:
        for copy in loads[1]:
            copy.wait()
    if last and stop == ratings.shape[0] or not last:
        for k in range(blocks):
            curve[...] += tile_sum(items[k][rank:] * panels[k][rank:])


def block_call(where, pattern, ratings, mask, given, panels, first=False, last=False, span=None, items=(), rows=512, loop=True, name="block"):
    users, width = ratings.shape
    rank = panels[0].shape[0] // 2
    wide = panels[0].shape[1]
    blocks = len(panels)
    span = span or (0, users)
    count = span[1] - span[0]
    shape = jax.ShapeDtypeStruct
    outs = []
    scratch = [
        pltpu.VMEM((blocks, 4 * rank, 2 * wide), BF16),
        pltpu.VMEM((blocks, 2 * rank, 2 * wide), BF16),
        pltpu.VMEM((blocks, 2 * wide, 4 * rank), BF16),
    ]
    if first:
        outs += [shape((users, 4 * rank), BF16), shape((4 * rank, users), BF16)]
        outs += [shape(x.shape, x.dtype) for x in (ratings, mask, given[1])]
        steps = users // rows
        scratch += [
            pltpu.VMEM((rank, users), F32),
            pltpu.SemaphoreType.DMA((2, steps)),
            pltpu.SemaphoreType.DMA((2, steps)),
            pltpu.SemaphoreType.DMA((2, width // wide - 1)),
        ]
    outs += [shape((rank, count), F32)] * 2 if last else [shape((users, 2 * rank), F32)]
    outs += [shape((1, 128), F32)] + [shape((2 * rank, wide), F32)] * blocks
    args = [ratings, mask, *given, *panels, *items]
    far = 4 if first else 0
    args = [pltpu.with_memory_space_constraint(a, pltpu.HBM) for a in args[:far]] + [pltpu.with_memory_space_constraint(a, pltpu.VMEM) for a in args[far:]]
    return pl.pallas_call(
        functools.partial(block_kernel, blocks, first, last, span, rows, users // pattern.shape[1], loop),
        in_specs=[SMEM, SMEM] + [HBM] * far + [VMEM] * (len(args) - far),
        out_specs=[VMEM] * len(outs),
        out_shape=outs,
        scratch_shapes=scratch,
        compiler_params=pltpu.CompilerParams(vmem_limit_bytes=24 * 1024 * 1024),
        cost_estimate=pl.CostEstimate(flops=2 * count * wide * blocks * rank * 54, bytes_accessed=8 * count * wide * blocks, transcendentals=0),
        name=name,
    )(where, pattern, *args)


def items_kernel(count, *refs):
    terms, curves, (grad, hess, sums) = refs[:count], refs[count:-3], refs[-3:]
    total = functools.reduce(jnp.add, [t[...] for t in terms])
    rank = total.shape[0] // 2
    grad[...] = total[:rank]
    hess[...] = total[rank:]
    squares = jnp.sum(total[:rank] * total[:rank], axis=0, keepdims=True)
    wide = squares.shape[1]
    if wide < 128:
        squares = jnp.concatenate([squares, jnp.zeros((1, 128 - wide), F32)], axis=1)
    curve = functools.reduce(jnp.add, [c[...] for c in curves])
    sums[...] = jnp.concatenate([squares, curve, jnp.zeros((6, 128), F32)], axis=0)


def small_call(kernel, args, outs, name):
    args = [pltpu.with_memory_space_constraint(a, pltpu.VMEM) for a in args]
    return pl.pallas_call(
        kernel,
        in_specs=[VMEM] * len(args),
        out_specs=[VMEM] * len(outs),
        out_shape=[jax.ShapeDtypeStruct(o, F32) for o in outs],
        compiler_params=pltpu.CompilerParams(vmem_limit_bytes=4 * 1024 * 1024),
        name=name,
    )(*args)


def items_call(terms, curves):
    rows, wide = terms[0].shape
    return small_call(
        functools.partial(items_kernel, len(terms)),
        [*terms, *curves],
        [(rows // 2, wide), (rows // 2, wide), (8, 128)],
        "items_total",
    )


def squares_kernel(a, b, sums, total, new):
    x = a[...] + b[...]
    total[...] = x
    new[...] = sums[...]
    new[0:1] += tile_sum(x * x)


def squares_call(a, b, sums):
    return small_call(squares_kernel, [a, b, sums], [a.shape, sums.shape], "squares")


def add_kernel(a, b, after, total):
    total[...] = a[...] + b[...]


def add_call(a, b, after):
    return small_call(add_kernel, [a, b, after], [a.shape], "add")[0]


def swap(x, axis, bit):
    return lax.ppermute(x, axis, [(i, i ^ bit) for i in range(lax.axis_size(axis))])


def bits(axis):
    return [1 << i for i in range(lax.axis_size(axis).bit_length() - 1)]


def per_device(ratings, entry_mask, pattern, left, left_dir, right, right_dir):
    rank = left.shape[1]
    wide = right.shape[0]
    n = lax.axis_size("users")
    me = lax.axis_index("users")
    core = lax.axis_index("items") % 2
    own = jnp.concatenate([right.T, right_dir.T], axis=0)
    direct = wide == 128
    if direct:
        panels = [own] + [swap(own, "users", k) for k in range(1, n)]
        index = [me ^ k for k in range(n)]
    else:
        panel = lax.all_gather(own, "users", axis=1, tiled=True)
        panels = [panel[:, i : i + 128] for i in range(0, panel.shape[1], 128)]
        index = list(range(len(panels)))

    def where(blocks):
        return jnp.stack([jnp.asarray(i, jnp.int32) for i in [index[k] for k in blocks] + [core]])

    table = pattern.T
    factors_t, factors, ratings, entry_mask, left_dir_t, acc, curve_a, item = block_call(
        where(range(len(panels))), table, ratings, entry_mask, [left.T, left_dir.T], panels[:1],
        first=True, rows=1024, loop=False, name="own_block",
    )
    items = [item]
    others = list(range(1, len(panels)))
    keep, send, curve_b, *rest = block_call(
        where(others), table, ratings, entry_mask, [factors_t, factors, acc, left_dir_t], panels[1:],
        last=True, rows=1024, loop=False, name="other_blocks",
    )
    items += rest
    got = swap(send, "items", 1)
    half = rank // 2
    g = keep[:half] + got[:half]
    h = keep[half:] + got[half:]
    across = bits("items")[1:]
    for bit in across[:-1]:
        g = g + swap(g, "items", bit)
        h = h + swap(h, "items", bit)
    other_g = swap(g, "items", across[-1])
    other_h = swap(h, "items", across[-1])
    if direct:
        terms = [items[0]] + [swap(items[k], "users", k) for k in range(1, n)]
    else:
        terms = [
            lax.psum_scatter(jnp.concatenate(items, axis=1), "users", scatter_dimension=1, tiled=True)
        ]
    grad_right, hess_right, sums = items_call(terms, [curve_a, curve_b])
    for bit in across:
        sums = sums + swap(sums, "items", bit)
    g, sums = squares_call(g, other_g, sums)
    h = add_call(h, other_h, sums)
    for bit in bits("users"):
        sums = sums + swap(sums, "users", bit)
    sums = sums + swap(sums, "items", 1)
    inner = jnp.sum(sums[:2], axis=1)

    def joined(mine):
        other = swap(mine, "items", 1)
        return jnp.concatenate([jnp.where(core == 0, mine, other), jnp.where(core == 0, other, mine)], axis=0)

    return joined(g).T, joined(h).T, grad_right.T, hess_right.T, inner


def solution(mesh):
    placed = (
        P(("copies", "users"), "items"),
        P(("copies", "users"), "items"),
        P(("copies", "users"), "items"),
        P(("copies", "users"), None),
        P(("copies", "users"), None),
        P(("copies", "items", "users"), None),
        P(("copies", "items", "users"), None),
    )
    return jax.shard_map(
        per_device,
        mesh=mesh,
        in_specs=placed,
        out_specs=(
            P(("copies", "users"), None),
            P(("copies", "users"), None),
            P(("copies", "items", "users"), None),
            P(("copies", "items", "users"), None),
            P("copies"),
        ),
        check_vma=False,
    )
```

time: 181 us -> 51 us (0.28)
  blocking collectives: 62.8 us -> 0 us
  matrix products: 42.7 us -> 0 us
  waiting for transfers between devices: 35 us -> 17.5 us
  between operations: 18.2 us -> 0.71 us
  starting transfers between devices: 0.34 us -> 15.6 us
  Pallas kernels: 0 us -> 12.9 us
  local copies, waits for them, and re-layouts: 12.5 us -> 0.77 us
  other arithmetic: 8.94 us -> 3.33 us
    dot_general x9 -> x0, matrix products: 42.7 us -> none  [mult(): jnp.dot(a, b, precision=lax.Precision.HIGHEST, preferred_element_type=jnp...]
    psum x1 -> x0, blocking collectives: 33.5 us -> none  [per_device(): curve = lax.psum(left_curve + right_curve, ('users', 'items'))]
    psum x1 -> x0, waiting for transfers between devices: 32.8 us -> none  [per_device(): grad_left, hess_left = lax.psum((user_grad, user_hess), 'items')]
    all_gather x2 -> x0, blocking collectives: 29.2 us -> none  [the longest x1 15.4 us: per_device(): lax.all_gather(right, 'users', axis=0, tiled=True)]
    ppermute x0 -> x15, waiting for transfers between devices: none -> 17.5 us  [swap(): lax.ppermute(x, axis, [(i, i ^ bit) for i in range(lax.axis_size(axis))])]
    ppermute x0 -> x15, starting transfers between devices: none -> 15.6 us  [swap(): lax.ppermute(x, axis, [(i, i ^ bit) for i in range(lax.axis_size(axis))])]
    pallas_call x0 -> x5, Pallas kernels: none -> 12.9 us  [the longest x2 12.1 us: block_call(): pl.pallas_call(functools.partial(block_kernel, blocks, first, last, span,...]
    unnamed x22 -> x2, local copies, waits for them, and re-layouts: 7.66 us -> 0.68 us
  transfers between devices with their start and end apart: 3 -> 15, of which waited for: 2 -> 7; matrix products, arithmetic and copies ran while one was open for 19% -> 3% of each run, Pallas kernels for 0% -> 13%
where the time goes in v2:
time: 51 us; the launch traced here: 50.8 us
  waiting for transfers between devices  17.5 us (34%)
  starting transfers between devices  15.6 us (31%)
  Pallas kernels  12.9 us (25%)
  other arithmetic  3.33 us (7%)
  local copies, waits for them, and re-layouts  0.77 us (2%)
  between operations  0.71 us (1%)
    ppermute x15, waiting for transfers between devices, swap(): lax.ppermute(x, axis, [(i, i ^ bit) for i in range(lax.axis_size(axis))])  17.5 us
    ppermute x15, starting transfers between devices, swap(): lax.ppermute(x, axis, [(i, i ^ bit) for i in range(lax.axis_size(axis))])  15.6 us
    pallas_call x2, Pallas kernels, block_call(): pl.pallas_call(functools.partial(block_kernel, blocks, first, last, span,...  12.1 us
    transpose x2, other arithmetic, per_device(): return (joined(g).T, joined(h).T, grad_right.T, hess_right.T, inner)  1.66 us
  transfers between devices with their start and end apart: 15, of which 7 were waited for; matrix products, arithmetic and copies ran while one was open for 3% of the time, Pallas kernels for 13%

profile of v2, /device:TPU:0, one launch (start us, length us, event | category | flops | bytes accessed | tf_op | source)
XLA Modules:
  0.0 50.8 jit_solution(11109638506144961092)
XLA Ops:
  0.6 0.8 %pad_maximum_fusion.refs_2_ = f32[128,128]{1,0:T(8,128)S(1)} fusion(f32[64,128]{1,0:T(8,128)} %bitcast.20, f32[64,128]{1,0:T(8,128)} %bitcast.21), kind=kLoop, calls=%fused_computation.8 | loop fusion | flops 16384 | bytes 131072 | tf_op jit(solution)/shard_map/concatenate | solution.py:290
  1.4 5.0 %collective-permute-start.2 = (f32[128,128]{1,0:T(8,128)S(1)}, f32[128,128]{1,0:T(8,128)S(1)}, u32[]{:S(2)}, u32[]{:S(2)}) collective-permute-start(f32[128,128]{1,0:T(8,128)S(1)} %pad_maximum_fusion.refs_2_), channel_id=1, source_target_pairs={{0,12},{4,8},{8,4},{12,0},{1,13},{5,9},{9,5},{13,1},{2,14},{6,10},... | collective-permute-start | bytes 196616 | tf_op jit(solution)/shard_map/ppermute | solution.py:277
  6.5 0.6 %collective-permute-start = (f32[128,128]{1,0:T(8,128)S(1)}, f32[128,128]{1,0:T(8,128)S(1)}, u32[]{:S(2)}, u32[]{:S(2)}) collective-permute-start(f32[128,128]{1,0:T(8,128)S(1)} %pad_maximum_fusion.refs_2_), channel_id=1, source_target_pairs={{0,4},{4,0},{8,12},{12,8},{1,5},{5,1},{9,13},{13,9},{2,6},{6,2},{1... | collective-permute-start | bytes 196616 | tf_op jit(solution)/shard_map/ppermute | solution.py:277
  7.1 0.1 stack.31.where
  7.2 0.7 %copy-done = s32[16,4]{0,1:T(4,128)S(1)} copy-done((s32[16,4]{0,1:T(4,128)S(1)}, s32[16,4]{0,1:T(4,128)}, u32[]{:S(2)}) %copy-start) | copy-done | bytes 280
  7.9 5.8 %own_block.1 = (bf16[2048,256]{1,0:T(8,128)(2,1)S(1)}, bf16[256,2048]{1,0:T(8,128)(2,1)S(1)}, f32[2048,512]{1,0:T(8,128)S(1)}, s32[2048,512]{1,0:T(8,128)S(1)}, ...) custom-call(s32[5]{0:T(128)S(1)} %stack.31.where, ...), custom_call_target="tpu_custom_call" | custom-call | flops 1811939328 | bytes 2097152 | tf_op jit(solution)/shard_map/own_block/pallas_call | solution.py:209
  13.7 0.1 pad_add_fusion.where
  13.8 6.3 %other_blocks.1 = (f32[64,2048]{1,0:T(8,128)S(1)}, f32[64,2048]{1,0:T(8,128)S(1)}, f32[1,128]{1,0:T(1,128)S(1)}, f32[128,128]{1,0:T(8,128)S(1)}, f32[128,128]{1,0:T(8,128)S(1)}, /*index=5*/f32[128,128]{1,0:T(8,128)S(1)}) custom-call(s32[4]{0:T(128)S(1)} %pad_add_fusion.where, s32[4,16]{1,0:T(4,128)S(1)} %bitcast.17, ...), custom_call_target="tpu_custom_call" | custom-call | flops 5435817984 | bytes 6291456 | tf_op jit(solution)/shard_map/other_blocks/pallas_call | solution.py:209
  20.1 0.1 collective-permute-start.3
  20.2 1.9 %collective-permute-done.3 = f32[64,2048]{1,0:T(8,128)S(1)} collective-permute-done((f32[64,2048]{1,0:T(8,128)S(1)}, f32[64,2048]{1,0:T(8,128)S(1)}, u32[]{:S(2)}, u32[]{:S(2)}) %collective-permute-start.3) | collective-permute-done | bytes 524320 | tf_op jit(solution)/shard_map/ppermute | solution.py:277
  22.1 0.1 slice_add_fusion
  22.1 1.7 %collective-permute-start.4 = (f32[32,2048]{1,0:T(8,128)S(1)}, f32[32,2048]{1,0:T(8,128)S(1)}, u32[]{:S(2)}, u32[]{:S(2)}) collective-permute-start(f32[32,2048]{1,0:T(8,128)S(1)} %get-tuple-element.44.a), channel_id=1, source_target_pairs={{0,2},{1,3},{2,0},{3,1},{4,6},{5,7},{6,4},{7,5},{8,10},{9,11},{10,... | collective-permute-start | bytes 786440 | tf_op jit(solution)/shard_map/ppermute | solution.py:277
  23.8 0.4 collective-permute-start.10
  24.2 1.4 %collective-permute-start.5 = (f32[128,128]{1,0:T(8,128)S(1)}, f32[128,128]{1,0:T(8,128)S(1)}, u32[]{:S(2)}, u32[]{:S(2)}) collective-permute-start(f32[128,128]{1,0:T(8,128)S(1)} %get-tuple-element.33), channel_id=1, source_target_pairs={{0,4},{4,0},{8,12},{12,8},{1,5},{5,1},{9,13},{13,9},{2,6},{6,2},{1... | collective-permute-start | bytes 196616 | tf_op jit(solution)/shard_map/ppermute | solution.py:277
  25.6 3.0 %collective-permute-start.6 = (f32[128,128]{1,0:T(8,128)S(1)}, f32[128,128]{1,0:T(8,128)S(1)}, u32[]{:S(2)}, u32[]{:S(2)}) collective-permute-start(f32[128,128]{1,0:T(8,128)S(1)} %get-tuple-element.34), channel_id=1, source_target_pairs={{0,8},{4,12},{8,0},{12,4},{1,9},{5,13},{9,1},{13,5},{2,10},{6,14},... | collective-permute-start | bytes 196616 | tf_op jit(solution)/shard_map/ppermute | solution.py:277
  28.6 4.3 %collective-permute-done.6.refs_2_ = f32[128,128]{1,0:T(8,128)S(1)} collective-permute-done((f32[128,128]{1,0:T(8,128)S(1)}, f32[128,128]{1,0:T(8,128)S(1)}, u32[]{:S(2)}, u32[]{:S(2)}) %collective-permute-start.6) | collective-permute-done | bytes 65568 | tf_op jit(solution)/shard_map/ppermute | solution.py:277
  33.0 1.7 %collective-permute-done.7.refs_3_ = f32[128,128]{1,0:T(8,128)S(1)} collective-permute-done((f32[128,128]{1,0:T(8,128)S(1)}, f32[128,128]{1,0:T(8,128)S(1)}, u32[]{:S(2)}, u32[]{:S(2)}) %collective-permute-start.7) | collective-permute-done | bytes 65568 | tf_op jit(solution)/shard_map/ppermute | solution.py:277
  34.7 0.6 %items_total.1 = (f32[64,128]{1,0:T(8,128)}, f32[64,128]{1,0:T(8,128)}, f32[8,128]{1,0:T(8,128)S(1)}) custom-call(f32[128,128]{1,0:T(8,128)S(1)} %get-tuple-element.32.refs_0_, f32[128,128]{1,0:T(8,128)S(1)} %collective-permute-done.5.refs_1_, f32[128,128]{1,0:T(8,128)S(1)} %collective-permute-done.6.refs_2_, f32[128,128]{1,0:T(8,128)S(1)} %collective-permute-done.7.refs_3_, ...), custom_call_target="tpu_custom_call" | custom-call | tf_op jit(solution)/shard_map/items_total/pallas_call | solution.py:237
  35.3 1.5 %collective-permute-start.8 = (f32[8,128]{1,0:T(8,128)S(1)}, f32[8,128]{1,0:T(8,128)S(1)}, u32[]{:S(2)}, u32[]{:S(2)}) collective-permute-start(f32[8,128]{1,0:T(8,128)S(1)} %get-tuple-element.38), channel_id=1, source_target_pairs={{0,2},{1,3},{2,0},{3,1},{4,6},{5,7},{6,4},{7,5},{8,10},{9,11},{10,... | collective-permute-start | bytes 12296 | tf_op jit(solution)/shard_map/ppermute | solution.py:277
  36.8 2.1 %collective-permute-done.8 = f32[8,128]{1,0:T(8,128)S(1)} collective-permute-done((f32[8,128]{1,0:T(8,128)S(1)}, f32[8,128]{1,0:T(8,128)S(1)}, u32[]{:S(2)}, u32[]{:S(2)}) %collective-permute-start.8) | collective-permute-done | bytes 4128 | tf_op jit(solution)/shard_map/ppermute | solution.py:277
  38.9 0.1 squares.1
  39.0 0.1 collective-permute-start.9
  39.1 0.1 collective-permute-start.12
  39.1 3.6 %collective-permute-done.12 = f32[8,128]{1,0:T(8,128)S(1)} collective-permute-done((f32[8,128]{1,0:T(8,128)S(1)}, f32[8,128]{1,0:T(8,128)S(1)}, u32[]{:S(2)}, u32[]{:S(2)}) %collective-permute-start.12) | collective-permute-done | bytes 4128 | tf_op jit(solution)/shard_map/ppermute | solution.py:277
  42.7 1.2 %collective-permute-start.13 = (f32[8,128]{1,0:T(8,128)S(1)}, f32[8,128]{1,0:T(8,128)S(1)}, u32[]{:S(2)}, u32[]{:S(2)}) collective-permute-start(f32[8,128]{1,0:T(8,128)S(1)} %add.27), channel_id=1, source_target_pairs={{0,8},{4,12},{8,0},{12,4},{1,9},{5,13},{9,1},{13,5},{2,10},{6,14},... | collective-permute-start | bytes 12296 | tf_op jit(solution)/shard_map/ppermute | solution.py:277
  43.9 3.3 %collective-permute-done.13 = f32[8,128]{1,0:T(8,128)S(1)} collective-permute-done((f32[8,128]{1,0:T(8,128)S(1)}, f32[8,128]{1,0:T(8,128)S(1)}, u32[]{:S(2)}, u32[]{:S(2)}) %collective-permute-start.13) | collective-permute-done | bytes 4128 | tf_op jit(solution)/shard_map/ppermute | solution.py:277
  47.3 0.6 %collective-permute-start.11 = (f32[32,2048]{1,0:T(8,128)S(1)}, f32[32,2048]{1,0:T(8,128)S(1)}, u32[]{:S(2)}, u32[]{:S(2)}) collective-permute-start(f32[32,2048]{1,0:T(8,128)S(1)} %add.38), channel_id=1, source_target_pairs={{0,1},{1,0},{2,3},{3,2},{4,5},{5,4},{6,7},{7,6},{8,9},{9,8},{10,11... | collective-permute-start | bytes 786440 | tf_op jit(solution)/shard_map/ppermute | solution.py:277
  47.9 0.6 %collective-permute-done.14 = f32[8,128]{1,0:T(8,128)S(1)} collective-permute-done((f32[8,128]{1,0:T(8,128)S(1)}, f32[8,128]{1,0:T(8,128)S(1)}, u32[]{:S(2)}, u32[]{:S(2)}) %collective-permute-start.14) | collective-permute-done | bytes 4128 | tf_op jit(solution)/shard_map/ppermute | solution.py:277
  48.4 0.6 %slice_reduce_fusion = f32[2]{0:T(128)} fusion(f32[8,128]{1,0:T(8,128)S(1)} %add.29), kind=kLoop, calls=%fused_computation.9 | loop fusion | flops 254 | bytes 1032 | tf_op jit(solution)/shard_map/reduce_sum | solution.py:339
  49.0 0.1 broadcast_select_fusion.3
  49.1 0.8 %maximum_bitcast_fusion = f32[2048,64]{0,1:T(8,128)} fusion(f32[32,2048]{1,0:T(8,128)S(1)} %get-tuple-element.48, f32[32,2048]{1,0:T(8,128)S(1)} %get-tuple-element.47), kind=kLoop, calls=%fused_computation | loop fusion | flops 131072 | bytes 1048576 | tf_op jit(solution)/shard_map/transpose | solution.py:345
  50.0 0.8 %maximum_bitcast_fusion.1 = f32[2048,64]{0,1:T(8,128)} fusion(f32[32,2048]{1,0:T(8,128)S(1)} %get-tuple-element.46, f32[32,2048]{1,0:T(8,128)S(1)} %get-tuple-element.45), kind=kLoop, calls=%fused_computation.1 | loop fusion | flops 131072 | bytes 1048576 | tf_op jit(solution)/shard_map/transpose | solution.py:345
  (18 shorter events, 0.1 us)
Async XLA Ops:
  1.4 12.3 %collective-permute-start.2 = (f32[128,128]{1,0:T(8,128)S(1)}, f32[128,128]{1,0:T(8,128)S(1)}, u32[]{:S(2)}, u32[]{:S(2)}) collective-permute-start(f32[128,128]{1,0:T(8,128)S(1)} %pad_maximum_fusion.refs_2_), channel_id=1, source_target_pairs={{0,12},{4,8},{8,4},{12,0},{1,13},{5,9},{9,5},{13,1},{2,14},{6,10},... | collective-permute-start | bytes 196616 | tf_op jit(solution)/shard_map/ppermute | solution.py:277
  6.5 7.3 %collective-permute-start.1 = (f32[128,128]{1,0:T(8,128)S(1)}, f32[128,128]{1,0:T(8,128)S(1)}, u32[]{:S(2)}, u32[]{:S(2)}) collective-permute-start(f32[128,128]{1,0:T(8,128)S(1)} %pad_maximum_fusion.refs_2_), channel_id=1, source_target_pairs={{0,8},{4,12},{8,0},{12,4},{1,9},{5,13},{9,1},{13,5},{2,10},{6,14},... | collective-permute-start | bytes 196616 | tf_op jit(solution)/shard_map/ppermute | solution.py:277
  6.5 7.3 %collective-permute-start = (f32[128,128]{1,0:T(8,128)S(1)}, f32[128,128]{1,0:T(8,128)S(1)}, u32[]{:S(2)}, u32[]{:S(2)}) collective-permute-start(f32[128,128]{1,0:T(8,128)S(1)} %pad_maximum_fusion.refs_2_), channel_id=1, source_target_pairs={{0,4},{4,0},{8,12},{12,8},{1,5},{5,1},{9,13},{13,9},{2,6},{6,2},{1... | collective-permute-start | bytes 196616 | tf_op jit(solution)/shard_map/ppermute | solution.py:277
  7.2 0.7 %copy-start = (s32[16,4]{0,1:T(4,128)S(1)}, s32[16,4]{0,1:T(4,128)}, u32[]{:S(2)}) copy-start(s32[16,4]{0,1:T(4,128)} %param.9) | copy-start | bytes 772
  20.1 2.0 %collective-permute-start.3 = (f32[64,2048]{1,0:T(8,128)S(1)}, f32[64,2048]{1,0:T(8,128)S(1)}, u32[]{:S(2)}, u32[]{:S(2)}) collective-permute-start(f32[64,2048]{1,0:T(8,128)S(1)} %get-tuple-element.31), channel_id=1, source_target_pairs={{0,1},{1,0},{2,3},{3,2},{4,5},{5,4},{6,7},{7,6},{8,9},{9,8},{10,11... | collective-permute-start | bytes 1572872 | tf_op jit(solution)/shard_map/ppermute | solution.py:277
  22.1 16.8 %collective-permute-start.4 = (f32[32,2048]{1,0:T(8,128)S(1)}, f32[32,2048]{1,0:T(8,128)S(1)}, u32[]{:S(2)}, u32[]{:S(2)}) collective-permute-start(f32[32,2048]{1,0:T(8,128)S(1)} %get-tuple-element.44.a), channel_id=1, source_target_pairs={{0,2},{1,3},{2,0},{3,1},{4,6},{5,7},{6,4},{7,5},{8,10},{9,11},{10,... | collective-permute-start | bytes 786440 | tf_op jit(solution)/shard_map/ppermute | solution.py:277
  23.8 23.4 %collective-permute-start.10 = (f32[32,2048]{1,0:T(8,128)S(1)}, f32[32,2048]{1,0:T(8,128)S(1)}, u32[]{:S(2)}, u32[]{:S(2)}) collective-permute-start(f32[32,2048]{1,0:T(8,128)S(1)} %get-tuple-element.43.a), channel_id=1, source_target_pairs={{0,2},{1,3},{2,0},{3,1},{4,6},{5,7},{6,4},{7,5},{8,10},{9,11},{10,... | collective-permute-start | bytes 786440 | tf_op jit(solution)/shard_map/ppermute | solution.py:277
  24.2 4.4 %collective-permute-start.5 = (f32[128,128]{1,0:T(8,128)S(1)}, f32[128,128]{1,0:T(8,128)S(1)}, u32[]{:S(2)}, u32[]{:S(2)}) collective-permute-start(f32[128,128]{1,0:T(8,128)S(1)} %get-tuple-element.33), channel_id=1, source_target_pairs={{0,4},{4,0},{8,12},{12,8},{1,5},{5,1},{9,13},{13,9},{2,6},{6,2},{1... | collective-permute-start | bytes 196616 | tf_op jit(solution)/shard_map/ppermute | solution.py:277
  25.6 7.4 %collective-permute-start.6 = (f32[128,128]{1,0:T(8,128)S(1)}, f32[128,128]{1,0:T(8,128)S(1)}, u32[]{:S(2)}, u32[]{:S(2)}) collective-permute-start(f32[128,128]{1,0:T(8,128)S(1)} %get-tuple-element.34), channel_id=1, source_target_pairs={{0,8},{4,12},{8,0},{12,4},{1,9},{5,13},{9,1},{13,5},{2,10},{6,14},... | collective-permute-start | bytes 196616 | tf_op jit(solution)/shard_map/ppermute | solution.py:277
  28.6 6.1 %collective-permute-start.7 = (f32[128,128]{1,0:T(8,128)S(1)}, f32[128,128]{1,0:T(8,128)S(1)}, u32[]{:S(2)}, u32[]{:S(2)}) collective-permute-start(f32[128,128]{1,0:T(8,128)S(1)} %get-tuple-element.35), channel_id=1, source_target_pairs={{0,12},{4,8},{8,4},{12,0},{1,13},{5,9},{9,5},{13,1},{2,14},{6,10},... | collective-permute-start | bytes 196616 | tf_op jit(solution)/shard_map/ppermute | solution.py:277
  35.3 3.6 %collective-permute-start.8 = (f32[8,128]{1,0:T(8,128)S(1)}, f32[8,128]{1,0:T(8,128)S(1)}, u32[]{:S(2)}, u32[]{:S(2)}) collective-permute-start(f32[8,128]{1,0:T(8,128)S(1)} %get-tuple-element.38), channel_id=1, source_target_pairs={{0,2},{1,3},{2,0},{3,1},{4,6},{5,7},{6,4},{7,5},{8,10},{9,11},{10,... | collective-permute-start | bytes 12296 | tf_op jit(solution)/shard_map/ppermute | solution.py:277
  39.0 10.1 %collective-permute-start.9 = (f32[32,2048]{1,0:T(8,128)S(1)}, f32[32,2048]{1,0:T(8,128)S(1)}, u32[]{:S(2)}, u32[]{:S(2)}) collective-permute-start(f32[32,2048]{1,0:T(8,128)S(1)} %get-tuple-element.39), channel_id=1, source_target_pairs={{0,1},{1,0},{2,3},{3,2},{4,5},{5,4},{6,7},{7,6},{8,9},{9,8},{10,11... | collective-permute-start | bytes 786440 | tf_op jit(solution)/shard_map/ppermute | solution.py:277
  39.1 3.7 %collective-permute-start.12 = (f32[8,128]{1,0:T(8,128)S(1)}, f32[8,128]{1,0:T(8,128)S(1)}, u32[]{:S(2)}, u32[]{:S(2)}) collective-permute-start(f32[8,128]{1,0:T(8,128)S(1)} %get-tuple-element.40.after), channel_id=1, source_target_pairs={{0,4},{4,0},{8,12},{12,8},{1,5},{5,1},{9,13},{13,9},{2,6},{6,2},{1... | collective-permute-start | bytes 12296 | tf_op jit(solution)/shard_map/ppermute | solution.py:277
  42.7 4.5 %collective-permute-start.13 = (f32[8,128]{1,0:T(8,128)S(1)}, f32[8,128]{1,0:T(8,128)S(1)}, u32[]{:S(2)}, u32[]{:S(2)}) collective-permute-start(f32[8,128]{1,0:T(8,128)S(1)} %add.27), channel_id=1, source_target_pairs={{0,8},{4,12},{8,0},{12,4},{1,9},{5,13},{9,1},{13,5},{2,10},{6,14},... | collective-permute-start | bytes 12296 | tf_op jit(solution)/shard_map/ppermute | solution.py:277
  47.2 1.2 %collective-permute-start.14 = (f32[8,128]{1,0:T(8,128)S(1)}, f32[8,128]{1,0:T(8,128)S(1)}, u32[]{:S(2)}, u32[]{:S(2)}) collective-permute-start(f32[8,128]{1,0:T(8,128)S(1)} %add.28), channel_id=1, source_target_pairs={{0,1},{1,0},{2,3},{3,2},{4,5},{5,4},{6,7},{7,6},{8,9},{9,8},{10,11... | collective-permute-start | bytes 12296 | tf_op jit(solution)/shard_map/ppermute | solution.py:277
  47.3 2.6 %collective-permute-start.11 = (f32[32,2048]{1,0:T(8,128)S(1)}, f32[32,2048]{1,0:T(8,128)S(1)}, u32[]{:S(2)}, u32[]{:S(2)}) collective-permute-start(f32[32,2048]{1,0:T(8,128)S(1)} %add.38), channel_id=1, source_target_pairs={{0,1},{1,0},{2,3},{3,2},{4,5},{5,4},{6,7},{7,6},{8,9},{9,8},{10,11... | collective-permute-start | bytes 786440 | tf_op jit(solution)/shard_map/ppermute | solution.py:277

commit v3 on v2

--- a/solution.py
+++ b/solution.py
@@ -28,7 +28,7 @@
     return functools.reduce(jnp.add, [total[:, i : i + 128] for i in range(0, total.shape[1], 128)])
 
 
-def first_loads(where, rows, factors, factors_to, factor_sems, grids, grids_to, own_sems, other_sems):
+def first_loads(where, rows, factors, factors_to, factor_sems, grids, grids_to, own_sems):
     users, width = grids[0].shape
     wide = 128
     block = lambda k: pl.ds(pl.multiple_of(where[k] * wide, wide), wide)
@@ -41,19 +41,24 @@
                 for i, (a, b) in enumerate(zip(factors, factors_to))
             ]
             + [
-                pltpu.make_async_copy(a.at[here, block(0)], b.at[here, block(0)], own_sems.at[i, step])
+                pltpu.make_async_copy(a.at[here, block(0)], b.at[here], own_sems.at[i, step])
                 for i, (a, b) in enumerate(zip(grids, grids_to))
             ]
         )
-    rest = [
-        pltpu.make_async_copy(a.at[:, block(k)], b.at[:, block(k)], other_sems.at[i, k - 1])
-        for k in range(1, width // wide)
+    return steps
+
+
+def other_loads(where, blocks, here, grids, grids_to, sems):
+    wide = 128
+    block = lambda k: pl.ds(pl.multiple_of(where[k] * wide, wide), wide)
+    return [
+        pltpu.make_async_copy(a.at[here, block(k)], b.at[:, block(k)], sems.at[i, j])
+        for j, k in enumerate(blocks)
         for i, (a, b) in enumerate(zip(grids, grids_to))
     ]
-    return steps, rest
-
-
-def block_kernel(blocks, first, last, span, rows, tile, loop, where, pattern, ratings, mask, *refs):
+
+
+def block_kernel(blocks, first, last, span, rows, tile, where, pattern, ratings, mask, *refs):
     refs = list(refs)
     take = lambda n: [refs.pop(0) for _ in range(n)]
     if first:
@@ -63,10 +68,8 @@
         left_dir = take(1)[0] if last else None
     panels = take(blocks)
     start, stop = span
-    items_in = take(blocks) if last and start > 0 else None
     if first:
-        factors_t, factors, ratings_hbm, mask_hbm = *take(2), ratings, mask
-        ratings, mask, left_dir = take(3)
+        factors_t, factors, all_ratings, all_mask, left_dir = take(5)
     if last:
         keep, send = take(2)
     else:
@@ -75,12 +78,16 @@
     items = take(blocks)
     forward, forward_low, back = take(3)
     if first:
-        left, factor_sems, own_sems, other_sems = refs
+        left, own_ratings, own_mask, factor_sems, own_sems, other_sems = refs
         loads = first_loads(
             where, rows, (left_hbm, left_dir_hbm), (left, left_dir), factor_sems,
-            (ratings_hbm, mask_hbm), (ratings, mask), own_sems, other_sems,
+            (ratings, mask), (own_ratings, own_mask), own_sems,
         )
-        for copy in itertools.chain(*loads[0], loads[1]):
+        late = other_loads(
+            where, range(1, ratings.shape[1] // 128), pl.ds(0, mask.shape[0]),
+            (ratings, mask), (all_ratings, all_mask), other_sems,
+        )
+        for copy in itertools.chain(*loads):
             copy.start()
     rank2, wide = panels[0].shape
     rank = rank2 // 2
@@ -111,14 +118,17 @@
         high, low = halves(s)
         back[k, :, : 2 * rank] = high
         back[k, :, 2 * rank :] = low
-        items[k][...] = jnp.zeros_like(items[k]) if items_in is None else items_in[k][...]
+        items[k][...] = jnp.zeros_like(items[k])
     curve[...] = jnp.zeros_like(curve)
 
     def do(step):
-        here = pl.ds(step if isinstance(step, int) else pl.multiple_of(step, rows), rows)
+        here = pl.ds(step, rows)
         if first:
-            for copy in loads[0][step // rows]:
+            for copy in loads[step // rows]:
                 copy.wait()
+            if step == start:
+                for copy in late:
+                    copy.start()
             both = jnp.concatenate([left[:, here], left_dir[:, here]], axis=0)
             high, low = halves(both)
             factors[: 2 * rank, here] = high
@@ -130,9 +140,13 @@
         else:
             total = acc[here, :]
         for k in range(blocks):
-            columns = pl.ds(pl.multiple_of(where[k] * wide, wide), wide)
+            if first:
+                rating, seen = own_ratings[here, :], own_mask[here, :]
+            else:
+                columns = pl.ds(pl.multiple_of(where[k] * wide, wide), wide)
+                rating, seen = ratings[here, columns], mask[here, columns]
+            seen = seen.astype(F32)
             raw = dot(factors_t[here, :], forward[k]) + dot(factors_t[here, : 2 * rank], forward_low[k])
-            seen = mask[here, columns].astype(F32)
             seen = jnp.concatenate(
                 [
                     seen[t * tile : (t + 1) * tile]
@@ -141,7 +155,7 @@
                 ],
                 axis=0,
             )
-            res = seen * (raw[:, :wide] - ratings[here, columns])
+            res = seen * (raw[:, :wide] - rating)
             change = seen * raw[:, wide:]
             rc_high, rc_low = halves(jnp.concatenate([res, change], axis=1))
             out = dot(rc_high, back[k])
@@ -153,7 +167,7 @@
             items[k][rank:] += got[:rank, wide:] + got[rank:, :wide]
         if last:
             user = total.T
-            there = pl.ds(step - start if isinstance(step, int) else pl.multiple_of(step - start, rows), rows)
+            there = pl.ds(step - start, rows)
             keep[:, there] = user[:rank]
             send[:, there] = user[rank:]
             turned = own_first(left_dir[:, here])
@@ -161,23 +175,16 @@
         else:
             acc_out[here, :] = total
 
-    if loop:
-        def body(i, c):
-            do(start + i * rows)
-            return c
-        lax.fori_loop(0, (stop - start) // rows, body, 0)
-    else:
-        for s in range(start, stop, rows):
-            do(s)
+    for s in range(start, stop, rows):
+        do(s)
     if first:
-        for copy in loads[1]:
+        for copy in late:
             copy.wait()
-    if last and stop == ratings.shape[0] or not last:
-        for k in range(blocks):
-            curve[...] += tile_sum(items[k][rank:] * panels[k][rank:])
-
-
-def block_call(where, pattern, ratings, mask, given, panels, first=False, last=False, span=None, items=(), rows=512, loop=True, name="block"):
+    for k in range(blocks):
+        curve[...] += tile_sum(items[k][rank:] * panels[k][rank:])
+
+
+def block_call(where, pattern, ratings, mask, given, panels, first=False, last=False, span=None, rows=512, name="block"):
     users, width = ratings.shape
     rank = panels[0].shape[0] // 2
     wide = panels[0].shape[1]
@@ -197,17 +204,19 @@
         steps = users // rows
         scratch += [
             pltpu.VMEM((rank, users), F32),
+            pltpu.VMEM((users, wide), ratings.dtype),
+            pltpu.VMEM((users, wide), mask.dtype),
             pltpu.SemaphoreType.DMA((2, steps)),
             pltpu.SemaphoreType.DMA((2, steps)),
             pltpu.SemaphoreType.DMA((2, width // wide - 1)),
         ]
     outs += [shape((rank, count), F32)] * 2 if last else [shape((users, 2 * rank), F32)]
     outs += [shape((1, 128), F32)] + [shape((2 * rank, wide), F32)] * blocks
-    args = [ratings, mask, *given, *panels, *items]
+    args = [ratings, mask, *given, *panels]
     far = 4 if first else 0
     args = [pltpu.with_memory_space_constraint(a, pltpu.HBM) for a in args[:far]] + [pltpu.with_memory_space_constraint(a, pltpu.VMEM) for a in args[far:]]
     return pl.pallas_call(
-        functools.partial(block_kernel, blocks, first, last, span, rows, users // pattern.shape[1], loop),
+        functools.partial(block_kernel, blocks, first, last, span, rows, users // pattern.shape[1]),
         in_specs=[SMEM, SMEM] + [HBM] * far + [VMEM] * (len(args) - far),
         out_specs=[VMEM] * len(outs),
         out_shape=outs,
@@ -215,11 +224,11 @@
         compiler_params=pltpu.CompilerParams(vmem_limit_bytes=24 * 1024 * 1024),
         cost_estimate=pl.CostEstimate(flops=2 * count * wide * blocks * rank * 54, bytes_accessed=8 * count * wide * blocks, transcendentals=0),
         name=name,
-    )(where, pattern, *args)
-
-
-def items_kernel(count, *refs):
-    terms, curves, (grad, hess, sums) = refs[:count], refs[count:-3], refs[-3:]
+    )(where, pltpu.with_memory_space_constraint(pattern, pltpu.HBM), *args)
+
+
+def items_kernel(count, curves, *refs):
+    terms, curve, (grad, hess, sums) = refs[:count], refs[count : count + curves], refs[count + curves :]
     total = functools.reduce(jnp.add, [t[...] for t in terms])
     rank = total.shape[0] // 2
     grad[...] = total[:rank]
@@ -228,7 +237,7 @@
     wide = squares.shape[1]
     if wide < 128:
         squares = jnp.concatenate([squares, jnp.zeros((1, 128 - wide), F32)], axis=1)
-    curve = functools.reduce(jnp.add, [c[...] for c in curves])
+    curve = functools.reduce(jnp.add, [c[...] for c in curve])
     sums[...] = jnp.concatenate([squares, curve, jnp.zeros((6, 128), F32)], axis=0)
 
 
@@ -245,24 +254,23 @@
 
 
 def items_call(terms, curves):
-    rows, wide = terms[0].shape
     return small_call(
-        functools.partial(items_kernel, len(terms)),
+        functools.partial(items_kernel, len(terms), len(curves)),
         [*terms, *curves],
-        [(rows // 2, wide), (rows // 2, wide), (8, 128)],
+        [(terms[0].shape[0] // 2, terms[0].shape[1])] * 2 + [(8, 128)],
         "items_total",
     )
 
 
-def squares_kernel(a, b, sums, total, new):
+def squares_kernel(copies, a, b, sums, total, new):
     x = a[...] + b[...]
     total[...] = x
     new[...] = sums[...]
-    new[0:1] += tile_sum(x * x)
-
-
-def squares_call(a, b, sums):
-    return small_call(squares_kernel, [a, b, sums], [a.shape, sums.shape], "squares")
+    new[0:1] += tile_sum(x * x) * (1.0 / copies)
+
+
+def squares_call(a, b, sums, copies):
+    return small_call(functools.partial(squares_kernel, copies), [a, b, sums], [a.shape, sums.shape], "squares")
 
 
 def add_kernel(a, b, after, total):
@@ -273,8 +281,32 @@
     return small_call(add_kernel, [a, b, after], [a.shape], "add")[0]
 
 
+def inner_kernel(a, b, g, h, inner):
+    x = a[...] + b[...]
+    inner[0] = jnp.sum(x[0:1])
+    inner[1] = jnp.sum(x[1:2])
+
+
+def inner_call(a, b, g, h):
+    a, b = (pltpu.with_memory_space_constraint(x, pltpu.VMEM) for x in (a, b))
+    return pl.pallas_call(
+        inner_kernel,
+        in_specs=[VMEM, VMEM, HBM, HBM],
+        out_specs=SMEM,
+        out_shape=jax.ShapeDtypeStruct((2,), F32),
+        compiler_params=pltpu.CompilerParams(vmem_limit_bytes=4 * 1024 * 1024),
+        name="inner",
+    )(a, b, g, h)
+
+
 def swap(x, axis, bit):
     return lax.ppermute(x, axis, [(i, i ^ bit) for i in range(lax.axis_size(axis))])
+
+
+def swap_both(x, users_bit, items_bit):
+    users, items = lax.axis_size("users"), lax.axis_size("items")
+    pairs = [(u * items + i, (u ^ users_bit) * items + (i ^ items_bit)) for u in range(users) for i in range(items)]
+    return lax.ppermute(x, ("users", "items"), pairs)
 
 
 def bits(axis):
@@ -303,15 +335,14 @@
     table = pattern.T
     factors_t, factors, ratings, entry_mask, left_dir_t, acc, curve_a, item = block_call(
         where(range(len(panels))), table, ratings, entry_mask, [left.T, left_dir.T], panels[:1],
-        first=True, rows=1024, loop=False, name="own_block",
+        first=True, rows=1024, name="own_block",
     )
-    items = [item]
     others = list(range(1, len(panels)))
     keep, send, curve_b, *rest = block_call(
         where(others), table, ratings, entry_mask, [factors_t, factors, acc, left_dir_t], panels[1:],
-        last=True, rows=1024, loop=False, name="other_blocks",
+        last=True, rows=1024, name="other_blocks",
     )
-    items += rest
+    items = [item, *rest]
     got = swap(send, "items", 1)
     half = rank // 2
     g = keep[:half] + got[:half]
@@ -323,26 +354,28 @@
     other_g = swap(g, "items", across[-1])
     other_h = swap(h, "items", across[-1])
     if direct:
-        terms = [items[0]] + [swap(items[k], "users", k) for k in range(1, n)]
+        terms = [items[0]] + [swap(items[k], "users", k) for k in range(n - 1, 0, -1)]
     else:
         terms = [
             lax.psum_scatter(jnp.concatenate(items, axis=1), "users", scatter_dimension=1, tiled=True)
         ]
     grad_right, hess_right, sums = items_call(terms, [curve_a, curve_b])
-    for bit in across:
+    g, sums = squares_call(g, other_g, sums, lax.axis_size("items") // 2)
+    h = add_call(h, other_h, sums)
+    for bit in across[:-1]:
         sums = sums + swap(sums, "items", bit)
-    g, sums = squares_call(g, other_g, sums)
-    h = add_call(h, other_h, sums)
-    for bit in bits("users"):
+    sums = (sums + swap(sums, "users", 1)) + (swap(sums, "items", across[-1]) + swap_both(sums, 1, across[-1]))
+    for bit in bits("users")[1:]:
         sums = sums + swap(sums, "users", bit)
-    sums = sums + swap(sums, "items", 1)
-    inner = jnp.sum(sums[:2], axis=1)
+    far = swap(sums, "items", 1)
 
     def joined(mine):
         other = swap(mine, "items", 1)
         return jnp.concatenate([jnp.where(core == 0, mine, other), jnp.where(core == 0, other, mine)], axis=0)
 
-    return joined(g).T, joined(h).T, grad_right.T, hess_right.T, inner
+    g, h = joined(g), joined(h)
+    inner = inner_call(sums, far, g, h)
+    return g.T, h.T, grad_right.T, hess_right.T, inner
 
 
 def solution(mesh):

time: 51 us -> 45.7 us (0.90)
  waiting for transfers between devices: 17.5 us -> 11.7 us
  starting transfers between devices: 15.6 us -> 17.7 us
  other arithmetic: 3.33 us -> 2.12 us
  local copies, waits for them, and re-layouts: 0.77 us -> 0.08 us
    ppermute x15, waiting for transfers between devices: 17.5 us -> 10.7 us  [swap(): lax.ppermute(x, axis, [(i, i ^ bit) for i in range(lax.axis_size(axis))])]
    transpose x2 -> x0, other arithmetic: 1.66 us -> none  [per_device(): return (joined(g).T, joined(h).T, grad_right.T, hess_right.T, inner)]
    concatenate x0 -> x1, other arithmetic: none -> 1.1 us  [joined(): jnp.concatenate([jnp.where(core == 0, mine, other), jnp.where(core == 0,...]
    ppermute x0 -> x1, starting transfers between devices: none -> 1.07 us  [swap_both(): return lax.ppermute(x, ('users', 'items'), pairs)]
    ppermute x0 -> x1, waiting for transfers between devices: none -> 1.02 us  [swap_both(): return lax.ppermute(x, ('users', 'items'), pairs)]
    ppermute x15, starting transfers between devices: 15.6 us -> 16.6 us  [swap(): lax.ppermute(x, axis, [(i, i ^ bit) for i in range(lax.axis_size(axis))])]
    unnamed x2 -> x0, local copies, waits for them, and re-layouts: 0.68 us -> none
    pallas_call x0 -> x1, Pallas kernels: none -> 0.64 us  [inner_call(): pl.pallas_call(inner_kernel, in_specs=[VMEM, VMEM, HBM, HBM], out_specs=S...]
  transfers between devices with their start and end apart: 15 -> 16, of which waited for: 7 -> 7; matrix products, arithmetic and copies ran while one was open for 3% -> 3% of each run, Pallas kernels for 13% -> 14%
where the time goes in v3:
time: 45.7 us; the launch traced here: 45.4 us
  starting transfers between devices  17.7 us (39%)
  Pallas kernels  13.1 us (29%)
  waiting for transfers between devices  11.7 us (26%)
  other arithmetic  2.12 us (5%)
  between operations  0.72 us (2%)
    ppermute x15, starting transfers between devices, swap(): lax.ppermute(x, axis, [(i, i ^ bit) for i in range(lax.axis_size(axis))])  16.6 us
    pallas_call x2, Pallas kernels, block_call(): pl.pallas_call(functools.partial(block_kernel, blocks, first, last, span,...  11.8 us
    ppermute x15, waiting for transfers between devices, swap(): lax.ppermute(x, axis, [(i, i ^ bit) for i in range(lax.axis_size(axis))])  10.7 us
    concatenate x1, other arithmetic, joined(): jnp.concatenate([jnp.where(core == 0, mine, other), jnp.where(core == 0,...  1.1 us
    ppermute x1, starting transfers between devices, swap_both(): return lax.ppermute(x, ('users', 'items'), pairs)  1.07 us
    ppermute x1, waiting for transfers between devices, swap_both(): return lax.ppermute(x, ('users', 'items'), pairs)  1.02 us
  transfers between devices with their start and end apart: 16, of which 7 were waited for; matrix products, arithmetic and copies ran while one was open for 3% of the time, Pallas kernels for 14%

profile of v3, /device:TPU:0, one launch (start us, length us, event | category | flops | bytes accessed | tf_op | source)
XLA Modules:
  0.0 45.4 jit_solution(4354407616320835470)
XLA Ops:
  0.6 0.8 %pad_maximum_fusion.2.refs_2_ = f32[128,128]{1,0:T(8,128)S(1)} fusion(f32[64,128]{1,0:T(8,128)} %bitcast.18, f32[64,128]{1,0:T(8,128)} %bitcast.19), kind=kLoop, calls=%fused_computation.8 | loop fusion | flops 16384 | bytes 131072 | tf_op jit(solution)/shard_map/concatenate | solution.py:322
  1.4 5.0 %collective-permute-start.2 = (f32[128,128]{1,0:T(8,128)S(1)}, f32[128,128]{1,0:T(8,128)S(1)}, u32[]{:S(2)}, u32[]{:S(2)}) collective-permute-start(f32[128,128]{1,0:T(8,128)S(1)} %pad_maximum_fusion.2.refs_2_), channel_id=1, source_target_pairs={{0,12},{4,8},{8,4},{12,0},{1,13},{5,9},{9,5},{13,1},{2,14},{6,10},... | collective-permute-start | bytes 196616 | tf_op jit(solution)/shard_map/ppermute | solution.py:303
  6.5 0.6 %collective-permute-start = (f32[128,128]{1,0:T(8,128)S(1)}, f32[128,128]{1,0:T(8,128)S(1)}, u32[]{:S(2)}, u32[]{:S(2)}) collective-permute-start(f32[128,128]{1,0:T(8,128)S(1)} %pad_maximum_fusion.2.refs_2_), channel_id=1, source_target_pairs={{0,4},{4,0},{8,12},{12,8},{1,5},{5,1},{9,13},{13,9},{2,6},{6,2},{1... | collective-permute-start | bytes 196616 | tf_op jit(solution)/shard_map/ppermute | solution.py:303
  7.1 0.1 stack.31.where
  7.2 5.4 %own_block.1 = (bf16[2048,256]{1,0:T(8,128)(2,1)S(1)}, bf16[256,2048]{1,0:T(8,128)(2,1)S(1)}, f32[2048,512]{1,0:T(8,128)S(1)}, s32[2048,512]{1,0:T(8,128)S(1)}, ...) custom-call(s32[5]{0:T(128)S(1)} %stack.31.where, ...), custom_call_target="tpu_custom_call" | custom-call | flops 1811939328 | bytes 2097152 | tf_op jit(solution)/shard_map/own_block/pallas_call | solution.py:218
  12.6 0.1 pad_add_fusion.where
  12.7 0.0 collective-permute-done.1.refs_5_
  12.7 6.4 %other_blocks.1 = (f32[64,2048]{1,0:T(8,128)S(1)}, f32[64,2048]{1,0:T(8,128)S(1)}, f32[1,128]{1,0:T(1,128)S(1)}, f32[128,128]{1,0:T(8,128)S(1)}, f32[128,128]{1,0:T(8,128)S(1)}, /*index=5*/f32[128,128]{1,0:T(8,128)S(1)}) custom-call(s32[4]{0:T(128)S(1)} %pad_add_fusion.where, s32[4,16]{1,0:T(4,128)} %bitcast.21, f32[2048,512]{1,0:T(8,128)S(1)} %get-tuple-element.24.ratings, ...), custom_call_target="tpu_custom_call" | custom-call | flops 5435817984 | bytes 6291456 | tf_op jit(solution)/shard_map/other_blocks/pallas_call | solution.py:218
  19.0 0.1 collective-permute-start.3
  19.1 1.9 %collective-permute-done.3 = f32[64,2048]{1,0:T(8,128)S(1)} collective-permute-done((f32[64,2048]{1,0:T(8,128)S(1)}, f32[64,2048]{1,0:T(8,128)S(1)}, u32[]{:S(2)}, u32[]{:S(2)}) %collective-permute-start.3) | collective-permute-done | bytes 524320 | tf_op jit(solution)/shard_map/ppermute | solution.py:303
  21.0 0.1 slice_add_fusion
  21.1 1.7 %collective-permute-start.4 = (f32[32,2048]{1,0:T(8,128)S(1)}, f32[32,2048]{1,0:T(8,128)S(1)}, u32[]{:S(2)}, u32[]{:S(2)}) collective-permute-start(f32[32,2048]{1,0:T(8,128)S(1)} %get-tuple-element.44.a), channel_id=1, source_target_pairs={{0,2},{1,3},{2,0},{3,1},{4,6},{5,7},{6,4},{7,5},{8,10},{9,11},{10,... | collective-permute-start | bytes 786440 | tf_op jit(solution)/shard_map/ppermute | solution.py:303
  22.8 3.6 %collective-permute-start.5 = (f32[128,128]{1,0:T(8,128)S(1)}, f32[128,128]{1,0:T(8,128)S(1)}, u32[]{:S(2)}, u32[]{:S(2)}) collective-permute-start(f32[128,128]{1,0:T(8,128)S(1)} %get-tuple-element.33), channel_id=1, source_target_pairs={{0,12},{4,8},{8,4},{12,0},{1,13},{5,9},{9,5},{13,1},{2,14},{6,10},... | collective-permute-start | bytes 196616 | tf_op jit(solution)/shard_map/ppermute | solution.py:303
  26.4 0.8 %collective-permute-start.7 = (f32[128,128]{1,0:T(8,128)S(1)}, f32[128,128]{1,0:T(8,128)S(1)}, u32[]{:S(2)}, u32[]{:S(2)}) collective-permute-start(f32[128,128]{1,0:T(8,128)S(1)} %get-tuple-element.35), channel_id=1, source_target_pairs={{0,4},{4,0},{8,12},{12,8},{1,5},{5,1},{9,13},{13,9},{2,6},{6,2},{1... | collective-permute-start | bytes 196616 | tf_op jit(solution)/shard_map/ppermute | solution.py:303
  27.2 0.4 collective-permute-start.9
  27.6 2.0 %collective-permute-done.5.refs_1_ = f32[128,128]{1,0:T(8,128)S(1)} collective-permute-done((f32[128,128]{1,0:T(8,128)S(1)}, f32[128,128]{1,0:T(8,128)S(1)}, u32[]{:S(2)}, u32[]{:S(2)}) %collective-permute-start.5) | collective-permute-done | bytes 65568 | tf_op jit(solution)/shard_map/ppermute | solution.py:303
  29.6 2.5 %collective-permute-done.6.refs_2_ = f32[128,128]{1,0:T(8,128)S(1)} collective-permute-done((f32[128,128]{1,0:T(8,128)S(1)}, f32[128,128]{1,0:T(8,128)S(1)}, u32[]{:S(2)}, u32[]{:S(2)}) %collective-permute-start.6) | collective-permute-done | bytes 65568 | tf_op jit(solution)/shard_map/ppermute | solution.py:303
  32.1 0.6 %items_total.1 = (f32[64,128]{1,0:T(8,128)}, f32[64,128]{1,0:T(8,128)}, f32[8,128]{1,0:T(8,128)S(1)}) custom-call(f32[128,128]{1,0:T(8,128)S(1)} %get-tuple-element.32.refs_0_, f32[128,128]{1,0:T(8,128)S(1)} %collective-permute-done.5.refs_1_, f32[128,128]{1,0:T(8,128)S(1)} %collective-permute-done.6.refs_2_, f32[128,128]{1,0:T(8,128)S(1)} %collective-permute-done.7.refs_3_, ...), custom_call_target="tpu_custom_call" | custom-call | tf_op jit(solution)/shard_map/items_total/pallas_call | solution.py:246
  32.7 0.1 squares.1
  32.8 0.1 collective-permute-start.8
  32.9 1.1 %collective-permute-start.13 = (f32[8,128]{1,0:T(8,128)S(1)}, f32[8,128]{1,0:T(8,128)S(1)}, u32[]{:S(2)}, u32[]{:S(2)}) collective-permute-start(f32[8,128]{1,0:T(8,128)S(1)} %get-tuple-element.40.after), channel_id=1, source_target_pairs={{0,6},{1,7},{2,4},{3,5},{4,2},{5,3},{6,0},{7,1},{8,14},{9,15},{10,... | collective-permute-start | bytes 12296 | tf_op jit(solution)/shard_map/ppermute | solution.py:309
  34.0 1.5 %collective-permute-start.12 = (f32[8,128]{1,0:T(8,128)S(1)}, f32[8,128]{1,0:T(8,128)S(1)}, u32[]{:S(2)}, u32[]{:S(2)}) collective-permute-start(f32[8,128]{1,0:T(8,128)S(1)} %get-tuple-element.40.after), channel_id=1, source_target_pairs={{0,2},{1,3},{2,0},{3,1},{4,6},{5,7},{6,4},{7,5},{8,10},{9,11},{10,... | collective-permute-start | bytes 12296 | tf_op jit(solution)/shard_map/ppermute | solution.py:303
  35.4 1.0 %collective-permute-start.11 = (f32[8,128]{1,0:T(8,128)S(1)}, f32[8,128]{1,0:T(8,128)S(1)}, u32[]{:S(2)}, u32[]{:S(2)}) collective-permute-start(f32[8,128]{1,0:T(8,128)S(1)} %get-tuple-element.40.after), channel_id=1, source_target_pairs={{0,4},{4,0},{8,12},{12,8},{1,5},{5,1},{9,13},{13,9},{2,6},{6,2},{1... | collective-permute-start | bytes 12296 | tf_op jit(solution)/shard_map/ppermute | solution.py:303
  36.4 1.0 %collective-permute-done.13 = f32[8,128]{1,0:T(8,128)S(1)} collective-permute-done((f32[8,128]{1,0:T(8,128)S(1)}, f32[8,128]{1,0:T(8,128)S(1)}, u32[]{:S(2)}, u32[]{:S(2)}) %collective-permute-start.13) | collective-permute-done | bytes 4128 | tf_op jit(solution)/shard_map/ppermute | solution.py:309
  37.5 0.1 collective-permute-done.12
  37.6 1.5 %collective-permute-done.11 = f32[8,128]{1,0:T(8,128)S(1)} collective-permute-done((f32[8,128]{1,0:T(8,128)S(1)}, f32[8,128]{1,0:T(8,128)S(1)}, u32[]{:S(2)}, u32[]{:S(2)}) %collective-permute-start.11) | collective-permute-done | bytes 4128 | tf_op jit(solution)/shard_map/ppermute | solution.py:303
  39.1 1.8 %collective-permute-start.14 = (f32[8,128]{1,0:T(8,128)S(1)}, f32[8,128]{1,0:T(8,128)S(1)}, u32[]{:S(2)}, u32[]{:S(2)}) collective-permute-start(f32[8,128]{1,0:T(8,128)S(1)} %add_add_fusion), channel_id=1, source_target_pairs={{0,8},{4,12},{8,0},{12,4},{1,9},{5,13},{9,1},{13,5},{2,10},{6,14},... | collective-permute-start | bytes 12296 | tf_op jit(solution)/shard_map/ppermute | solution.py:303
  40.9 0.1 collective-permute-start.10
  40.9 2.6 %collective-permute-done.14 = f32[8,128]{1,0:T(8,128)S(1)} collective-permute-done((f32[8,128]{1,0:T(8,128)S(1)}, f32[8,128]{1,0:T(8,128)S(1)}, u32[]{:S(2)}, u32[]{:S(2)}) %collective-permute-start.14) | collective-permute-done | bytes 4128 | tf_op jit(solution)/shard_map/ppermute | solution.py:303
  43.6 0.1 broadcast_select_fusion.3
  43.7 1.1 %pad_maximum_fusion = (f32[64,2048]{1,0:T(8,128)S(1)}, f32[2048,64]{0,1:T(8,128)}, f32[2048,64]{0,1:T(8,128)}, f32[64,2048]{1,0:T(8,128)S(1)}) fusion(f32[32,2048]{1,0:T(8,128)S(1)} %get-tuple-element.52, f32[32,2048]{1,0:T(8,128)S(1)} %get-tuple-element.51, f32[32,2048]{1,0:T(8,128)S(1)} %get-tuple-element.50, f32[32,2048]{1,0:T(8,128)S(1)} %get-tuple-element.49), kind=kLoop, calls=%fused_computation | loop fusion | flops 262144 | bytes 3145728 | tf_op jit(solution)/shard_map/concatenate | solution.py:374
  44.8 0.6 %inner.1 = f32[2]{0:T(128)} custom-call(f32[8,128]{1,0:T(8,128)S(1)} %add.29.a, f32[8,128]{1,0:T(8,128)S(1)} %collective-permute-done.15.b, f32[64,2048]{1,0:T(8,128)S(1)} %get-tuple-element.47.g, f32[64,2048]{1,0:T(8,128)S(1)} %get-tuple-element.54.h), custom_call_target="tpu_custom_call" | custom-call | tf_op jit(solution)/shard_map/inner/pallas_call | solution.py:292
  (15 shorter events, 0.1 us)
Async XLA Ops:
  1.4 11.2 %collective-permute-start.2 = (f32[128,128]{1,0:T(8,128)S(1)}, f32[128,128]{1,0:T(8,128)S(1)}, u32[]{:S(2)}, u32[]{:S(2)}) collective-permute-start(f32[128,128]{1,0:T(8,128)S(1)} %pad_maximum_fusion.2.refs_2_), channel_id=1, source_target_pairs={{0,12},{4,8},{8,4},{12,0},{1,13},{5,9},{9,5},{13,1},{2,14},{6,10},... | collective-permute-start | bytes 196616 | tf_op jit(solution)/shard_map/ppermute | solution.py:303
  6.5 6.2 %collective-permute-start.1 = (f32[128,128]{1,0:T(8,128)S(1)}, f32[128,128]{1,0:T(8,128)S(1)}, u32[]{:S(2)}, u32[]{:S(2)}) collective-permute-start(f32[128,128]{1,0:T(8,128)S(1)} %pad_maximum_fusion.2.refs_2_), channel_id=1, source_target_pairs={{0,8},{4,12},{8,0},{12,4},{1,9},{5,13},{9,1},{13,5},{2,10},{6,14},... | collective-permute-start | bytes 196616 | tf_op jit(solution)/shard_map/ppermute | solution.py:303
  6.5 6.2 %collective-permute-start = (f32[128,128]{1,0:T(8,128)S(1)}, f32[128,128]{1,0:T(8,128)S(1)}, u32[]{:S(2)}, u32[]{:S(2)}) collective-permute-start(f32[128,128]{1,0:T(8,128)S(1)} %pad_maximum_fusion.2.refs_2_), channel_id=1, source_target_pairs={{0,4},{4,0},{8,12},{12,8},{1,5},{5,1},{9,13},{13,9},{2,6},{6,2},{1... | collective-permute-start | bytes 196616 | tf_op jit(solution)/shard_map/ppermute | solution.py:303
  19.0 2.0 %collective-permute-start.3 = (f32[64,2048]{1,0:T(8,128)S(1)}, f32[64,2048]{1,0:T(8,128)S(1)}, u32[]{:S(2)}, u32[]{:S(2)}) collective-permute-start(f32[64,2048]{1,0:T(8,128)S(1)} %get-tuple-element.31), channel_id=1, source_target_pairs={{0,1},{1,0},{2,3},{3,2},{4,5},{5,4},{6,7},{7,6},{8,9},{9,8},{10,11... | collective-permute-start | bytes 1572872 | tf_op jit(solution)/shard_map/ppermute | solution.py:303
  21.1 11.7 %collective-permute-start.4 = (f32[32,2048]{1,0:T(8,128)S(1)}, f32[32,2048]{1,0:T(8,128)S(1)}, u32[]{:S(2)}, u32[]{:S(2)}) collective-permute-start(f32[32,2048]{1,0:T(8,128)S(1)} %get-tuple-element.44.a), channel_id=1, source_target_pairs={{0,2},{1,3},{2,0},{3,1},{4,6},{5,7},{6,4},{7,5},{8,10},{9,11},{10,... | collective-permute-start | bytes 786440 | tf_op jit(solution)/shard_map/ppermute | solution.py:303
  22.8 6.8 %collective-permute-start.5 = (f32[128,128]{1,0:T(8,128)S(1)}, f32[128,128]{1,0:T(8,128)S(1)}, u32[]{:S(2)}, u32[]{:S(2)}) collective-permute-start(f32[128,128]{1,0:T(8,128)S(1)} %get-tuple-element.33), channel_id=1, source_target_pairs={{0,12},{4,8},{8,4},{12,0},{1,13},{5,9},{9,5},{13,1},{2,14},{6,10},... | collective-permute-start | bytes 196616 | tf_op jit(solution)/shard_map/ppermute | solution.py:303
  26.4 5.7 %collective-permute-start.6 = (f32[128,128]{1,0:T(8,128)S(1)}, f32[128,128]{1,0:T(8,128)S(1)}, u32[]{:S(2)}, u32[]{:S(2)}) collective-permute-start(f32[128,128]{1,0:T(8,128)S(1)} %get-tuple-element.34), channel_id=1, source_target_pairs={{0,8},{4,12},{8,0},{12,4},{1,9},{5,13},{9,1},{13,5},{2,10},{6,14},... | collective-permute-start | bytes 196616 | tf_op jit(solution)/shard_map/ppermute | solution.py:303
  26.4 5.7 %collective-permute-start.7 = (f32[128,128]{1,0:T(8,128)S(1)}, f32[128,128]{1,0:T(8,128)S(1)}, u32[]{:S(2)}, u32[]{:S(2)}) collective-permute-start(f32[128,128]{1,0:T(8,128)S(1)} %get-tuple-element.35), channel_id=1, source_target_pairs={{0,4},{4,0},{8,12},{12,8},{1,5},{5,1},{9,13},{13,9},{2,6},{6,2},{1... | collective-permute-start | bytes 196616 | tf_op jit(solution)/shard_map/ppermute | solution.py:303
  27.2 13.6 %collective-permute-start.9 = (f32[32,2048]{1,0:T(8,128)S(1)}, f32[32,2048]{1,0:T(8,128)S(1)}, u32[]{:S(2)}, u32[]{:S(2)}) collective-permute-start(f32[32,2048]{1,0:T(8,128)S(1)} %get-tuple-element.43.a), channel_id=1, source_target_pairs={{0,2},{1,3},{2,0},{3,1},{4,6},{5,7},{6,4},{7,5},{8,10},{9,11},{10,... | collective-permute-start | bytes 786440 | tf_op jit(solution)/shard_map/ppermute | solution.py:303
  32.8 10.8 %collective-permute-start.8 = (f32[32,2048]{1,0:T(8,128)S(1)}, f32[32,2048]{1,0:T(8,128)S(1)}, u32[]{:S(2)}, u32[]{:S(2)}) collective-permute-start(f32[32,2048]{1,0:T(8,128)S(1)} %get-tuple-element.39), channel_id=1, source_target_pairs={{0,1},{1,0},{2,3},{3,2},{4,5},{5,4},{6,7},{7,6},{8,9},{9,8},{10,11... | collective-permute-start | bytes 786440 | tf_op jit(solution)/shard_map/ppermute | solution.py:303
  32.9 4.6 %collective-permute-start.13 = (f32[8,128]{1,0:T(8,128)S(1)}, f32[8,128]{1,0:T(8,128)S(1)}, u32[]{:S(2)}, u32[]{:S(2)}) collective-permute-start(f32[8,128]{1,0:T(8,128)S(1)} %get-tuple-element.40.after), channel_id=1, source_target_pairs={{0,6},{1,7},{2,4},{3,5},{4,2},{5,3},{6,0},{7,1},{8,14},{9,15},{10,... | collective-permute-start | bytes 12296 | tf_op jit(solution)/shard_map/ppermute | solution.py:309
  34.0 3.6 %collective-permute-start.12 = (f32[8,128]{1,0:T(8,128)S(1)}, f32[8,128]{1,0:T(8,128)S(1)}, u32[]{:S(2)}, u32[]{:S(2)}) collective-permute-start(f32[8,128]{1,0:T(8,128)S(1)} %get-tuple-element.40.after), channel_id=1, source_target_pairs={{0,2},{1,3},{2,0},{3,1},{4,6},{5,7},{6,4},{7,5},{8,10},{9,11},{10,... | collective-permute-start | bytes 12296 | tf_op jit(solution)/shard_map/ppermute | solution.py:303
  35.4 3.6 %collective-permute-start.11 = (f32[8,128]{1,0:T(8,128)S(1)}, f32[8,128]{1,0:T(8,128)S(1)}, u32[]{:S(2)}, u32[]{:S(2)}) collective-permute-start(f32[8,128]{1,0:T(8,128)S(1)} %get-tuple-element.40.after), channel_id=1, source_target_pairs={{0,4},{4,0},{8,12},{12,8},{1,5},{5,1},{9,13},{13,9},{2,6},{6,2},{1... | collective-permute-start | bytes 12296 | tf_op jit(solution)/shard_map/ppermute | solution.py:303
  39.1 4.5 %collective-permute-start.14 = (f32[8,128]{1,0:T(8,128)S(1)}, f32[8,128]{1,0:T(8,128)S(1)}, u32[]{:S(2)}, u32[]{:S(2)}) collective-permute-start(f32[8,128]{1,0:T(8,128)S(1)} %add_add_fusion), channel_id=1, source_target_pairs={{0,8},{4,12},{8,0},{12,4},{1,9},{5,13},{9,1},{13,5},{2,10},{6,14},... | collective-permute-start | bytes 12296 | tf_op jit(solution)/shard_map/ppermute | solution.py:303
  40.9 2.8 %collective-permute-start.10 = (f32[32,2048]{1,0:T(8,128)S(1)}, f32[32,2048]{1,0:T(8,128)S(1)}, u32[]{:S(2)}, u32[]{:S(2)}) collective-permute-start(f32[32,2048]{1,0:T(8,128)S(1)} %add.41), channel_id=1, source_target_pairs={{0,1},{1,0},{2,3},{3,2},{4,5},{5,4},{6,7},{7,6},{8,9},{9,8},{10,11... | collective-permute-start | bytes 786440 | tf_op jit(solution)/shard_map/ppermute | solution.py:303
  43.6 1.2 %collective-permute-start.15 = (f32[8,128]{1,0:T(8,128)S(1)}, f32[8,128]{1,0:T(8,128)S(1)}, u32[]{:S(2)}, u32[]{:S(2)}) collective-permute-start(f32[8,128]{1,0:T(8,128)S(1)} %add.29.a), channel_id=1, source_target_pairs={{0,1},{1,0},{2,3},{3,2},{4,5},{5,4},{6,7},{7,6},{8,9},{9,8},{10,11... | collective-permute-start | bytes 12296 | tf_op jit(solution)/shard_map/ppermute | solution.py:303

commit v4 on v3

--- a/solution.py
+++ b/solution.py
@@ -9,6 +9,7 @@
 
 F32 = jnp.float32
 BF16 = jnp.bfloat16
+HEAVY = 20_000_000_000
 SMEM = pl.BlockSpec(memory_space=pltpu.SMEM)
 VMEM = pl.BlockSpec(memory_space=pltpu.VMEM)
 HBM = pl.BlockSpec(memory_space=pltpu.HBM)
@@ -241,7 +242,7 @@
     sums[...] = jnp.concatenate([squares, curve, jnp.zeros((6, 128), F32)], axis=0)
 
 
-def small_call(kernel, args, outs, name):
+def small_call(kernel, args, outs, name, flops=0):
     args = [pltpu.with_memory_space_constraint(a, pltpu.VMEM) for a in args]
     return pl.pallas_call(
         kernel,
@@ -249,6 +250,7 @@
         out_specs=[VMEM] * len(outs),
         out_shape=[jax.ShapeDtypeStruct(o, F32) for o in outs],
         compiler_params=pltpu.CompilerParams(vmem_limit_bytes=4 * 1024 * 1024),
+        cost_estimate=pl.CostEstimate(flops=flops, bytes_accessed=0, transcendentals=0),
         name=name,
     )(*args)
 
@@ -259,6 +261,7 @@
         [*terms, *curves],
         [(terms[0].shape[0] // 2, terms[0].shape[1])] * 2 + [(8, 128)],
         "items_total",
+        HEAVY,
     )
 
 
@@ -360,12 +363,11 @@
             lax.psum_scatter(jnp.concatenate(items, axis=1), "users", scatter_dimension=1, tiled=True)
         ]
     grad_right, hess_right, sums = items_call(terms, [curve_a, curve_b])
-    g, sums = squares_call(g, other_g, sums, lax.axis_size("items") // 2)
+    for bit in across:
+        sums = sums + swap(sums, "items", bit)
+    g, sums = squares_call(g, other_g, sums, 1)
     h = add_call(h, other_h, sums)
-    for bit in across[:-1]:
-        sums = sums + swap(sums, "items", bit)
-    sums = (sums + swap(sums, "users", 1)) + (swap(sums, "items", across[-1]) + swap_both(sums, 1, across[-1]))
-    for bit in bits("users")[1:]:
+    for bit in bits("users"):
         sums = sums + swap(sums, "users", bit)
     far = swap(sums, "items", 1)
 

time: 45.7 us -> 43.4 us (0.950)
  waiting for transfers between devices: 11.7 us -> 9.81 us
    ppermute x1 -> x0, starting transfers between devices: 1.07 us -> none  [swap_both(): return lax.ppermute(x, ('users', 'items'), pairs)]
    ppermute x1 -> x0, waiting for transfers between devices: 1.02 us -> none  [swap_both(): return lax.ppermute(x, ('users', 'items'), pairs)]
    ppermute x15, waiting for transfers between devices: 10.7 us -> 9.81 us  [swap(): lax.ppermute(x, axis, [(i, i ^ bit) for i in range(lax.axis_size(axis))])]
    ppermute x15, starting transfers between devices: 16.6 us -> 17.3 us  [swap(): lax.ppermute(x, axis, [(i, i ^ bit) for i in range(lax.axis_size(axis))])]
  transfers between devices with their start and end apart: 16 -> 15, of which waited for: 7 -> 6; matrix products, arithmetic and copies ran while one was open for 3% -> 3% of each run, Pallas kernels for 14% -> 14%
where the time goes in v4:
time: 43.4 us; the launch traced here: 43.2 us
  starting transfers between devices  17.3 us (40%)
  Pallas kernels  13.1 us (30%)
  waiting for transfers between devices  9.81 us (23%)
  other arithmetic  2.13 us (5%)
  between operations  0.72 us (2%)
    ppermute x15, starting transfers between devices, swap(): lax.ppermute(x, axis, [(i, i ^ bit) for i in range(lax.axis_size(axis))])  17.3 us
    pallas_call x2, Pallas kernels, block_call(): pl.pallas_call(functools.partial(block_kernel, blocks, first, last, span,...  11.8 us
    ppermute x15, waiting for transfers between devices, swap(): lax.ppermute(x, axis, [(i, i ^ bit) for i in range(lax.axis_size(axis))])  9.81 us
    concatenate x1, other arithmetic, joined(): jnp.concatenate([jnp.where(core == 0, mine, other), jnp.where(core == 0,...  1.1 us
  transfers between devices with their start and end apart: 15, of which 6 were waited for; matrix products, arithmetic and copies ran while one was open for 3% of the time, Pallas kernels for 14%

profile of v4, /device:TPU:0, one launch (start us, length us, event | category | flops | bytes accessed | tf_op | source)
XLA Modules:
  0.0 43.2 jit_solution(872633414723523417)
XLA Ops:
  0.6 0.8 %pad_maximum_fusion.2.refs_2_ = f32[128,128]{1,0:T(8,128)S(1)} fusion(f32[64,128]{1,0:T(8,128)} %bitcast.18, f32[64,128]{1,0:T(8,128)} %bitcast.19), kind=kLoop, calls=%fused_computation.8 | loop fusion | flops 16384 | bytes 131072 | tf_op jit(solution)/shard_map/concatenate | solution.py:325
  1.4 5.0 %collective-permute-start.2 = (f32[128,128]{1,0:T(8,128)S(1)}, f32[128,128]{1,0:T(8,128)S(1)}, u32[]{:S(2)}, u32[]{:S(2)}) collective-permute-start(f32[128,128]{1,0:T(8,128)S(1)} %pad_maximum_fusion.2.refs_2_), channel_id=1, source_target_pairs={{0,12},{4,8},{8,4},{12,0},{1,13},{5,9},{9,5},{13,1},{2,14},{6,10},... | collective-permute-start | bytes 196616 | tf_op jit(solution)/shard_map/ppermute | solution.py:306
  6.5 0.6 %collective-permute-start = (f32[128,128]{1,0:T(8,128)S(1)}, f32[128,128]{1,0:T(8,128)S(1)}, u32[]{:S(2)}, u32[]{:S(2)}) collective-permute-start(f32[128,128]{1,0:T(8,128)S(1)} %pad_maximum_fusion.2.refs_2_), channel_id=1, source_target_pairs={{0,4},{4,0},{8,12},{12,8},{1,5},{5,1},{9,13},{13,9},{2,6},{6,2},{1... | collective-permute-start | bytes 196616 | tf_op jit(solution)/shard_map/ppermute | solution.py:306
  7.1 0.1 stack.31.where
  7.2 5.4 %own_block.1 = (bf16[2048,256]{1,0:T(8,128)(2,1)S(1)}, bf16[256,2048]{1,0:T(8,128)(2,1)S(1)}, f32[2048,512]{1,0:T(8,128)S(1)}, s32[2048,512]{1,0:T(8,128)S(1)}, ...) custom-call(s32[5]{0:T(128)S(1)} %stack.31.where, ...), custom_call_target="tpu_custom_call" | custom-call | flops 1811939328 | bytes 2097152 | tf_op jit(solution)/shard_map/own_block/pallas_call | solution.py:219
  12.6 0.1 pad_add_fusion.where
  12.7 0.0 collective-permute-done.2.refs_6_
  12.7 0.0 collective-permute-done.1.refs_5_
  12.7 6.4 %other_blocks.1 = (f32[64,2048]{1,0:T(8,128)S(1)}, f32[64,2048]{1,0:T(8,128)S(1)}, f32[1,128]{1,0:T(1,128)S(1)}, f32[128,128]{1,0:T(8,128)S(1)}, f32[128,128]{1,0:T(8,128)S(1)}, /*index=5*/f32[128,128]{1,0:T(8,128)S(1)}) custom-call(s32[4]{0:T(128)S(1)} %pad_add_fusion.where, s32[4,16]{1,0:T(4,128)} %bitcast.21, f32[2048,512]{1,0:T(8,128)S(1)} %get-tuple-element.24.ratings, ...), custom_call_target="tpu_custom_call" | custom-call | flops 5435817984 | bytes 6291456 | tf_op jit(solution)/shard_map/other_blocks/pallas_call | solution.py:219
  19.0 0.1 collective-permute-start.3
  19.1 3.8 %collective-permute-start.5 = (f32[128,128]{1,0:T(8,128)S(1)}, f32[128,128]{1,0:T(8,128)S(1)}, u32[]{:S(2)}, u32[]{:S(2)}) collective-permute-start(f32[128,128]{1,0:T(8,128)S(1)} %get-tuple-element.33), channel_id=1, source_target_pairs={{0,12},{4,8},{8,4},{12,0},{1,13},{5,9},{9,5},{13,1},{2,14},{6,10},... | collective-permute-start | bytes 196616 | tf_op jit(solution)/shard_map/ppermute | solution.py:306
  23.0 0.0 collective-permute-start.6
  23.0 0.6 %collective-permute-start.7 = (f32[128,128]{1,0:T(8,128)S(1)}, f32[128,128]{1,0:T(8,128)S(1)}, u32[]{:S(2)}, u32[]{:S(2)}) collective-permute-start(f32[128,128]{1,0:T(8,128)S(1)} %get-tuple-element.35), channel_id=1, source_target_pairs={{0,4},{4,0},{8,12},{12,8},{1,5},{5,1},{9,13},{13,9},{2,6},{6,2},{1... | collective-permute-start | bytes 196616 | tf_op jit(solution)/shard_map/ppermute | solution.py:306
  23.6 0.1 slice_add_fusion
  23.7 1.7 %collective-permute-start.4 = (f32[32,2048]{1,0:T(8,128)S(1)}, f32[32,2048]{1,0:T(8,128)S(1)}, u32[]{:S(2)}, u32[]{:S(2)}) collective-permute-start(f32[32,2048]{1,0:T(8,128)S(1)} %get-tuple-element.44.a), channel_id=1, source_target_pairs={{0,2},{1,3},{2,0},{3,1},{4,6},{5,7},{6,4},{7,5},{8,10},{9,11},{10,... | collective-permute-start | bytes 786440 | tf_op jit(solution)/shard_map/ppermute | solution.py:306
  25.3 0.7 %collective-permute-done.5.refs_1_ = f32[128,128]{1,0:T(8,128)S(1)} collective-permute-done((f32[128,128]{1,0:T(8,128)S(1)}, f32[128,128]{1,0:T(8,128)S(1)}, u32[]{:S(2)}, u32[]{:S(2)}) %collective-permute-start.5) | collective-permute-done | bytes 65568 | tf_op jit(solution)/shard_map/ppermute | solution.py:306
  26.1 2.6 %collective-permute-done.6.refs_2_ = f32[128,128]{1,0:T(8,128)S(1)} collective-permute-done((f32[128,128]{1,0:T(8,128)S(1)}, f32[128,128]{1,0:T(8,128)S(1)}, u32[]{:S(2)}, u32[]{:S(2)}) %collective-permute-start.6) | collective-permute-done | bytes 65568 | tf_op jit(solution)/shard_map/ppermute | solution.py:306
  28.7 0.6 %items_total.1 = (f32[64,128]{1,0:T(8,128)}, f32[64,128]{1,0:T(8,128)}, f32[8,128]{1,0:T(8,128)S(1)}) custom-call(f32[128,128]{1,0:T(8,128)S(1)} %get-tuple-element.32.refs_0_, f32[128,128]{1,0:T(8,128)S(1)} %collective-permute-done.5.refs_1_, f32[128,128]{1,0:T(8,128)S(1)} %collective-permute-done.6.refs_2_, f32[128,128]{1,0:T(8,128)S(1)} %collective-permute-done.7.refs_3_, ...), custom_call_target="tpu_custom_call" | custom-call | flops 20000000000 | tf_op jit(solution)/shard_map/items_total/pallas_call | solution.py:247
  29.3 1.5 %collective-permute-start.8 = (f32[8,128]{1,0:T(8,128)S(1)}, f32[8,128]{1,0:T(8,128)S(1)}, u32[]{:S(2)}, u32[]{:S(2)}) collective-permute-start(f32[8,128]{1,0:T(8,128)S(1)} %get-tuple-element.38), channel_id=1, source_target_pairs={{0,2},{1,3},{2,0},{3,1},{4,6},{5,7},{6,4},{7,5},{8,10},{9,11},{10,... | collective-permute-start | bytes 12296 | tf_op jit(solution)/shard_map/ppermute | solution.py:306
  30.9 0.5 %collective-permute-start.10 = (f32[32,2048]{1,0:T(8,128)S(1)}, f32[32,2048]{1,0:T(8,128)S(1)}, u32[]{:S(2)}, u32[]{:S(2)}) collective-permute-start(f32[32,2048]{1,0:T(8,128)S(1)} %get-tuple-element.43.a), channel_id=1, source_target_pairs={{0,2},{1,3},{2,0},{3,1},{4,6},{5,7},{6,4},{7,5},{8,10},{9,11},{10,... | collective-permute-start | bytes 786440 | tf_op jit(solution)/shard_map/ppermute | solution.py:306
  31.4 1.6 %collective-permute-done.8 = f32[8,128]{1,0:T(8,128)S(1)} collective-permute-done((f32[8,128]{1,0:T(8,128)S(1)}, f32[8,128]{1,0:T(8,128)S(1)}, u32[]{:S(2)}, u32[]{:S(2)}) %collective-permute-start.8) | collective-permute-done | bytes 4128 | tf_op jit(solution)/shard_map/ppermute | solution.py:306
  33.0 0.1 squares.1
  33.0 0.1 collective-permute-start.9
  33.1 1.7 %collective-permute-start.12 = (f32[8,128]{1,0:T(8,128)S(1)}, f32[8,128]{1,0:T(8,128)S(1)}, u32[]{:S(2)}, u32[]{:S(2)}) collective-permute-start(f32[8,128]{1,0:T(8,128)S(1)} %get-tuple-element.40.after), channel_id=1, source_target_pairs={{0,4},{4,0},{8,12},{12,8},{1,5},{5,1},{9,13},{13,9},{2,6},{6,2},{1... | collective-permute-start | bytes 12296 | tf_op jit(solution)/shard_map/ppermute | solution.py:306
  34.8 2.0 %collective-permute-done.12 = f32[8,128]{1,0:T(8,128)S(1)} collective-permute-done((f32[8,128]{1,0:T(8,128)S(1)}, f32[8,128]{1,0:T(8,128)S(1)}, u32[]{:S(2)}, u32[]{:S(2)}) %collective-permute-start.12) | collective-permute-done | bytes 4128 | tf_op jit(solution)/shard_map/ppermute | solution.py:306
  36.8 1.5 %collective-permute-start.13 = (f32[8,128]{1,0:T(8,128)S(1)}, f32[8,128]{1,0:T(8,128)S(1)}, u32[]{:S(2)}, u32[]{:S(2)}) collective-permute-start(f32[8,128]{1,0:T(8,128)S(1)} %add.24), channel_id=1, source_target_pairs={{0,8},{4,12},{8,0},{12,4},{1,9},{5,13},{9,1},{13,5},{2,10},{6,14},... | collective-permute-start | bytes 12296 | tf_op jit(solution)/shard_map/ppermute | solution.py:306
  38.3 0.4 collective-permute-done.10.b
  38.8 0.1 collective-permute-start.11
  38.9 2.4 %collective-permute-done.13 = f32[8,128]{1,0:T(8,128)S(1)} collective-permute-done((f32[8,128]{1,0:T(8,128)S(1)}, f32[8,128]{1,0:T(8,128)S(1)}, u32[]{:S(2)}, u32[]{:S(2)}) %collective-permute-start.13) | collective-permute-done | bytes 4128 | tf_op jit(solution)/shard_map/ppermute | solution.py:306
  41.3 0.1 broadcast_select_fusion.3
  41.4 1.1 %pad_maximum_fusion = (f32[64,2048]{1,0:T(8,128)S(1)}, f32[2048,64]{0,1:T(8,128)}, f32[2048,64]{0,1:T(8,128)}, f32[64,2048]{1,0:T(8,128)S(1)}) fusion(f32[32,2048]{1,0:T(8,128)S(1)} %get-tuple-element.52, f32[32,2048]{1,0:T(8,128)S(1)} %get-tuple-element.51, f32[32,2048]{1,0:T(8,128)S(1)} %get-tuple-element.50, f32[32,2048]{1,0:T(8,128)S(1)} %get-tuple-element.49), kind=kLoop, calls=%fused_computation | loop fusion | flops 262144 | bytes 3145728 | tf_op jit(solution)/shard_map/concatenate | solution.py:376
  42.5 0.6 %inner.1 = f32[2]{0:T(128)} custom-call(f32[8,128]{1,0:T(8,128)S(1)} %add.25.a, f32[8,128]{1,0:T(8,128)S(1)} %collective-permute-done.14.b, f32[64,2048]{1,0:T(8,128)S(1)} %get-tuple-element.47.g, f32[64,2048]{1,0:T(8,128)S(1)} %get-tuple-element.54.h), custom_call_target="tpu_custom_call" | custom-call | tf_op jit(solution)/shard_map/inner/pallas_call | solution.py:295
  (14 shorter events, 0.1 us)
Async XLA Ops:
  1.4 11.2 %collective-permute-start.2 = (f32[128,128]{1,0:T(8,128)S(1)}, f32[128,128]{1,0:T(8,128)S(1)}, u32[]{:S(2)}, u32[]{:S(2)}) collective-permute-start(f32[128,128]{1,0:T(8,128)S(1)} %pad_maximum_fusion.2.refs_2_), channel_id=1, source_target_pairs={{0,12},{4,8},{8,4},{12,0},{1,13},{5,9},{9,5},{13,1},{2,14},{6,10},... | collective-permute-start | bytes 196616 | tf_op jit(solution)/shard_map/ppermute | solution.py:306
  6.5 6.2 %collective-permute-start.1 = (f32[128,128]{1,0:T(8,128)S(1)}, f32[128,128]{1,0:T(8,128)S(1)}, u32[]{:S(2)}, u32[]{:S(2)}) collective-permute-start(f32[128,128]{1,0:T(8,128)S(1)} %pad_maximum_fusion.2.refs_2_), channel_id=1, source_target_pairs={{0,8},{4,12},{8,0},{12,4},{1,9},{5,13},{9,1},{13,5},{2,10},{6,14},... | collective-permute-start | bytes 196616 | tf_op jit(solution)/shard_map/ppermute | solution.py:306
  6.5 6.2 %collective-permute-start = (f32[128,128]{1,0:T(8,128)S(1)}, f32[128,128]{1,0:T(8,128)S(1)}, u32[]{:S(2)}, u32[]{:S(2)}) collective-permute-start(f32[128,128]{1,0:T(8,128)S(1)} %pad_maximum_fusion.2.refs_2_), channel_id=1, source_target_pairs={{0,4},{4,0},{8,12},{12,8},{1,5},{5,1},{9,13},{13,9},{2,6},{6,2},{1... | collective-permute-start | bytes 196616 | tf_op jit(solution)/shard_map/ppermute | solution.py:306
  19.0 4.6 %collective-permute-start.3 = (f32[64,2048]{1,0:T(8,128)S(1)}, f32[64,2048]{1,0:T(8,128)S(1)}, u32[]{:S(2)}, u32[]{:S(2)}) collective-permute-start(f32[64,2048]{1,0:T(8,128)S(1)} %get-tuple-element.31), channel_id=1, source_target_pairs={{0,1},{1,0},{2,3},{3,2},{4,5},{5,4},{6,7},{7,6},{8,9},{9,8},{10,11... | collective-permute-start | bytes 1572872 | tf_op jit(solution)/shard_map/ppermute | solution.py:306
  19.1 6.9 %collective-permute-start.5 = (f32[128,128]{1,0:T(8,128)S(1)}, f32[128,128]{1,0:T(8,128)S(1)}, u32[]{:S(2)}, u32[]{:S(2)}) collective-permute-start(f32[128,128]{1,0:T(8,128)S(1)} %get-tuple-element.33), channel_id=1, source_target_pairs={{0,12},{4,8},{8,4},{12,0},{1,13},{5,9},{9,5},{13,1},{2,14},{6,10},... | collective-permute-start | bytes 196616 | tf_op jit(solution)/shard_map/ppermute | solution.py:306
  23.0 5.7 %collective-permute-start.6 = (f32[128,128]{1,0:T(8,128)S(1)}, f32[128,128]{1,0:T(8,128)S(1)}, u32[]{:S(2)}, u32[]{:S(2)}) collective-permute-start(f32[128,128]{1,0:T(8,128)S(1)} %get-tuple-element.34), channel_id=1, source_target_pairs={{0,8},{4,12},{8,0},{12,4},{1,9},{5,13},{9,1},{13,5},{2,10},{6,14},... | collective-permute-start | bytes 196616 | tf_op jit(solution)/shard_map/ppermute | solution.py:306
  23.0 5.7 %collective-permute-start.7 = (f32[128,128]{1,0:T(8,128)S(1)}, f32[128,128]{1,0:T(8,128)S(1)}, u32[]{:S(2)}, u32[]{:S(2)}) collective-permute-start(f32[128,128]{1,0:T(8,128)S(1)} %get-tuple-element.35), channel_id=1, source_target_pairs={{0,4},{4,0},{8,12},{12,8},{1,5},{5,1},{9,13},{13,9},{2,6},{6,2},{1... | collective-permute-start | bytes 196616 | tf_op jit(solution)/shard_map/ppermute | solution.py:306
  23.7 9.3 %collective-permute-start.4 = (f32[32,2048]{1,0:T(8,128)S(1)}, f32[32,2048]{1,0:T(8,128)S(1)}, u32[]{:S(2)}, u32[]{:S(2)}) collective-permute-start(f32[32,2048]{1,0:T(8,128)S(1)} %get-tuple-element.44.a), channel_id=1, source_target_pairs={{0,2},{1,3},{2,0},{3,1},{4,6},{5,7},{6,4},{7,5},{8,10},{9,11},{10,... | collective-permute-start | bytes 786440 | tf_op jit(solution)/shard_map/ppermute | solution.py:306
  29.3 3.6 %collective-permute-start.8 = (f32[8,128]{1,0:T(8,128)S(1)}, f32[8,128]{1,0:T(8,128)S(1)}, u32[]{:S(2)}, u32[]{:S(2)}) collective-permute-start(f32[8,128]{1,0:T(8,128)S(1)} %get-tuple-element.38), channel_id=1, source_target_pairs={{0,2},{1,3},{2,0},{3,1},{4,6},{5,7},{6,4},{7,5},{8,10},{9,11},{10,... | collective-permute-start | bytes 12296 | tf_op jit(solution)/shard_map/ppermute | solution.py:306
  30.9 7.9 %collective-permute-start.10 = (f32[32,2048]{1,0:T(8,128)S(1)}, f32[32,2048]{1,0:T(8,128)S(1)}, u32[]{:S(2)}, u32[]{:S(2)}) collective-permute-start(f32[32,2048]{1,0:T(8,128)S(1)} %get-tuple-element.43.a), channel_id=1, source_target_pairs={{0,2},{1,3},{2,0},{3,1},{4,6},{5,7},{6,4},{7,5},{8,10},{9,11},{10,... | collective-permute-start | bytes 786440 | tf_op jit(solution)/shard_map/ppermute | solution.py:306
  33.0 8.3 %collective-permute-start.9 = (f32[32,2048]{1,0:T(8,128)S(1)}, f32[32,2048]{1,0:T(8,128)S(1)}, u32[]{:S(2)}, u32[]{:S(2)}) collective-permute-start(f32[32,2048]{1,0:T(8,128)S(1)} %get-tuple-element.39), channel_id=1, source_target_pairs={{0,1},{1,0},{2,3},{3,2},{4,5},{5,4},{6,7},{7,6},{8,9},{9,8},{10,11... | collective-permute-start | bytes 786440 | tf_op jit(solution)/shard_map/ppermute | solution.py:306
  33.1 3.7 %collective-permute-start.12 = (f32[8,128]{1,0:T(8,128)S(1)}, f32[8,128]{1,0:T(8,128)S(1)}, u32[]{:S(2)}, u32[]{:S(2)}) collective-permute-start(f32[8,128]{1,0:T(8,128)S(1)} %get-tuple-element.40.after), channel_id=1, source_target_pairs={{0,4},{4,0},{8,12},{12,8},{1,5},{5,1},{9,13},{13,9},{2,6},{6,2},{1... | collective-permute-start | bytes 12296 | tf_op jit(solution)/shard_map/ppermute | solution.py:306
  36.8 4.5 %collective-permute-start.13 = (f32[8,128]{1,0:T(8,128)S(1)}, f32[8,128]{1,0:T(8,128)S(1)}, u32[]{:S(2)}, u32[]{:S(2)}) collective-permute-start(f32[8,128]{1,0:T(8,128)S(1)} %add.24), channel_id=1, source_target_pairs={{0,8},{4,12},{8,0},{12,4},{1,9},{5,13},{9,1},{13,5},{2,10},{6,14},... | collective-permute-start | bytes 12296 | tf_op jit(solution)/shard_map/ppermute | solution.py:306
  38.8 2.6 %collective-permute-start.11 = (f32[32,2048]{1,0:T(8,128)S(1)}, f32[32,2048]{1,0:T(8,128)S(1)}, u32[]{:S(2)}, u32[]{:S(2)}) collective-permute-start(f32[32,2048]{1,0:T(8,128)S(1)} %add.34), channel_id=1, source_target_pairs={{0,1},{1,0},{2,3},{3,2},{4,5},{5,4},{6,7},{7,6},{8,9},{9,8},{10,11... | collective-permute-start | bytes 786440 | tf_op jit(solution)/shard_map/ppermute | solution.py:306
  41.3 1.2 %collective-permute-start.14 = (f32[8,128]{1,0:T(8,128)S(1)}, f32[8,128]{1,0:T(8,128)S(1)}, u32[]{:S(2)}, u32[]{:S(2)}) collective-permute-start(f32[8,128]{1,0:T(8,128)S(1)} %add.25.a), channel_id=1, source_target_pairs={{0,1},{1,0},{2,3},{3,2},{4,5},{5,4},{6,7},{7,6},{8,9},{9,8},{10,11... | collective-permute-start | bytes 12296 | tf_op jit(solution)/shard_map/ppermute | solution.py:306

commit v5 on v4

--- a/solution.py
+++ b/solution.py
@@ -140,6 +140,7 @@
             total = None
         else:
             total = acc[here, :]
+        highs, lows = [], []
         for k in range(blocks):
             if first:
                 rating, seen = own_ratings[here, :], own_mask[here, :]
@@ -162,10 +163,14 @@
             out = dot(rc_high, back[k])
             out = out[:, : 2 * rank] + out[:, 2 * rank :] + dot(rc_low, back[k, :, : 2 * rank])
             total = out if total is None else total + out
-            got = dot(factors[:, here], rc_high)
-            got = got[: 2 * rank] + got[2 * rank :] + dot(factors[: 2 * rank, here], rc_low)
-            items[k][:rank] += got[:rank, :wide]
-            items[k][rank:] += got[:rank, wide:] + got[rank:, :wide]
+            highs.append(rc_high)
+            lows.append(rc_low)
+        f = factors[:, here]
+        got = dot(f, jnp.concatenate(highs, axis=1))
+        got = got[: 2 * rank] + got[2 * rank :] + dot(f[: 2 * rank], jnp.concatenate(lows, axis=1))
+        for k in range(blocks):
+            items[k][:rank] += got[:rank, 2 * k * wide : (2 * k + 1) * wide]
+            items[k][rank:] += got[:rank, (2 * k + 1) * wide : (2 * k + 2) * wide] + got[rank:, 2 * k * wide : (2 * k + 1) * wide]
         if last:
             user = total.T
             there = pl.ds(step - start, rows)
@@ -343,7 +348,7 @@
     others = list(range(1, len(panels)))
     keep, send, curve_b, *rest = block_call(
         where(others), table, ratings, entry_mask, [factors_t, factors, acc, left_dir_t], panels[1:],
-        last=True, rows=1024, name="other_blocks",
+        last=True, rows=2048, name="other_blocks",
     )
     items = [item, *rest]
     got = swap(send, "items", 1)

time: 43.4 us -> 43 us (level)
  Pallas kernels: 13.1 us -> 12.6 us
    pallas_call x2, Pallas kernels: 11.8 us -> 11.2 us  [block_call(): pl.pallas_call(functools.partial(block_kernel, blocks, first, last, span,...]
  transfers between devices with their start and end apart: 15 -> 15, of which waited for: 6 -> 6; matrix products, arithmetic and copies ran while one was open for 3% -> 3% of each run, Pallas kernels for 14% -> 15%
where the time goes in v5:
time: 43 us; the launch traced here: 42.7 us
  starting transfers between devices  17.3 us (40%)
  Pallas kernels  12.6 us (29%)
  waiting for transfers between devices  9.79 us (23%)
  other arithmetic  2.13 us (5%)
  between operations  0.72 us (2%)
    ppermute x15, starting transfers between devices, swap(): lax.ppermute(x, axis, [(i, i ^ bit) for i in range(lax.axis_size(axis))])  17.3 us
    pallas_call x2, Pallas kernels, block_call(): pl.pallas_call(functools.partial(block_kernel, blocks, first, last, span,...  11.2 us
    ppermute x15, waiting for transfers between devices, swap(): lax.ppermute(x, axis, [(i, i ^ bit) for i in range(lax.axis_size(axis))])  9.79 us
    concatenate x1, other arithmetic, joined(): jnp.concatenate([jnp.where(core == 0, mine, other), jnp.where(core == 0,...  1.1 us
  transfers between devices with their start and end apart: 15, of which 6 were waited for; matrix products, arithmetic and copies ran while one was open for 3% of the time, Pallas kernels for 15%

profile of v5, /device:TPU:0, one launch (start us, length us, event | category | flops | bytes accessed | tf_op | source)
XLA Modules:
  0.0 42.7 jit_solution(14621921919936764785)
XLA Ops:
  0.6 0.8 %pad_maximum_fusion.2.refs_2_ = f32[128,128]{1,0:T(8,128)S(1)} fusion(f32[64,128]{1,0:T(8,128)} %bitcast.18, f32[64,128]{1,0:T(8,128)} %bitcast.19), kind=kLoop, calls=%fused_computation.8 | loop fusion | flops 16384 | bytes 131072 | tf_op jit(solution)/shard_map/concatenate | solution.py:330
  1.4 5.0 %collective-permute-start.2 = (f32[128,128]{1,0:T(8,128)S(1)}, f32[128,128]{1,0:T(8,128)S(1)}, u32[]{:S(2)}, u32[]{:S(2)}) collective-permute-start(f32[128,128]{1,0:T(8,128)S(1)} %pad_maximum_fusion.2.refs_2_), channel_id=1, source_target_pairs={{0,12},{4,8},{8,4},{12,0},{1,13},{5,9},{9,5},{13,1},{2,14},{6,10},... | collective-permute-start | bytes 196616 | tf_op jit(solution)/shard_map/ppermute | solution.py:311
  6.5 0.0 collective-permute-start.1
  6.5 0.6 %collective-permute-start = (f32[128,128]{1,0:T(8,128)S(1)}, f32[128,128]{1,0:T(8,128)S(1)}, u32[]{:S(2)}, u32[]{:S(2)}) collective-permute-start(f32[128,128]{1,0:T(8,128)S(1)} %pad_maximum_fusion.2.refs_2_), channel_id=1, source_target_pairs={{0,4},{4,0},{8,12},{12,8},{1,5},{5,1},{9,13},{13,9},{2,6},{6,2},{1... | collective-permute-start | bytes 196616 | tf_op jit(solution)/shard_map/ppermute | solution.py:311
  7.1 0.1 stack.31.where
  7.2 5.6 %own_block.1 = (bf16[2048,256]{1,0:T(8,128)(2,1)S(1)}, bf16[256,2048]{1,0:T(8,128)(2,1)S(1)}, f32[2048,512]{1,0:T(8,128)S(1)}, s32[2048,512]{1,0:T(8,128)S(1)}, ...) custom-call(s32[5]{0:T(128)S(1)} %stack.31.where, ...), custom_call_target="tpu_custom_call" | custom-call | flops 1811939328 | bytes 2097152 | tf_op jit(solution)/shard_map/own_block/pallas_call | solution.py:224
  12.8 0.1 pad_add_fusion.where
  12.9 0.0 collective-permute-done.2.refs_6_
  12.9 0.0 collective-permute-done.1.refs_5_
  12.9 5.6 %other_blocks.1 = (f32[64,2048]{1,0:T(8,128)S(1)}, f32[64,2048]{1,0:T(8,128)S(1)}, f32[1,128]{1,0:T(1,128)S(1)}, f32[128,128]{1,0:T(8,128)S(1)}, f32[128,128]{1,0:T(8,128)S(1)}, /*index=5*/f32[128,128]{1,0:T(8,128)S(1)}) custom-call(s32[4]{0:T(128)S(1)} %pad_add_fusion.where, s32[4,16]{1,0:T(4,128)} %bitcast.21, f32[2048,512]{1,0:T(8,128)S(1)} %get-tuple-element.24.ratings, ...), custom_call_target="tpu_custom_call" | custom-call | flops 5435817984 | bytes 6291456 | tf_op jit(solution)/shard_map/other_blocks/pallas_call | solution.py:224
  18.5 0.1 collective-permute-start.3
  18.6 3.9 %collective-permute-start.5 = (f32[128,128]{1,0:T(8,128)S(1)}, f32[128,128]{1,0:T(8,128)S(1)}, u32[]{:S(2)}, u32[]{:S(2)}) collective-permute-start(f32[128,128]{1,0:T(8,128)S(1)} %get-tuple-element.33), channel_id=1, source_target_pairs={{0,12},{4,8},{8,4},{12,0},{1,13},{5,9},{9,5},{13,1},{2,14},{6,10},... | collective-permute-start | bytes 196616 | tf_op jit(solution)/shard_map/ppermute | solution.py:311
  22.5 0.6 %collective-permute-start.7 = (f32[128,128]{1,0:T(8,128)S(1)}, f32[128,128]{1,0:T(8,128)S(1)}, u32[]{:S(2)}, u32[]{:S(2)}) collective-permute-start(f32[128,128]{1,0:T(8,128)S(1)} %get-tuple-element.35), channel_id=1, source_target_pairs={{0,4},{4,0},{8,12},{12,8},{1,5},{5,1},{9,13},{13,9},{2,6},{6,2},{1... | collective-permute-start | bytes 196616 | tf_op jit(solution)/shard_map/ppermute | solution.py:311
  23.1 0.1 slice_add_fusion
  23.2 1.6 %collective-permute-start.4 = (f32[32,2048]{1,0:T(8,128)S(1)}, f32[32,2048]{1,0:T(8,128)S(1)}, u32[]{:S(2)}, u32[]{:S(2)}) collective-permute-start(f32[32,2048]{1,0:T(8,128)S(1)} %get-tuple-element.44.a), channel_id=1, source_target_pairs={{0,2},{1,3},{2,0},{3,1},{4,6},{5,7},{6,4},{7,5},{8,10},{9,11},{10,... | collective-permute-start | bytes 786440 | tf_op jit(solution)/shard_map/ppermute | solution.py:311
  24.8 0.7 %collective-permute-done.5.refs_1_ = f32[128,128]{1,0:T(8,128)S(1)} collective-permute-done((f32[128,128]{1,0:T(8,128)S(1)}, f32[128,128]{1,0:T(8,128)S(1)}, u32[]{:S(2)}, u32[]{:S(2)}) %collective-permute-start.5) | collective-permute-done | bytes 65568 | tf_op jit(solution)/shard_map/ppermute | solution.py:311
  25.5 2.7 %collective-permute-done.6.refs_2_ = f32[128,128]{1,0:T(8,128)S(1)} collective-permute-done((f32[128,128]{1,0:T(8,128)S(1)}, f32[128,128]{1,0:T(8,128)S(1)}, u32[]{:S(2)}, u32[]{:S(2)}) %collective-permute-start.6) | collective-permute-done | bytes 65568 | tf_op jit(solution)/shard_map/ppermute | solution.py:311
  28.2 0.6 %items_total.1 = (f32[64,128]{1,0:T(8,128)}, f32[64,128]{1,0:T(8,128)}, f32[8,128]{1,0:T(8,128)S(1)}) custom-call(f32[128,128]{1,0:T(8,128)S(1)} %get-tuple-element.32.refs_0_, f32[128,128]{1,0:T(8,128)S(1)} %collective-permute-done.5.refs_1_, f32[128,128]{1,0:T(8,128)S(1)} %collective-permute-done.6.refs_2_, f32[128,128]{1,0:T(8,128)S(1)} %collective-permute-done.7.refs_3_, ...), custom_call_target="tpu_custom_call" | custom-call | flops 20000000000 | tf_op jit(solution)/shard_map/items_total/pallas_call | solution.py:252
  28.9 1.5 %collective-permute-start.8 = (f32[8,128]{1,0:T(8,128)S(1)}, f32[8,128]{1,0:T(8,128)S(1)}, u32[]{:S(2)}, u32[]{:S(2)}) collective-permute-start(f32[8,128]{1,0:T(8,128)S(1)} %get-tuple-element.38), channel_id=1, source_target_pairs={{0,2},{1,3},{2,0},{3,1},{4,6},{5,7},{6,4},{7,5},{8,10},{9,11},{10,... | collective-permute-start | bytes 12296 | tf_op jit(solution)/shard_map/ppermute | solution.py:311
  30.4 0.5 %collective-permute-start.10 = (f32[32,2048]{1,0:T(8,128)S(1)}, f32[32,2048]{1,0:T(8,128)S(1)}, u32[]{:S(2)}, u32[]{:S(2)}) collective-permute-start(f32[32,2048]{1,0:T(8,128)S(1)} %get-tuple-element.43.a), channel_id=1, source_target_pairs={{0,2},{1,3},{2,0},{3,1},{4,6},{5,7},{6,4},{7,5},{8,10},{9,11},{10,... | collective-permute-start | bytes 786440 | tf_op jit(solution)/shard_map/ppermute | solution.py:311
  30.9 1.6 %collective-permute-done.8 = f32[8,128]{1,0:T(8,128)S(1)} collective-permute-done((f32[8,128]{1,0:T(8,128)S(1)}, f32[8,128]{1,0:T(8,128)S(1)}, u32[]{:S(2)}, u32[]{:S(2)}) %collective-permute-start.8) | collective-permute-done | bytes 4128 | tf_op jit(solution)/shard_map/ppermute | solution.py:311
  32.5 0.1 squares.1
  32.5 0.1 collective-permute-start.9
  32.6 1.7 %collective-permute-start.12 = (f32[8,128]{1,0:T(8,128)S(1)}, f32[8,128]{1,0:T(8,128)S(1)}, u32[]{:S(2)}, u32[]{:S(2)}) collective-permute-start(f32[8,128]{1,0:T(8,128)S(1)} %get-tuple-element.40.after), channel_id=1, source_target_pairs={{0,4},{4,0},{8,12},{12,8},{1,5},{5,1},{9,13},{13,9},{2,6},{6,2},{1... | collective-permute-start | bytes 12296 | tf_op jit(solution)/shard_map/ppermute | solution.py:311
  34.3 2.0 %collective-permute-done.12 = f32[8,128]{1,0:T(8,128)S(1)} collective-permute-done((f32[8,128]{1,0:T(8,128)S(1)}, f32[8,128]{1,0:T(8,128)S(1)}, u32[]{:S(2)}, u32[]{:S(2)}) %collective-permute-start.12) | collective-permute-done | bytes 4128 | tf_op jit(solution)/shard_map/ppermute | solution.py:311
  36.3 1.6 %collective-permute-start.13 = (f32[8,128]{1,0:T(8,128)S(1)}, f32[8,128]{1,0:T(8,128)S(1)}, u32[]{:S(2)}, u32[]{:S(2)}) collective-permute-start(f32[8,128]{1,0:T(8,128)S(1)} %add.24), channel_id=1, source_target_pairs={{0,8},{4,12},{8,0},{12,4},{1,9},{5,13},{9,1},{13,5},{2,10},{6,14},... | collective-permute-start | bytes 12296 | tf_op jit(solution)/shard_map/ppermute | solution.py:311
  37.9 0.3 collective-permute-done.10.b
  38.2 0.1 collective-permute-start.11
  38.3 2.5 %collective-permute-done.13 = f32[8,128]{1,0:T(8,128)S(1)} collective-permute-done((f32[8,128]{1,0:T(8,128)S(1)}, f32[8,128]{1,0:T(8,128)S(1)}, u32[]{:S(2)}, u32[]{:S(2)}) %collective-permute-start.13) | collective-permute-done | bytes 4128 | tf_op jit(solution)/shard_map/ppermute | solution.py:311
  40.8 0.1 broadcast_select_fusion.3
  40.9 1.1 %pad_maximum_fusion = (f32[64,2048]{1,0:T(8,128)S(1)}, f32[2048,64]{0,1:T(8,128)}, f32[2048,64]{0,1:T(8,128)}, f32[64,2048]{1,0:T(8,128)S(1)}) fusion(f32[32,2048]{1,0:T(8,128)S(1)} %get-tuple-element.52, f32[32,2048]{1,0:T(8,128)S(1)} %get-tuple-element.51, f32[32,2048]{1,0:T(8,128)S(1)} %get-tuple-element.50, f32[32,2048]{1,0:T(8,128)S(1)} %get-tuple-element.49), kind=kLoop, calls=%fused_computation | loop fusion | flops 262144 | bytes 3145728 | tf_op jit(solution)/shard_map/concatenate | solution.py:381
  42.0 0.6 %inner.1 = f32[2]{0:T(128)} custom-call(f32[8,128]{1,0:T(8,128)S(1)} %add.25.a, f32[8,128]{1,0:T(8,128)S(1)} %collective-permute-done.14.b, f32[64,2048]{1,0:T(8,128)S(1)} %get-tuple-element.47.g, f32[64,2048]{1,0:T(8,128)S(1)} %get-tuple-element.54.h), custom_call_target="tpu_custom_call" | custom-call | tf_op jit(solution)/shard_map/inner/pallas_call | solution.py:300
  (14 shorter events, 0.1 us)
Async XLA Ops:
  1.4 11.5 %collective-permute-start.2 = (f32[128,128]{1,0:T(8,128)S(1)}, f32[128,128]{1,0:T(8,128)S(1)}, u32[]{:S(2)}, u32[]{:S(2)}) collective-permute-start(f32[128,128]{1,0:T(8,128)S(1)} %pad_maximum_fusion.2.refs_2_), channel_id=1, source_target_pairs={{0,12},{4,8},{8,4},{12,0},{1,13},{5,9},{9,5},{13,1},{2,14},{6,10},... | collective-permute-start | bytes 196616 | tf_op jit(solution)/shard_map/ppermute | solution.py:311
  6.5 6.4 %collective-permute-start.1 = (f32[128,128]{1,0:T(8,128)S(1)}, f32[128,128]{1,0:T(8,128)S(1)}, u32[]{:S(2)}, u32[]{:S(2)}) collective-permute-start(f32[128,128]{1,0:T(8,128)S(1)} %pad_maximum_fusion.2.refs_2_), channel_id=1, source_target_pairs={{0,8},{4,12},{8,0},{12,4},{1,9},{5,13},{9,1},{13,5},{2,10},{6,14},... | collective-permute-start | bytes 196616 | tf_op jit(solution)/shard_map/ppermute | solution.py:311
  6.5 6.4 %collective-permute-start = (f32[128,128]{1,0:T(8,128)S(1)}, f32[128,128]{1,0:T(8,128)S(1)}, u32[]{:S(2)}, u32[]{:S(2)}) collective-permute-start(f32[128,128]{1,0:T(8,128)S(1)} %pad_maximum_fusion.2.refs_2_), channel_id=1, source_target_pairs={{0,4},{4,0},{8,12},{12,8},{1,5},{5,1},{9,13},{13,9},{2,6},{6,2},{1... | collective-permute-start | bytes 196616 | tf_op jit(solution)/shard_map/ppermute | solution.py:311
  18.5 4.6 %collective-permute-start.3 = (f32[64,2048]{1,0:T(8,128)S(1)}, f32[64,2048]{1,0:T(8,128)S(1)}, u32[]{:S(2)}, u32[]{:S(2)}) collective-permute-start(f32[64,2048]{1,0:T(8,128)S(1)} %get-tuple-element.31), channel_id=1, source_target_pairs={{0,1},{1,0},{2,3},{3,2},{4,5},{5,4},{6,7},{7,6},{8,9},{9,8},{10,11... | collective-permute-start | bytes 1572872 | tf_op jit(solution)/shard_map/ppermute | solution.py:311
  18.6 6.9 %collective-permute-start.5 = (f32[128,128]{1,0:T(8,128)S(1)}, f32[128,128]{1,0:T(8,128)S(1)}, u32[]{:S(2)}, u32[]{:S(2)}) collective-permute-start(f32[128,128]{1,0:T(8,128)S(1)} %get-tuple-element.33), channel_id=1, source_target_pairs={{0,12},{4,8},{8,4},{12,0},{1,13},{5,9},{9,5},{13,1},{2,14},{6,10},... | collective-permute-start | bytes 196616 | tf_op jit(solution)/shard_map/ppermute | solution.py:311
  22.5 5.7 %collective-permute-start.6 = (f32[128,128]{1,0:T(8,128)S(1)}, f32[128,128]{1,0:T(8,128)S(1)}, u32[]{:S(2)}, u32[]{:S(2)}) collective-permute-start(f32[128,128]{1,0:T(8,128)S(1)} %get-tuple-element.34), channel_id=1, source_target_pairs={{0,8},{4,12},{8,0},{12,4},{1,9},{5,13},{9,1},{13,5},{2,10},{6,14},... | collective-permute-start | bytes 196616 | tf_op jit(solution)/shard_map/ppermute | solution.py:311
  22.5 5.7 %collective-permute-start.7 = (f32[128,128]{1,0:T(8,128)S(1)}, f32[128,128]{1,0:T(8,128)S(1)}, u32[]{:S(2)}, u32[]{:S(2)}) collective-permute-start(f32[128,128]{1,0:T(8,128)S(1)} %get-tuple-element.35), channel_id=1, source_target_pairs={{0,4},{4,0},{8,12},{12,8},{1,5},{5,1},{9,13},{13,9},{2,6},{6,2},{1... | collective-permute-start | bytes 196616 | tf_op jit(solution)/shard_map/ppermute | solution.py:311
  23.2 9.3 %collective-permute-start.4 = (f32[32,2048]{1,0:T(8,128)S(1)}, f32[32,2048]{1,0:T(8,128)S(1)}, u32[]{:S(2)}, u32[]{:S(2)}) collective-permute-start(f32[32,2048]{1,0:T(8,128)S(1)} %get-tuple-element.44.a), channel_id=1, source_target_pairs={{0,2},{1,3},{2,0},{3,1},{4,6},{5,7},{6,4},{7,5},{8,10},{9,11},{10,... | collective-permute-start | bytes 786440 | tf_op jit(solution)/shard_map/ppermute | solution.py:311
  28.9 3.6 %collective-permute-start.8 = (f32[8,128]{1,0:T(8,128)S(1)}, f32[8,128]{1,0:T(8,128)S(1)}, u32[]{:S(2)}, u32[]{:S(2)}) collective-permute-start(f32[8,128]{1,0:T(8,128)S(1)} %get-tuple-element.38), channel_id=1, source_target_pairs={{0,2},{1,3},{2,0},{3,1},{4,6},{5,7},{6,4},{7,5},{8,10},{9,11},{10,... | collective-permute-start | bytes 12296 | tf_op jit(solution)/shard_map/ppermute | solution.py:311
  30.4 7.8 %collective-permute-start.10 = (f32[32,2048]{1,0:T(8,128)S(1)}, f32[32,2048]{1,0:T(8,128)S(1)}, u32[]{:S(2)}, u32[]{:S(2)}) collective-permute-start(f32[32,2048]{1,0:T(8,128)S(1)} %get-tuple-element.43.a), channel_id=1, source_target_pairs={{0,2},{1,3},{2,0},{3,1},{4,6},{5,7},{6,4},{7,5},{8,10},{9,11},{10,... | collective-permute-start | bytes 786440 | tf_op jit(solution)/shard_map/ppermute | solution.py:311
  32.5 8.3 %collective-permute-start.9 = (f32[32,2048]{1,0:T(8,128)S(1)}, f32[32,2048]{1,0:T(8,128)S(1)}, u32[]{:S(2)}, u32[]{:S(2)}) collective-permute-start(f32[32,2048]{1,0:T(8,128)S(1)} %get-tuple-element.39), channel_id=1, source_target_pairs={{0,1},{1,0},{2,3},{3,2},{4,5},{5,4},{6,7},{7,6},{8,9},{9,8},{10,11... | collective-permute-start | bytes 786440 | tf_op jit(solution)/shard_map/ppermute | solution.py:311
  32.6 3.7 %collective-permute-start.12 = (f32[8,128]{1,0:T(8,128)S(1)}, f32[8,128]{1,0:T(8,128)S(1)}, u32[]{:S(2)}, u32[]{:S(2)}) collective-permute-start(f32[8,128]{1,0:T(8,128)S(1)} %get-tuple-element.40.after), channel_id=1, source_target_pairs={{0,4},{4,0},{8,12},{12,8},{1,5},{5,1},{9,13},{13,9},{2,6},{6,2},{1... | collective-permute-start | bytes 12296 | tf_op jit(solution)/shard_map/ppermute | solution.py:311
  36.3 4.5 %collective-permute-start.13 = (f32[8,128]{1,0:T(8,128)S(1)}, f32[8,128]{1,0:T(8,128)S(1)}, u32[]{:S(2)}, u32[]{:S(2)}) collective-permute-start(f32[8,128]{1,0:T(8,128)S(1)} %add.24), channel_id=1, source_target_pairs={{0,8},{4,12},{8,0},{12,4},{1,9},{5,13},{9,1},{13,5},{2,10},{6,14},... | collective-permute-start | bytes 12296 | tf_op jit(solution)/shard_map/ppermute | solution.py:311
  38.2 2.7 %collective-permute-start.11 = (f32[32,2048]{1,0:T(8,128)S(1)}, f32[32,2048]{1,0:T(8,128)S(1)}, u32[]{:S(2)}, u32[]{:S(2)}) collective-permute-start(f32[32,2048]{1,0:T(8,128)S(1)} %add.34), channel_id=1, source_target_pairs={{0,1},{1,0},{2,3},{3,2},{4,5},{5,4},{6,7},{7,6},{8,9},{9,8},{10,11... | collective-permute-start | bytes 786440 | tf_op jit(solution)/shard_map/ppermute | solution.py:311
  40.8 1.2 %collective-permute-start.14 = (f32[8,128]{1,0:T(8,128)S(1)}, f32[8,128]{1,0:T(8,128)S(1)}, u32[]{:S(2)}, u32[]{:S(2)}) collective-permute-start(f32[8,128]{1,0:T(8,128)S(1)} %add.25.a), channel_id=1, source_target_pairs={{0,1},{1,0},{2,3},{3,2},{4,5},{5,4},{6,7},{7,6},{8,9},{9,8},{10,11... | collective-permute-start | bytes 12296 | tf_op jit(solution)/shard_map/ppermute | solution.py:311

commit v6 on v5

--- a/solution.py
+++ b/solution.py
@@ -88,7 +88,7 @@
             where, range(1, ratings.shape[1] // 128), pl.ds(0, mask.shape[0]),
             (ratings, mask), (all_ratings, all_mask), other_sems,
         )
-        for copy in itertools.chain(*loads):
+        for copy in itertools.chain(*loads, late):
             copy.start()
     rank2, wide = panels[0].shape
     rank = rank2 // 2
@@ -127,9 +127,6 @@
         if first:
             for copy in loads[step // rows]:
                 copy.wait()
-            if step == start:
-                for copy in late:
-                    copy.start()
             both = jnp.concatenate([left[:, here], left_dir[:, here]], axis=0)
             high, low = halves(both)
             factors[: 2 * rank, here] = high
@@ -233,18 +230,28 @@
     )(where, pltpu.with_memory_space_constraint(pattern, pltpu.HBM), *args)
 
 
-def items_kernel(count, curves, *refs):
-    terms, curve, (grad, hess, sums) = refs[:count], refs[count : count + curves], refs[count + curves :]
-    total = functools.reduce(jnp.add, [t[...] for t in terms])
-    rank = total.shape[0] // 2
-    grad[...] = total[:rank]
-    hess[...] = total[rank:]
-    squares = jnp.sum(total[:rank] * total[:rank], axis=0, keepdims=True)
+def items_kernel(count, *refs):
+    terms, curves, (total, sums) = refs[:count], refs[count:-2], refs[-2:]
+    x = functools.reduce(jnp.add, [t[...] for t in terms])
+    total[...] = x
+    grad = x[: x.shape[0] // 2]
+    squares = jnp.sum(grad * grad, axis=0, keepdims=True)
     wide = squares.shape[1]
     if wide < 128:
         squares = jnp.concatenate([squares, jnp.zeros((1, 128 - wide), F32)], axis=1)
-    curve = functools.reduce(jnp.add, [c[...] for c in curve])
+    curve = functools.reduce(jnp.add, [c[...] for c in curves])
     sums[...] = jnp.concatenate([squares, curve, jnp.zeros((6, 128), F32)], axis=0)
+
+
+def parts_kernel(total, after, grad, hess):
+    rank = grad.shape[0]
+    grad[...] = total[:rank]
+    hess[...] = total[rank:]
+
+
+def parts_call(total, after):
+    shape = (total.shape[0] // 2, total.shape[1])
+    return small_call(parts_kernel, [total, after], [shape, shape], "parts")
 
 
 def small_call(kernel, args, outs, name, flops=0):
@@ -262,9 +269,9 @@
 
 def items_call(terms, curves):
     return small_call(
-        functools.partial(items_kernel, len(terms), len(curves)),
+        functools.partial(items_kernel, len(terms)),
         [*terms, *curves],
-        [(terms[0].shape[0] // 2, terms[0].shape[1])] * 2 + [(8, 128)],
+        [terms[0].shape, (8, 128)],
         "items_total",
         HEAVY,
     )
@@ -343,7 +350,7 @@
     table = pattern.T
     factors_t, factors, ratings, entry_mask, left_dir_t, acc, curve_a, item = block_call(
         where(range(len(panels))), table, ratings, entry_mask, [left.T, left_dir.T], panels[:1],
-        first=True, rows=1024, name="own_block",
+        first=True, rows=512, name="own_block",
     )
     others = list(range(1, len(panels)))
     keep, send, curve_b, *rest = block_call(
@@ -362,16 +369,17 @@
     other_g = swap(g, "items", across[-1])
     other_h = swap(h, "items", across[-1])
     if direct:
-        terms = [items[0]] + [swap(items[k], "users", k) for k in range(n - 1, 0, -1)]
+        terms = [items[0]] + [swap(items[k], "users", k) for k in [2,3,1]]
     else:
         terms = [
             lax.psum_scatter(jnp.concatenate(items, axis=1), "users", scatter_dimension=1, tiled=True)
         ]
-    grad_right, hess_right, sums = items_call(terms, [curve_a, curve_b])
+    total, sums = items_call(terms, [curve_a, curve_b])
     for bit in across:
         sums = sums + swap(sums, "items", bit)
     g, sums = squares_call(g, other_g, sums, 1)
     h = add_call(h, other_h, sums)
+    grad_right, hess_right = parts_call(total, sums)
     for bit in bits("users"):
         sums = sums + swap(sums, "users", bit)
     far = swap(sums, "items", 1)

time: 43 us -> 42 us (0.977)
  waiting for transfers between devices: 9.79 us -> 9.12 us
    ppermute x15, waiting for transfers between devices: 9.79 us -> 9.12 us  [swap(): lax.ppermute(x, axis, [(i, i ^ bit) for i in range(lax.axis_size(axis))])]
  transfers between devices with their start and end apart: 15 -> 15, of which waited for: 6 -> 7; matrix products, arithmetic and copies ran while one was open for 3% -> 3% of each run, Pallas kernels for 15% -> 14%
where the time goes in v6:
time: 42 us; the launch traced here: 41.8 us
  starting transfers between devices  17.5 us (42%)
  Pallas kernels  12.2 us (29%)
  waiting for transfers between devices  9.12 us (22%)
  other arithmetic  2.12 us (5%)
  between operations  0.71 us (2%)
    ppermute x15, starting transfers between devices, swap(): lax.ppermute(x, axis, [(i, i ^ bit) for i in range(lax.axis_size(axis))])  17.5 us
    pallas_call x2, Pallas kernels, block_call(): pl.pallas_call(functools.partial(block_kernel, blocks, first, last, span,...  10.8 us
    ppermute x15, waiting for transfers between devices, swap(): lax.ppermute(x, axis, [(i, i ^ bit) for i in range(lax.axis_size(axis))])  9.12 us
    concatenate x1, other arithmetic, joined(): jnp.concatenate([jnp.where(core == 0, mine, other), jnp.where(core == 0,...  1.1 us
  transfers between devices with their start and end apart: 15, of which 7 were waited for; matrix products, arithmetic and copies ran while one was open for 3% of the time, Pallas kernels for 14%

profile of v6, /device:TPU:0, one launch (start us, length us, event | category | flops | bytes accessed | tf_op | source)
XLA Modules:
  0.0 41.8 jit_solution(16996639604860905598)
XLA Ops:
  0.6 0.8 %pad_maximum_fusion.2.refs_2_ = f32[128,128]{1,0:T(8,128)S(1)} fusion(f32[64,128]{1,0:T(8,128)} %bitcast.18, f32[64,128]{1,0:T(8,128)} %bitcast.19), kind=kLoop, calls=%fused_computation.8 | loop fusion | flops 16384 | bytes 131072 | tf_op jit(solution)/shard_map/concatenate | solution.py:337
  1.4 5.0 %collective-permute-start.2 = (f32[128,128]{1,0:T(8,128)S(1)}, f32[128,128]{1,0:T(8,128)S(1)}, u32[]{:S(2)}, u32[]{:S(2)}) collective-permute-start(f32[128,128]{1,0:T(8,128)S(1)} %pad_maximum_fusion.2.refs_2_), channel_id=1, source_target_pairs={{0,12},{4,8},{8,4},{12,0},{1,13},{5,9},{9,5},{13,1},{2,14},{6,10},... | collective-permute-start | bytes 196616 | tf_op jit(solution)/shard_map/ppermute | solution.py:318
  6.5 0.6 %collective-permute-start = (f32[128,128]{1,0:T(8,128)S(1)}, f32[128,128]{1,0:T(8,128)S(1)}, u32[]{:S(2)}, u32[]{:S(2)}) collective-permute-start(f32[128,128]{1,0:T(8,128)S(1)} %pad_maximum_fusion.2.refs_2_), channel_id=1, source_target_pairs={{0,4},{4,0},{8,12},{12,8},{1,5},{5,1},{9,13},{13,9},{2,6},{6,2},{1... | collective-permute-start | bytes 196616 | tf_op jit(solution)/shard_map/ppermute | solution.py:318
  7.1 0.1 stack.31.where
  7.2 5.2 %own_block.1 = (bf16[2048,256]{1,0:T(8,128)(2,1)S(1)}, bf16[256,2048]{1,0:T(8,128)(2,1)S(1)}, f32[2048,512]{1,0:T(8,128)S(1)}, s32[2048,512]{1,0:T(8,128)S(1)}, ...) custom-call(s32[5]{0:T(128)S(1)} %stack.31.where, ...), custom_call_target="tpu_custom_call" | custom-call | flops 1811939328 | bytes 2097152 | tf_op jit(solution)/shard_map/own_block/pallas_call | solution.py:221
  12.4 0.1 pad_add_fusion.where
  12.5 0.0 collective-permute-done.2.refs_6_
  12.5 5.6 %other_blocks.1 = (f32[64,2048]{1,0:T(8,128)S(1)}, f32[64,2048]{1,0:T(8,128)S(1)}, f32[1,128]{1,0:T(1,128)S(1)}, f32[128,128]{1,0:T(8,128)S(1)}, f32[128,128]{1,0:T(8,128)S(1)}, /*index=5*/f32[128,128]{1,0:T(8,128)S(1)}) custom-call(s32[4]{0:T(128)S(1)} %pad_add_fusion.where, s32[4,16]{1,0:T(4,128)} %bitcast.21, f32[2048,512]{1,0:T(8,128)S(1)} %get-tuple-element.25.ratings, ...), custom_call_target="tpu_custom_call" | custom-call | flops 5435817984 | bytes 6291456 | tf_op jit(solution)/shard_map/other_blocks/pallas_call | solution.py:221
  18.1 0.1 collective-permute-start.3
  18.2 2.4 %collective-permute-start.5 = (f32[128,128]{1,0:T(8,128)S(1)}, f32[128,128]{1,0:T(8,128)S(1)}, u32[]{:S(2)}, u32[]{:S(2)}) collective-permute-start(f32[128,128]{1,0:T(8,128)S(1)} %get-tuple-element.34), channel_id=1, source_target_pairs={{0,8},{4,12},{8,0},{12,4},{1,9},{5,13},{9,1},{13,5},{2,10},{6,14},... | collective-permute-start | bytes 196616 | tf_op jit(solution)/shard_map/ppermute | solution.py:318
  20.6 1.6 %collective-permute-start.6 = (f32[128,128]{1,0:T(8,128)S(1)}, f32[128,128]{1,0:T(8,128)S(1)}, u32[]{:S(2)}, u32[]{:S(2)}) collective-permute-start(f32[128,128]{1,0:T(8,128)S(1)} %get-tuple-element.35), channel_id=1, source_target_pairs={{0,12},{4,8},{8,4},{12,0},{1,13},{5,9},{9,5},{13,1},{2,14},{6,10},... | collective-permute-start | bytes 196616 | tf_op jit(solution)/shard_map/ppermute | solution.py:318
  22.2 0.5 %collective-permute-start.7 = (f32[128,128]{1,0:T(8,128)S(1)}, f32[128,128]{1,0:T(8,128)S(1)}, u32[]{:S(2)}, u32[]{:S(2)}) collective-permute-start(f32[128,128]{1,0:T(8,128)S(1)} %get-tuple-element.36), channel_id=1, source_target_pairs={{0,4},{4,0},{8,12},{12,8},{1,5},{5,1},{9,13},{13,9},{2,6},{6,2},{1... | collective-permute-start | bytes 196616 | tf_op jit(solution)/shard_map/ppermute | solution.py:318
  22.6 0.1 slice_add_fusion
  22.7 1.6 %collective-permute-start.4 = (f32[32,2048]{1,0:T(8,128)S(1)}, f32[32,2048]{1,0:T(8,128)S(1)}, u32[]{:S(2)}, u32[]{:S(2)}) collective-permute-start(f32[32,2048]{1,0:T(8,128)S(1)} %get-tuple-element.46.a), channel_id=1, source_target_pairs={{0,2},{1,3},{2,0},{3,1},{4,6},{5,7},{6,4},{7,5},{8,10},{9,11},{10,... | collective-permute-start | bytes 786440 | tf_op jit(solution)/shard_map/ppermute | solution.py:318
  24.3 0.8 %collective-permute-done.5.refs_1_ = f32[128,128]{1,0:T(8,128)S(1)} collective-permute-done((f32[128,128]{1,0:T(8,128)S(1)}, f32[128,128]{1,0:T(8,128)S(1)}, u32[]{:S(2)}, u32[]{:S(2)}) %collective-permute-start.5) | collective-permute-done | bytes 65568 | tf_op jit(solution)/shard_map/ppermute | solution.py:318
  25.1 2.2 %collective-permute-done.6.refs_2_ = f32[128,128]{1,0:T(8,128)S(1)} collective-permute-done((f32[128,128]{1,0:T(8,128)S(1)}, f32[128,128]{1,0:T(8,128)S(1)}, u32[]{:S(2)}, u32[]{:S(2)}) %collective-permute-start.6) | collective-permute-done | bytes 65568 | tf_op jit(solution)/shard_map/ppermute | solution.py:318
  27.3 0.5 %collective-permute-done.7.refs_3_ = f32[128,128]{1,0:T(8,128)S(1)} collective-permute-done((f32[128,128]{1,0:T(8,128)S(1)}, f32[128,128]{1,0:T(8,128)S(1)}, u32[]{:S(2)}, u32[]{:S(2)}) %collective-permute-start.7) | collective-permute-done | bytes 65568 | tf_op jit(solution)/shard_map/ppermute | solution.py:318
  27.8 1.7 %collective-permute-start.8 = (f32[8,128]{1,0:T(8,128)S(1)}, f32[8,128]{1,0:T(8,128)S(1)}, u32[]{:S(2)}, u32[]{:S(2)}) collective-permute-start(f32[8,128]{1,0:T(8,128)S(1)} %get-tuple-element.39), channel_id=1, source_target_pairs={{0,2},{1,3},{2,0},{3,1},{4,6},{5,7},{6,4},{7,5},{8,10},{9,11},{10,... | collective-permute-start | bytes 12296 | tf_op jit(solution)/shard_map/ppermute | solution.py:318
  29.5 0.4 collective-permute-start.10
  29.9 1.6 %collective-permute-done.8 = f32[8,128]{1,0:T(8,128)S(1)} collective-permute-done((f32[8,128]{1,0:T(8,128)S(1)}, f32[8,128]{1,0:T(8,128)S(1)}, u32[]{:S(2)}, u32[]{:S(2)}) %collective-permute-start.8) | collective-permute-done | bytes 4128 | tf_op jit(solution)/shard_map/ppermute | solution.py:318
  31.5 0.1 squares.1
  31.5 0.1 collective-permute-start.9
  31.6 1.1 %collective-permute-start.12 = (f32[8,128]{1,0:T(8,128)S(1)}, f32[8,128]{1,0:T(8,128)S(1)}, u32[]{:S(2)}, u32[]{:S(2)}) collective-permute-start(f32[8,128]{1,0:T(8,128)S(1)} %get-tuple-element.41.after), channel_id=1, source_target_pairs={{0,4},{4,0},{8,12},{12,8},{1,5},{5,1},{9,13},{13,9},{2,6},{6,2},{1... | collective-permute-start | bytes 12296 | tf_op jit(solution)/shard_map/ppermute | solution.py:318
  32.7 2.6 %collective-permute-done.12 = f32[8,128]{1,0:T(8,128)S(1)} collective-permute-done((f32[8,128]{1,0:T(8,128)S(1)}, f32[8,128]{1,0:T(8,128)S(1)}, u32[]{:S(2)}, u32[]{:S(2)}) %collective-permute-start.12) | collective-permute-done | bytes 4128 | tf_op jit(solution)/shard_map/ppermute | solution.py:318
  35.3 2.4 %collective-permute-start.13 = (f32[8,128]{1,0:T(8,128)S(1)}, f32[8,128]{1,0:T(8,128)S(1)}, u32[]{:S(2)}, u32[]{:S(2)}) collective-permute-start(f32[8,128]{1,0:T(8,128)S(1)} %add.24), channel_id=1, source_target_pairs={{0,8},{4,12},{8,0},{12,4},{1,9},{5,13},{9,1},{13,5},{2,10},{6,14},... | collective-permute-start | bytes 12296 | tf_op jit(solution)/shard_map/ppermute | solution.py:318
  37.7 0.6 %parts.1 = (f32[64,128]{1,0:T(8,128)}, f32[64,128]{1,0:T(8,128)}) custom-call(f32[128,128]{1,0:T(8,128)S(1)} %get-tuple-element.42.total, f32[8,128]{1,0:T(8,128)S(1)} %get-tuple-element.41.after), custom_call_target="tpu_custom_call" | custom-call | tf_op jit(solution)/shard_map/parts/pallas_call | solution.py:259
  38.4 0.1 collective-permute-start.11
  38.4 1.3 %collective-permute-done.13 = f32[8,128]{1,0:T(8,128)S(1)} collective-permute-done((f32[8,128]{1,0:T(8,128)S(1)}, f32[8,128]{1,0:T(8,128)S(1)}, u32[]{:S(2)}, u32[]{:S(2)}) %collective-permute-start.13) | collective-permute-done | bytes 4128 | tf_op jit(solution)/shard_map/ppermute | solution.py:318
  39.8 0.1 broadcast_select_fusion.3
  39.9 0.1 collective-permute-done.11
  40.0 1.1 %pad_maximum_fusion = (f32[64,2048]{1,0:T(8,128)S(1)}, f32[2048,64]{0,1:T(8,128)}, f32[2048,64]{0,1:T(8,128)}, f32[64,2048]{1,0:T(8,128)S(1)}) fusion(f32[32,2048]{1,0:T(8,128)S(1)} %get-tuple-element.54, f32[32,2048]{1,0:T(8,128)S(1)} %get-tuple-element.53, f32[32,2048]{1,0:T(8,128)S(1)} %get-tuple-element.52, f32[32,2048]{1,0:T(8,128)S(1)} %get-tuple-element.51), kind=kLoop, calls=%fused_computation | loop fusion | flops 262144 | bytes 3145728 | tf_op jit(solution)/shard_map/concatenate | solution.py:389
  41.1 0.6 %inner.1 = f32[2]{0:T(128)} custom-call(f32[8,128]{1,0:T(8,128)S(1)} %add.25.a, f32[8,128]{1,0:T(8,128)S(1)} %collective-permute-done.14.b, f32[64,2048]{1,0:T(8,128)S(1)} %get-tuple-element.49.g, f32[64,2048]{1,0:T(8,128)S(1)} %get-tuple-element.56.h), custom_call_target="tpu_custom_call" | custom-call | tf_op jit(solution)/shard_map/inner/pallas_call | solution.py:307
  (15 shorter events, 0.1 us)
Async XLA Ops:
  1.4 11.1 %collective-permute-start.2 = (f32[128,128]{1,0:T(8,128)S(1)}, f32[128,128]{1,0:T(8,128)S(1)}, u32[]{:S(2)}, u32[]{:S(2)}) collective-permute-start(f32[128,128]{1,0:T(8,128)S(1)} %pad_maximum_fusion.2.refs_2_), channel_id=1, source_target_pairs={{0,12},{4,8},{8,4},{12,0},{1,13},{5,9},{9,5},{13,1},{2,14},{6,10},... | collective-permute-start | bytes 196616 | tf_op jit(solution)/shard_map/ppermute | solution.py:318
  6.5 6.0 %collective-permute-start.1 = (f32[128,128]{1,0:T(8,128)S(1)}, f32[128,128]{1,0:T(8,128)S(1)}, u32[]{:S(2)}, u32[]{:S(2)}) collective-permute-start(f32[128,128]{1,0:T(8,128)S(1)} %pad_maximum_fusion.2.refs_2_), channel_id=1, source_target_pairs={{0,8},{4,12},{8,0},{12,4},{1,9},{5,13},{9,1},{13,5},{2,10},{6,14},... | collective-permute-start | bytes 196616 | tf_op jit(solution)/shard_map/ppermute | solution.py:318
  6.5 6.0 %collective-permute-start = (f32[128,128]{1,0:T(8,128)S(1)}, f32[128,128]{1,0:T(8,128)S(1)}, u32[]{:S(2)}, u32[]{:S(2)}) collective-permute-start(f32[128,128]{1,0:T(8,128)S(1)} %pad_maximum_fusion.2.refs_2_), channel_id=1, source_target_pairs={{0,4},{4,0},{8,12},{12,8},{1,5},{5,1},{9,13},{13,9},{2,6},{6,2},{1... | collective-permute-start | bytes 196616 | tf_op jit(solution)/shard_map/ppermute | solution.py:318
  18.1 4.5 %collective-permute-start.3 = (f32[64,2048]{1,0:T(8,128)S(1)}, f32[64,2048]{1,0:T(8,128)S(1)}, u32[]{:S(2)}, u32[]{:S(2)}) collective-permute-start(f32[64,2048]{1,0:T(8,128)S(1)} %get-tuple-element.32), channel_id=1, source_target_pairs={{0,1},{1,0},{2,3},{3,2},{4,5},{5,4},{6,7},{7,6},{8,9},{9,8},{10,11... | collective-permute-start | bytes 1572872 | tf_op jit(solution)/shard_map/ppermute | solution.py:318
  18.2 6.9 %collective-permute-start.5 = (f32[128,128]{1,0:T(8,128)S(1)}, f32[128,128]{1,0:T(8,128)S(1)}, u32[]{:S(2)}, u32[]{:S(2)}) collective-permute-start(f32[128,128]{1,0:T(8,128)S(1)} %get-tuple-element.34), channel_id=1, source_target_pairs={{0,8},{4,12},{8,0},{12,4},{1,9},{5,13},{9,1},{13,5},{2,10},{6,14},... | collective-permute-start | bytes 196616 | tf_op jit(solution)/shard_map/ppermute | solution.py:318
  20.6 6.7 %collective-permute-start.6 = (f32[128,128]{1,0:T(8,128)S(1)}, f32[128,128]{1,0:T(8,128)S(1)}, u32[]{:S(2)}, u32[]{:S(2)}) collective-permute-start(f32[128,128]{1,0:T(8,128)S(1)} %get-tuple-element.35), channel_id=1, source_target_pairs={{0,12},{4,8},{8,4},{12,0},{1,13},{5,9},{9,5},{13,1},{2,14},{6,10},... | collective-permute-start | bytes 196616 | tf_op jit(solution)/shard_map/ppermute | solution.py:318
  22.2 5.6 %collective-permute-start.7 = (f32[128,128]{1,0:T(8,128)S(1)}, f32[128,128]{1,0:T(8,128)S(1)}, u32[]{:S(2)}, u32[]{:S(2)}) collective-permute-start(f32[128,128]{1,0:T(8,128)S(1)} %get-tuple-element.36), channel_id=1, source_target_pairs={{0,4},{4,0},{8,12},{12,8},{1,5},{5,1},{9,13},{13,9},{2,6},{6,2},{1... | collective-permute-start | bytes 196616 | tf_op jit(solution)/shard_map/ppermute | solution.py:318
  22.7 8.8 %collective-permute-start.4 = (f32[32,2048]{1,0:T(8,128)S(1)}, f32[32,2048]{1,0:T(8,128)S(1)}, u32[]{:S(2)}, u32[]{:S(2)}) collective-permute-start(f32[32,2048]{1,0:T(8,128)S(1)} %get-tuple-element.46.a), channel_id=1, source_target_pairs={{0,2},{1,3},{2,0},{3,1},{4,6},{5,7},{6,4},{7,5},{8,10},{9,11},{10,... | collective-permute-start | bytes 786440 | tf_op jit(solution)/shard_map/ppermute | solution.py:318
  27.8 3.7 %collective-permute-start.8 = (f32[8,128]{1,0:T(8,128)S(1)}, f32[8,128]{1,0:T(8,128)S(1)}, u32[]{:S(2)}, u32[]{:S(2)}) collective-permute-start(f32[8,128]{1,0:T(8,128)S(1)} %get-tuple-element.39), channel_id=1, source_target_pairs={{0,2},{1,3},{2,0},{3,1},{4,6},{5,7},{6,4},{7,5},{8,10},{9,11},{10,... | collective-permute-start | bytes 12296 | tf_op jit(solution)/shard_map/ppermute | solution.py:318
  29.5 8.8 %collective-permute-start.10 = (f32[32,2048]{1,0:T(8,128)S(1)}, f32[32,2048]{1,0:T(8,128)S(1)}, u32[]{:S(2)}, u32[]{:S(2)}) collective-permute-start(f32[32,2048]{1,0:T(8,128)S(1)} %get-tuple-element.45.a), channel_id=1, source_target_pairs={{0,2},{1,3},{2,0},{3,1},{4,6},{5,7},{6,4},{7,5},{8,10},{9,11},{10,... | collective-permute-start | bytes 786440 | tf_op jit(solution)/shard_map/ppermute | solution.py:318
  31.5 8.3 %collective-permute-start.9 = (f32[32,2048]{1,0:T(8,128)S(1)}, f32[32,2048]{1,0:T(8,128)S(1)}, u32[]{:S(2)}, u32[]{:S(2)}) collective-permute-start(f32[32,2048]{1,0:T(8,128)S(1)} %get-tuple-element.40), channel_id=1, source_target_pairs={{0,1},{1,0},{2,3},{3,2},{4,5},{5,4},{6,7},{7,6},{8,9},{9,8},{10,11... | collective-permute-start | bytes 786440 | tf_op jit(solution)/shard_map/ppermute | solution.py:318
  31.6 3.7 %collective-permute-start.12 = (f32[8,128]{1,0:T(8,128)S(1)}, f32[8,128]{1,0:T(8,128)S(1)}, u32[]{:S(2)}, u32[]{:S(2)}) collective-permute-start(f32[8,128]{1,0:T(8,128)S(1)} %get-tuple-element.41.after), channel_id=1, source_target_pairs={{0,4},{4,0},{8,12},{12,8},{1,5},{5,1},{9,13},{13,9},{2,6},{6,2},{1... | collective-permute-start | bytes 12296 | tf_op jit(solution)/shard_map/ppermute | solution.py:318
  35.3 4.5 %collective-permute-start.13 = (f32[8,128]{1,0:T(8,128)S(1)}, f32[8,128]{1,0:T(8,128)S(1)}, u32[]{:S(2)}, u32[]{:S(2)}) collective-permute-start(f32[8,128]{1,0:T(8,128)S(1)} %add.24), channel_id=1, source_target_pairs={{0,8},{4,12},{8,0},{12,4},{1,9},{5,13},{9,1},{13,5},{2,10},{6,14},... | collective-permute-start | bytes 12296 | tf_op jit(solution)/shard_map/ppermute | solution.py:318
  38.4 1.6 %collective-permute-start.11 = (f32[32,2048]{1,0:T(8,128)S(1)}, f32[32,2048]{1,0:T(8,128)S(1)}, u32[]{:S(2)}, u32[]{:S(2)}) collective-permute-start(f32[32,2048]{1,0:T(8,128)S(1)} %add.34), channel_id=1, source_target_pairs={{0,1},{1,0},{2,3},{3,2},{4,5},{5,4},{6,7},{7,6},{8,9},{9,8},{10,11... | collective-permute-start | bytes 786440 | tf_op jit(solution)/shard_map/ppermute | solution.py:318
  39.8 1.3 %collective-permute-start.14 = (f32[8,128]{1,0:T(8,128)S(1)}, f32[8,128]{1,0:T(8,128)S(1)}, u32[]{:S(2)}, u32[]{:S(2)}) collective-permute-start(f32[8,128]{1,0:T(8,128)S(1)} %add.25.a), channel_id=1, source_target_pairs={{0,1},{1,0},{2,3},{3,2},{4,5},{5,4},{6,7},{7,6},{8,9},{9,8},{10,11... | collective-permute-start | bytes 12296 | tf_op jit(solution)/shard_map/ppermute | solution.py:318

commit v7 on v6

--- a/solution.py
+++ b/solution.py
@@ -93,7 +93,8 @@
     rank2, wide = panels[0].shape
     rank = rank2 // 2
     half = rank // 2
-    flip = where[ratings.shape[1] // wide if first else blocks] == 1
+    flip = where[ratings.shape[1] // wide] == 1
+    base = 0 if first else 1
 
     def own_first(x):
         return jnp.where(flip, jnp.concatenate([x[half:], x[:half]], axis=0), x)
@@ -142,14 +143,14 @@
             if first:
                 rating, seen = own_ratings[here, :], own_mask[here, :]
             else:
-                columns = pl.ds(pl.multiple_of(where[k] * wide, wide), wide)
+                columns = pl.ds(pl.multiple_of(where[base + k] * wide, wide), wide)
                 rating, seen = ratings[here, columns], mask[here, columns]
             seen = seen.astype(F32)
             raw = dot(factors_t[here, :], forward[k]) + dot(factors_t[here, : 2 * rank], forward_low[k])
             seen = jnp.concatenate(
                 [
                     seen[t * tile : (t + 1) * tile]
-                    * (pattern[where[k], step // tile + t].astype(F32) * (1.0 / 64.0))
+                    * (pattern[where[base + k], step // tile + t].astype(F32) * (1.0 / 64.0))
                     for t in range(rows // tile)
                 ],
                 axis=0,
@@ -344,17 +345,14 @@
         panels = [panel[:, i : i + 128] for i in range(0, panel.shape[1], 128)]
         index = list(range(len(panels)))
 
-    def where(blocks):
-        return jnp.stack([jnp.asarray(i, jnp.int32) for i in [index[k] for k in blocks] + [core]])
-
+    where = jnp.stack([jnp.asarray(i, jnp.int32) for i in [*index, core]])
     table = pattern.T
     factors_t, factors, ratings, entry_mask, left_dir_t, acc, curve_a, item = block_call(
-        where(range(len(panels))), table, ratings, entry_mask, [left.T, left_dir.T], panels[:1],
+        where, table, ratings, entry_mask, [left.T, left_dir.T], panels[:1],
         first=True, rows=512, name="own_block",
     )
-    others = list(range(1, len(panels)))
     keep, send, curve_b, *rest = block_call(
-        where(others), table, ratings, entry_mask, [factors_t, factors, acc, left_dir_t], panels[1:],
+        where, table, ratings, entry_mask, [factors_t, factors, acc, left_dir_t], panels[1:],
         last=True, rows=2048, name="other_blocks",
     )
     items = [item, *rest]

time: 42 us -> 41.9 us (level)
  no operation moved by 1% of the time
where the time goes in v7:
time: 41.9 us; the launch traced here: 41.7 us
  starting transfers between devices  17.5 us (42%)
  Pallas kernels  12.2 us (29%)
  waiting for transfers between devices  9.13 us (22%)
  other arithmetic  2.04 us (5%)
  between operations  0.73 us (2%)
    ppermute x15, starting transfers between devices, swap(): lax.ppermute(x, axis, [(i, i ^ bit) for i in range(lax.axis_size(axis))])  17.5 us
    pallas_call x2, Pallas kernels, block_call(): pl.pallas_call(functools.partial(block_kernel, blocks, first, last, span,...  10.8 us
    ppermute x15, waiting for transfers between devices, swap(): lax.ppermute(x, axis, [(i, i ^ bit) for i in range(lax.axis_size(axis))])  9.13 us
    concatenate x1, other arithmetic, joined(): jnp.concatenate([jnp.where(core == 0, mine, other), jnp.where(core == 0,...  1.1 us
  transfers between devices with their start and end apart: 15, of which 7 were waited for; matrix products, arithmetic and copies ran while one was open for 3% of the time, Pallas kernels for 14%

profile of v7, /device:TPU:0, one launch (start us, length us, event | category | flops | bytes accessed | tf_op | source)
XLA Modules:
  0.0 41.7 jit_solution(3738400052674449173)
XLA Ops:
  0.6 0.8 %pad_maximum_fusion.2.refs_2_ = f32[128,128]{1,0:T(8,128)S(1)} fusion(f32[64,128]{1,0:T(8,128)} %bitcast.18, f32[64,128]{1,0:T(8,128)} %bitcast.19), kind=kLoop, calls=%fused_computation.8 | loop fusion | flops 16384 | bytes 131072 | tf_op jit(solution)/shard_map/concatenate | solution.py:338
  1.4 5.0 %collective-permute-start.2 = (f32[128,128]{1,0:T(8,128)S(1)}, f32[128,128]{1,0:T(8,128)S(1)}, u32[]{:S(2)}, u32[]{:S(2)}) collective-permute-start(f32[128,128]{1,0:T(8,128)S(1)} %pad_maximum_fusion.2.refs_2_), channel_id=1, source_target_pairs={{0,12},{4,8},{8,4},{12,0},{1,13},{5,9},{9,5},{13,1},{2,14},{6,10},... | collective-permute-start | bytes 196616 | tf_op jit(solution)/shard_map/ppermute | solution.py:319
  6.5 0.6 %collective-permute-start = (f32[128,128]{1,0:T(8,128)S(1)}, f32[128,128]{1,0:T(8,128)S(1)}, u32[]{:S(2)}, u32[]{:S(2)}) collective-permute-start(f32[128,128]{1,0:T(8,128)S(1)} %pad_maximum_fusion.2.refs_2_), channel_id=1, source_target_pairs={{0,4},{4,0},{8,12},{12,8},{1,5},{5,1},{9,13},{13,9},{2,6},{6,2},{1... | collective-permute-start | bytes 196616 | tf_op jit(solution)/shard_map/ppermute | solution.py:319
  7.1 0.1 stack.23.where
  7.2 5.2 %own_block.1 = (bf16[2048,256]{1,0:T(8,128)(2,1)S(1)}, bf16[256,2048]{1,0:T(8,128)(2,1)S(1)}, f32[2048,512]{1,0:T(8,128)S(1)}, s32[2048,512]{1,0:T(8,128)S(1)}, ...) custom-call(s32[5]{0:T(128)S(1)} %stack.23.where, ...), custom_call_target="tpu_custom_call" | custom-call | flops 1811939328 | bytes 2097152 | tf_op jit(solution)/shard_map/own_block/pallas_call | solution.py:222
  12.4 0.0 collective-permute-done.1.refs_5_
  12.4 0.0 collective-permute-done.refs_4_
  12.4 5.6 %other_blocks.1 = (f32[64,2048]{1,0:T(8,128)S(1)}, f32[64,2048]{1,0:T(8,128)S(1)}, f32[1,128]{1,0:T(1,128)S(1)}, f32[128,128]{1,0:T(8,128)S(1)}, f32[128,128]{1,0:T(8,128)S(1)}, /*index=5*/f32[128,128]{1,0:T(8,128)S(1)}) custom-call(s32[5]{0:T(128)S(1)} %stack.23.where, s32[4,16]{1,0:T(4,128)} %bitcast.21, f32[2048,512]{1,0:T(8,128)S(1)} %get-tuple-element.25.ratings, ...), custom_call_target="tpu_custom_call" | custom-call | flops 5435817984 | bytes 6291456 | tf_op jit(solution)/shard_map/other_blocks/pallas_call | solution.py:222
  18.0 0.1 collective-permute-start.3
  18.1 2.4 %collective-permute-start.5 = (f32[128,128]{1,0:T(8,128)S(1)}, f32[128,128]{1,0:T(8,128)S(1)}, u32[]{:S(2)}, u32[]{:S(2)}) collective-permute-start(f32[128,128]{1,0:T(8,128)S(1)} %get-tuple-element.34), channel_id=1, source_target_pairs={{0,8},{4,12},{8,0},{12,4},{1,9},{5,13},{9,1},{13,5},{2,10},{6,14},... | collective-permute-start | bytes 196616 | tf_op jit(solution)/shard_map/ppermute | solution.py:319
  20.5 1.6 %collective-permute-start.6 = (f32[128,128]{1,0:T(8,128)S(1)}, f32[128,128]{1,0:T(8,128)S(1)}, u32[]{:S(2)}, u32[]{:S(2)}) collective-permute-start(f32[128,128]{1,0:T(8,128)S(1)} %get-tuple-element.35), channel_id=1, source_target_pairs={{0,12},{4,8},{8,4},{12,0},{1,13},{5,9},{9,5},{13,1},{2,14},{6,10},... | collective-permute-start | bytes 196616 | tf_op jit(solution)/shard_map/ppermute | solution.py:319
  22.1 0.5 %collective-permute-start.7 = (f32[128,128]{1,0:T(8,128)S(1)}, f32[128,128]{1,0:T(8,128)S(1)}, u32[]{:S(2)}, u32[]{:S(2)}) collective-permute-start(f32[128,128]{1,0:T(8,128)S(1)} %get-tuple-element.36), channel_id=1, source_target_pairs={{0,4},{4,0},{8,12},{12,8},{1,5},{5,1},{9,13},{13,9},{2,6},{6,2},{1... | collective-permute-start | bytes 196616 | tf_op jit(solution)/shard_map/ppermute | solution.py:319
  22.6 0.1 slice_add_fusion
  22.6 1.6 %collective-permute-start.4 = (f32[32,2048]{1,0:T(8,128)S(1)}, f32[32,2048]{1,0:T(8,128)S(1)}, u32[]{:S(2)}, u32[]{:S(2)}) collective-permute-start(f32[32,2048]{1,0:T(8,128)S(1)} %get-tuple-element.46.a), channel_id=1, source_target_pairs={{0,2},{1,3},{2,0},{3,1},{4,6},{5,7},{6,4},{7,5},{8,10},{9,11},{10,... | collective-permute-start | bytes 786440 | tf_op jit(solution)/shard_map/ppermute | solution.py:319
  24.2 0.8 %collective-permute-done.5.refs_1_ = f32[128,128]{1,0:T(8,128)S(1)} collective-permute-done((f32[128,128]{1,0:T(8,128)S(1)}, f32[128,128]{1,0:T(8,128)S(1)}, u32[]{:S(2)}, u32[]{:S(2)}) %collective-permute-start.5) | collective-permute-done | bytes 65568 | tf_op jit(solution)/shard_map/ppermute | solution.py:319
  25.0 2.2 %collective-permute-done.6.refs_2_ = f32[128,128]{1,0:T(8,128)S(1)} collective-permute-done((f32[128,128]{1,0:T(8,128)S(1)}, f32[128,128]{1,0:T(8,128)S(1)}, u32[]{:S(2)}, u32[]{:S(2)}) %collective-permute-start.6) | collective-permute-done | bytes 65568 | tf_op jit(solution)/shard_map/ppermute | solution.py:319
  27.2 0.5 %collective-permute-done.7.refs_3_ = f32[128,128]{1,0:T(8,128)S(1)} collective-permute-done((f32[128,128]{1,0:T(8,128)S(1)}, f32[128,128]{1,0:T(8,128)S(1)}, u32[]{:S(2)}, u32[]{:S(2)}) %collective-permute-start.7) | collective-permute-done | bytes 65568 | tf_op jit(solution)/shard_map/ppermute | solution.py:319
  27.7 1.7 %collective-permute-start.8 = (f32[8,128]{1,0:T(8,128)S(1)}, f32[8,128]{1,0:T(8,128)S(1)}, u32[]{:S(2)}, u32[]{:S(2)}) collective-permute-start(f32[8,128]{1,0:T(8,128)S(1)} %get-tuple-element.39), channel_id=1, source_target_pairs={{0,2},{1,3},{2,0},{3,1},{4,6},{5,7},{6,4},{7,5},{8,10},{9,11},{10,... | collective-permute-start | bytes 12296 | tf_op jit(solution)/shard_map/ppermute | solution.py:319
  29.4 0.4 collective-permute-start.10
  29.8 1.6 %collective-permute-done.8 = f32[8,128]{1,0:T(8,128)S(1)} collective-permute-done((f32[8,128]{1,0:T(8,128)S(1)}, f32[8,128]{1,0:T(8,128)S(1)}, u32[]{:S(2)}, u32[]{:S(2)}) %collective-permute-start.8) | collective-permute-done | bytes 4128 | tf_op jit(solution)/shard_map/ppermute | solution.py:319
  31.4 0.1 squares.1
  31.5 0.1 collective-permute-start.9
  31.5 1.1 %collective-permute-start.12 = (f32[8,128]{1,0:T(8,128)S(1)}, f32[8,128]{1,0:T(8,128)S(1)}, u32[]{:S(2)}, u32[]{:S(2)}) collective-permute-start(f32[8,128]{1,0:T(8,128)S(1)} %get-tuple-element.41.after), channel_id=1, source_target_pairs={{0,4},{4,0},{8,12},{12,8},{1,5},{5,1},{9,13},{13,9},{2,6},{6,2},{1... | collective-permute-start | bytes 12296 | tf_op jit(solution)/shard_map/ppermute | solution.py:319
  32.6 2.6 %collective-permute-done.12 = f32[8,128]{1,0:T(8,128)S(1)} collective-permute-done((f32[8,128]{1,0:T(8,128)S(1)}, f32[8,128]{1,0:T(8,128)S(1)}, u32[]{:S(2)}, u32[]{:S(2)}) %collective-permute-start.12) | collective-permute-done | bytes 4128 | tf_op jit(solution)/shard_map/ppermute | solution.py:319
  35.2 2.4 %collective-permute-start.13 = (f32[8,128]{1,0:T(8,128)S(1)}, f32[8,128]{1,0:T(8,128)S(1)}, u32[]{:S(2)}, u32[]{:S(2)}) collective-permute-start(f32[8,128]{1,0:T(8,128)S(1)} %add.24), channel_id=1, source_target_pairs={{0,8},{4,12},{8,0},{12,4},{1,9},{5,13},{9,1},{13,5},{2,10},{6,14},... | collective-permute-start | bytes 12296 | tf_op jit(solution)/shard_map/ppermute | solution.py:319
  37.6 0.6 %parts.1 = (f32[64,128]{1,0:T(8,128)}, f32[64,128]{1,0:T(8,128)}) custom-call(f32[128,128]{1,0:T(8,128)S(1)} %get-tuple-element.42.total, f32[8,128]{1,0:T(8,128)S(1)} %get-tuple-element.41.after), custom_call_target="tpu_custom_call" | custom-call | tf_op jit(solution)/shard_map/parts/pallas_call | solution.py:260
  38.3 0.1 collective-permute-start.11
  38.4 1.3 %collective-permute-done.13 = f32[8,128]{1,0:T(8,128)S(1)} collective-permute-done((f32[8,128]{1,0:T(8,128)S(1)}, f32[8,128]{1,0:T(8,128)S(1)}, u32[]{:S(2)}, u32[]{:S(2)}) %collective-permute-start.13) | collective-permute-done | bytes 4128 | tf_op jit(solution)/shard_map/ppermute | solution.py:319
  39.7 0.1 broadcast_select_fusion.3
  39.8 0.1 collective-permute-done.11
  40.0 1.1 %pad_maximum_fusion = (f32[64,2048]{1,0:T(8,128)S(1)}, f32[2048,64]{0,1:T(8,128)}, f32[2048,64]{0,1:T(8,128)}, f32[64,2048]{1,0:T(8,128)S(1)}) fusion(f32[32,2048]{1,0:T(8,128)S(1)} %get-tuple-element.54, f32[32,2048]{1,0:T(8,128)S(1)} %get-tuple-element.53, f32[32,2048]{1,0:T(8,128)S(1)} %get-tuple-element.52, f32[32,2048]{1,0:T(8,128)S(1)} %get-tuple-element.51), kind=kLoop, calls=%fused_computation | loop fusion | flops 262144 | bytes 3145728 | tf_op jit(solution)/shard_map/concatenate | solution.py:387
  41.1 0.6 %inner.1 = f32[2]{0:T(128)} custom-call(f32[8,128]{1,0:T(8,128)S(1)} %add.25.a, f32[8,128]{1,0:T(8,128)S(1)} %collective-permute-done.14.b, f32[64,2048]{1,0:T(8,128)S(1)} %get-tuple-element.49.g, f32[64,2048]{1,0:T(8,128)S(1)} %get-tuple-element.56.h), custom_call_target="tpu_custom_call" | custom-call | tf_op jit(solution)/shard_map/inner/pallas_call | solution.py:308
  (14 shorter events, 0.1 us)
Async XLA Ops:
  1.4 11.0 %collective-permute-start.2 = (f32[128,128]{1,0:T(8,128)S(1)}, f32[128,128]{1,0:T(8,128)S(1)}, u32[]{:S(2)}, u32[]{:S(2)}) collective-permute-start(f32[128,128]{1,0:T(8,128)S(1)} %pad_maximum_fusion.2.refs_2_), channel_id=1, source_target_pairs={{0,12},{4,8},{8,4},{12,0},{1,13},{5,9},{9,5},{13,1},{2,14},{6,10},... | collective-permute-start | bytes 196616 | tf_op jit(solution)/shard_map/ppermute | solution.py:319
  6.5 5.9 %collective-permute-start.1 = (f32[128,128]{1,0:T(8,128)S(1)}, f32[128,128]{1,0:T(8,128)S(1)}, u32[]{:S(2)}, u32[]{:S(2)}) collective-permute-start(f32[128,128]{1,0:T(8,128)S(1)} %pad_maximum_fusion.2.refs_2_), channel_id=1, source_target_pairs={{0,8},{4,12},{8,0},{12,4},{1,9},{5,13},{9,1},{13,5},{2,10},{6,14},... | collective-permute-start | bytes 196616 | tf_op jit(solution)/shard_map/ppermute | solution.py:319
  6.5 5.9 %collective-permute-start = (f32[128,128]{1,0:T(8,128)S(1)}, f32[128,128]{1,0:T(8,128)S(1)}, u32[]{:S(2)}, u32[]{:S(2)}) collective-permute-start(f32[128,128]{1,0:T(8,128)S(1)} %pad_maximum_fusion.2.refs_2_), channel_id=1, source_target_pairs={{0,4},{4,0},{8,12},{12,8},{1,5},{5,1},{9,13},{13,9},{2,6},{6,2},{1... | collective-permute-start | bytes 196616 | tf_op jit(solution)/shard_map/ppermute | solution.py:319
  18.0 4.5 %collective-permute-start.3 = (f32[64,2048]{1,0:T(8,128)S(1)}, f32[64,2048]{1,0:T(8,128)S(1)}, u32[]{:S(2)}, u32[]{:S(2)}) collective-permute-start(f32[64,2048]{1,0:T(8,128)S(1)} %get-tuple-element.32), channel_id=1, source_target_pairs={{0,1},{1,0},{2,3},{3,2},{4,5},{5,4},{6,7},{7,6},{8,9},{9,8},{10,11... | collective-permute-start | bytes 1572872 | tf_op jit(solution)/shard_map/ppermute | solution.py:319
  18.1 6.9 %collective-permute-start.5 = (f32[128,128]{1,0:T(8,128)S(1)}, f32[128,128]{1,0:T(8,128)S(1)}, u32[]{:S(2)}, u32[]{:S(2)}) collective-permute-start(f32[128,128]{1,0:T(8,128)S(1)} %get-tuple-element.34), channel_id=1, source_target_pairs={{0,8},{4,12},{8,0},{12,4},{1,9},{5,13},{9,1},{13,5},{2,10},{6,14},... | collective-permute-start | bytes 196616 | tf_op jit(solution)/shard_map/ppermute | solution.py:319
  20.5 6.7 %collective-permute-start.6 = (f32[128,128]{1,0:T(8,128)S(1)}, f32[128,128]{1,0:T(8,128)S(1)}, u32[]{:S(2)}, u32[]{:S(2)}) collective-permute-start(f32[128,128]{1,0:T(8,128)S(1)} %get-tuple-element.35), channel_id=1, source_target_pairs={{0,12},{4,8},{8,4},{12,0},{1,13},{5,9},{9,5},{13,1},{2,14},{6,10},... | collective-permute-start | bytes 196616 | tf_op jit(solution)/shard_map/ppermute | solution.py:319
  22.1 5.6 %collective-permute-start.7 = (f32[128,128]{1,0:T(8,128)S(1)}, f32[128,128]{1,0:T(8,128)S(1)}, u32[]{:S(2)}, u32[]{:S(2)}) collective-permute-start(f32[128,128]{1,0:T(8,128)S(1)} %get-tuple-element.36), channel_id=1, source_target_pairs={{0,4},{4,0},{8,12},{12,8},{1,5},{5,1},{9,13},{13,9},{2,6},{6,2},{1... | collective-permute-start | bytes 196616 | tf_op jit(solution)/shard_map/ppermute | solution.py:319
  22.6 8.8 %collective-permute-start.4 = (f32[32,2048]{1,0:T(8,128)S(1)}, f32[32,2048]{1,0:T(8,128)S(1)}, u32[]{:S(2)}, u32[]{:S(2)}) collective-permute-start(f32[32,2048]{1,0:T(8,128)S(1)} %get-tuple-element.46.a), channel_id=1, source_target_pairs={{0,2},{1,3},{2,0},{3,1},{4,6},{5,7},{6,4},{7,5},{8,10},{9,11},{10,... | collective-permute-start | bytes 786440 | tf_op jit(solution)/shard_map/ppermute | solution.py:319
  27.7 3.7 %collective-permute-start.8 = (f32[8,128]{1,0:T(8,128)S(1)}, f32[8,128]{1,0:T(8,128)S(1)}, u32[]{:S(2)}, u32[]{:S(2)}) collective-permute-start(f32[8,128]{1,0:T(8,128)S(1)} %get-tuple-element.39), channel_id=1, source_target_pairs={{0,2},{1,3},{2,0},{3,1},{4,6},{5,7},{6,4},{7,5},{8,10},{9,11},{10,... | collective-permute-start | bytes 12296 | tf_op jit(solution)/shard_map/ppermute | solution.py:319
  29.4 8.8 %collective-permute-start.10 = (f32[32,2048]{1,0:T(8,128)S(1)}, f32[32,2048]{1,0:T(8,128)S(1)}, u32[]{:S(2)}, u32[]{:S(2)}) collective-permute-start(f32[32,2048]{1,0:T(8,128)S(1)} %get-tuple-element.45.a), channel_id=1, source_target_pairs={{0,2},{1,3},{2,0},{3,1},{4,6},{5,7},{6,4},{7,5},{8,10},{9,11},{10,... | collective-permute-start | bytes 786440 | tf_op jit(solution)/shard_map/ppermute | solution.py:319
  31.5 8.3 %collective-permute-start.9 = (f32[32,2048]{1,0:T(8,128)S(1)}, f32[32,2048]{1,0:T(8,128)S(1)}, u32[]{:S(2)}, u32[]{:S(2)}) collective-permute-start(f32[32,2048]{1,0:T(8,128)S(1)} %get-tuple-element.40), channel_id=1, source_target_pairs={{0,1},{1,0},{2,3},{3,2},{4,5},{5,4},{6,7},{7,6},{8,9},{9,8},{10,11... | collective-permute-start | bytes 786440 | tf_op jit(solution)/shard_map/ppermute | solution.py:319
  31.5 3.7 %collective-permute-start.12 = (f32[8,128]{1,0:T(8,128)S(1)}, f32[8,128]{1,0:T(8,128)S(1)}, u32[]{:S(2)}, u32[]{:S(2)}) collective-permute-start(f32[8,128]{1,0:T(8,128)S(1)} %get-tuple-element.41.after), channel_id=1, source_target_pairs={{0,4},{4,0},{8,12},{12,8},{1,5},{5,1},{9,13},{13,9},{2,6},{6,2},{1... | collective-permute-start | bytes 12296 | tf_op jit(solution)/shard_map/ppermute | solution.py:319
  35.2 4.5 %collective-permute-start.13 = (f32[8,128]{1,0:T(8,128)S(1)}, f32[8,128]{1,0:T(8,128)S(1)}, u32[]{:S(2)}, u32[]{:S(2)}) collective-permute-start(f32[8,128]{1,0:T(8,128)S(1)} %add.24), channel_id=1, source_target_pairs={{0,8},{4,12},{8,0},{12,4},{1,9},{5,13},{9,1},{13,5},{2,10},{6,14},... | collective-permute-start | bytes 12296 | tf_op jit(solution)/shard_map/ppermute | solution.py:319
  38.3 1.6 %collective-permute-start.11 = (f32[32,2048]{1,0:T(8,128)S(1)}, f32[32,2048]{1,0:T(8,128)S(1)}, u32[]{:S(2)}, u32[]{:S(2)}) collective-permute-start(f32[32,2048]{1,0:T(8,128)S(1)} %add.28), channel_id=1, source_target_pairs={{0,1},{1,0},{2,3},{3,2},{4,5},{5,4},{6,7},{7,6},{8,9},{9,8},{10,11... | collective-permute-start | bytes 786440 | tf_op jit(solution)/shard_map/ppermute | solution.py:319
  39.7 1.3 %collective-permute-start.14 = (f32[8,128]{1,0:T(8,128)S(1)}, f32[8,128]{1,0:T(8,128)S(1)}, u32[]{:S(2)}, u32[]{:S(2)}) collective-permute-start(f32[8,128]{1,0:T(8,128)S(1)} %add.25.a), channel_id=1, source_target_pairs={{0,1},{1,0},{2,3},{3,2},{4,5},{5,4},{6,7},{7,6},{8,9},{9,8},{10,11... | collective-permute-start | bytes 12296 | tf_op jit(solution)/shard_map/ppermute | solution.py:319
